TPU v7x, 32 devices: a whole 2x2x4 slice. The times are simulated.
32 devices in a mesh: reorder: 4 (over z), pair: 8 (over y, x, core).
Axes of the slice: x: 2, y: 2, z: 4, core: 2. Of those that a mesh axis runs over, the one named last changes fastest.
Arguments:
- amps: bfloat16 [8, 8, 16, 4096], P('pair', 'reorder'), may hold values from -3 to 3
- tile_index: int32 [8, 8, 16], replicated, may hold values from 0 to 625, as said below
- ovov: bfloat16 [8, 8, 16, 4096], P('pair', 'reorder'), may hold values from -6 to 6
- cycle_ints: bfloat16 [8, 8, 25, 25, 4096], P('pair', 'reorder'), may hold values from -0.375 to 0.375
- history: bfloat16 [6, 8, 8, 16, 4096], P(None, 'pair', 'reorder'), may hold values from -6 to 6
- slab: int32 [8], replicated, may hold values from 0 to 199, as said below
- eps_occ: float32 [200], replicated, may hold values from -2 to -0.5
- eps_vir: float32 [1600], replicated, may hold values from 0.3 to 4
Outputs:
- new_amps: bfloat16 [8, 8, 16, 4096], P('pair', 'reorder')
- gram_row: float32 [7], replicated
Inputs may be any that keep to these rules, and one draw needn't show every extreme that they name: `tile_index`: entry (i, j, s) is a * 25 + b for the distinct tile (a, b) held in slot s of pair (i, j), or 625 for an empty slot. Live slots come first; each pair has 2 or more. At most 2 live tiles of one pair share a row a, reached. Pairs (i, 2m) and (i, 2m + 1) hold at most 24 live tiles together, reached; some pair holds 16. `slab`: distinct occupied orbitals.
All inputs are finite; a program needn't handle non-finite values.
Results may differ from a plain program's by a relative error of at most 0.008.
Values may be sent and summed in bfloat16 or wider, within the bound.
No kernel may reach another device: no remote copies, remote signals or barrier semaphores. Data moves between devices by JAX's collectives and lax.ppermute only.
A program may use at most 128 MiB of HBM per device.

v0:
```python
import jax
import jax.numpy as jnp
from jax import lax
from jax.sharding import PartitionSpec as P

TILE = 64
ROWCAP = 2


def match_lists(out_idx, in_idx, across):
    live_in = in_idx < across * across
    same = ((out_idx // across)[:, None] == (in_idx // across)[None, :]) & live_in[None, :]
    width = in_idx.shape[0]
    ranks = width - jnp.arange(width, dtype=jnp.int32)
    scores = jnp.where(same, ranks[None, :], jnp.zeros_like(ranks)[None, :])
    values, picks = lax.top_k(scores, ROWCAP)
    return (picks, values > 0)


def cycle_block(tiles, in_idx, ints_k, out_idx, out_pair):
    across = ints_k.shape[1]
    slots = out_idx.shape[0]
    picks, present = match_lists(out_idx, in_idx, across)
    cols_in = in_idx % across
    cols_out = out_idx % across
    left = tiles[picks] * present[..., None].astype(tiles.dtype)
    left = (
        left.reshape(slots, ROWCAP, TILE, TILE)
        .transpose(0, 2, 1, 3)
        .reshape(slots, TILE, ROWCAP * TILE)
    )
    right = ints_k[out_pair[:, None], cols_in[picks], cols_out[:, None]]
    right = right.reshape(slots, ROWCAP * TILE, TILE)
    return jnp.einsum("sak,skb->sab", left, right, preferred_element_type=jnp.float32)


def local(amps, tile_index, ovov, cycle_ints, history, slab, eps_occ, eps_vir):
    occ_dev, jdev, capt, tile_area = amps.shape
    ns = tile_index.shape[0]
    across = cycle_ints.shape[2]
    first_here = lax.axis_index("pair") * occ_dev
    second_here = lax.axis_index("reorder") * jdev
    rows_here = lax.all_gather(amps, "reorder", axis=1, tiled=True)
    turned = lax.all_to_all(rows_here, "pair", split_axis=1, concat_axis=0, tiled=True)
    local_idx = lax.dynamic_slice(tile_index, (first_here, second_here, 0), (occ_dev, jdev, capt))
    live = (local_idx < across * across).astype(jnp.float32)

    def cycle_for(first, out_idx, out_pair):
        tiles_i = turned[first]
        in_rows = lax.dynamic_slice_in_dim(tile_index[first], first_here, occ_dev, 0)
        total = cycle_block(tiles_i[0], in_rows[0], cycle_ints[0], out_idx, out_pair)
        return total.reshape(out_idx.shape[0], tile_area)

    def full_row(first):
        out_rows = lax.dynamic_slice_in_dim(tile_index[first], second_here, jdev, 0)
        out_pair = jnp.repeat(jnp.arange(jdev, dtype=jnp.int32), capt)
        return cycle_for(first, out_rows.reshape(-1), out_pair).reshape(jdev, capt, tile_area)

    cycle = lax.psum_scatter(
        jax.vmap(full_row)(jnp.arange(occ_dev * lax.axis_size("pair"), dtype=jnp.int32)).astype(
            jnp.bfloat16
        ),
        "pair",
        scatter_dimension=0,
        tiled=True,
    ).astype(jnp.float32)
    resid = (ovov.astype(jnp.float32) + cycle) * live[..., None]
    occ_pick = (slab[:, None] == jnp.arange(eps_occ.shape[0], dtype=jnp.int32)[None, :]).astype(
        jnp.float32
    )
    occ_energy = jnp.dot(occ_pick, eps_occ, precision=lax.Precision.HIGHEST)
    first_energy = lax.dynamic_slice_in_dim(occ_energy, first_here, occ_dev, 0)
    second_energy = lax.dynamic_slice_in_dim(occ_energy, second_here, jdev, 0)
    vir_tiles = eps_vir.reshape(across, TILE)
    tile_ids = jnp.arange(across, dtype=jnp.int32)
    row_pick = (jnp.minimum(local_idx // across, across - 1)[..., None] == tile_ids).astype(
        jnp.float32
    )
    col_pick = ((local_idx % across)[..., None] == tile_ids).astype(jnp.float32)
    row_energy = jnp.einsum("ijsn,np->ijsp", row_pick, vir_tiles, precision=lax.Precision.HIGHEST)
    col_energy = jnp.einsum("ijsn,np->ijsp", col_pick, vir_tiles, precision=lax.Precision.HIGHEST)
    denom = first_energy[:, None, None, None, None] + second_energy[None, :, None, None, None]
    denom = denom - row_energy[..., :, None] - col_energy[..., None, :]
    denom = denom.reshape(occ_dev, jdev, capt, tile_area)
    new_amps = ((amps.astype(jnp.float32) + resid / denom) * live[..., None]).astype(jnp.bfloat16)
    cross = jnp.einsum(
        "hijsx,ijsx->h",
        history,
        resid,
        precision=lax.Precision.HIGHEST,
        preferred_element_type=jnp.float32,
    )
    square = jnp.sum(resid * resid)
    cross, square = lax.psum((cross, square), ("reorder", "pair"))
    gram_row = jnp.concatenate([cross, jnp.sqrt(square)[None]]) / (TILE * ns)
    return (new_amps, gram_row)


def solution(mesh):
    in_specs = (
        P("pair", "reorder", None, None),
        P(),
        P("pair", "reorder", None, None),
        P("pair", "reorder", None, None, None),
        P(None, "pair", "reorder", None, None),
        P(),
        P(),
        P(),
    )
    out_specs = (P("pair", "reorder", None, None), P())
    return jax.shard_map(local, mesh=mesh, in_specs=in_specs, out_specs=out_specs, check_vma=False)
```

profile of v0, /device:TPU:0, one launch (start us, length us, event | category | flops | bytes accessed | tf_op | source)
XLA Modules:
  0.0 262.9 jit_solution(10106506345606179865)
XLA Ops:
  7.2 0.7 all-gather.2.cloned.1.call-update
  7.9 1.3 gather_fusion.1
  10.0 0.9 top_k.12
  10.9 29.3 %all-gather.2.cloned.1.call-done = bf16[1,8,16,4096]{3,2,0,1:T(8,128)(2,1)} async-done(((bf16[1,2,16,4096]{3,2,0,1:T(8,128)(2,1)}), bf16[1,8,16,4096]{3,2,0,1:T(8,128)(2,1)}) %all-gather.2.cloned.1.call-update) | async-done | bytes 1048592 | tf_op jit(solution)/shard_map/all_gather | solution.py:43
  40.2 3.7 %all-to-all-start = ((bf16[1,8,16,4096]{3,2,0,1:T(8,128)(2,1)}), bf16[1,8,16,4096]{3,2,0,1:T(8,128)(2,1)S(1)}, u32[]{:S(2)}, u32[]{:S(2)}) async-start(bf16[1,8,16,4096]{3,2,0,1:T(8,128)(2,1)} %all-gather.2.cloned.1.call-done), calls=%async_computation | async-start | bytes 2097152 | tf_op jit(solution)/shard_map/all_to_all | solution.py:44
  44.4 2.6 %gather_fusion.4 = s32[512]{0:T(512)S(1)} fusion(s32[8,16]{1,0:T(8,128)S(1)} %get-tuple-element.45, s32[512]{0:T(512)S(1)} %reshape.305), kind=kCustom, calls=%fused_computation.4 | custom fusion | bytes 8192 | tf_op jit(solution)/shard_map/vmap()/gather | solution.py:32
  47.7 18.0 %gather_fusion.2 = bf16[512,4096]{1,0:T(8,128)(2,1)} fusion(bf16[2,25,25,4096]{3,0,2,1:T(2,128)(2,1)} %bitcast.67, s32[512]{0:T(512)S(1)} %reshape.299), kind=kCustom, calls=%fused_computation.2 | custom fusion | bytes 8394752 | tf_op jit(solution)/shard_map/vmap()/gather | solution.py:32
  65.7 12.6 %reshape.184 = bf16[8,32,128,64]{3,2,1,0:T(8,128)(2,1)} reshape(bf16[512,4096]{1,0:T(8,128)(2,1)} %gather_fusion.2) | data formatting | bytes 8388608 | tf_op jit(solution)/shard_map/vmap()/reshape | solution.py:33
  78.4 1.0 copy-done.1
  79.4 1.8 gather_fusion
  81.2 18.0 %gather_fusion.3 = bf16[512,4096]{1,0:T(8,128)(2,1)} fusion(bf16[8,16,4096]{2,1,0:T(8,128)(2,1)S(1)} %gather_fusion, s32[512]{0:T(512)S(1)} %reshape.305), kind=kCustom, calls=%fused_computation.3 | custom fusion | bytes 8392704 | tf_op jit(solution)/shard_map/vmap()/gather | solution.py:26
  99.2 12.6 %gather.31 = bf16[8,32,2,64,64]{4,3,2,1,0:T(8,128)(2,1)} reshape(bf16[512,4096]{1,0:T(8,128)(2,1)} %gather_fusion.3) | data formatting | bytes 8388608 | tf_op jit(solution)/shard_map/vmap()/gather | solution.py:26
  111.8 7.2 %multiply_bitcast_fusion = bf16[8,32,64,2,64]{4,2,3,1,0:T(8,128)(2,1)} fusion(bf16[8,32,2,64,64]{4,3,2,1,0:T(8,128)(2,1)} %gather.31, bf16[8,32,2]{2,1,0:T(8,128)(2,1)S(1)} %copy.22), kind=kLoop, calls=%fused_computation.5 | loop fusion | flops 2097152 | bytes 8389632 | tf_op jit(solution)/shard_map/vmap()/transpose | solution.py:29
  119.1 16.3 %copy.23 = bf16[8,32,64,2,64]{4,3,2,1,0:T(2,128)(2,1)} copy(bf16[8,32,64,2,64]{4,2,3,1,0:T(8,128)(2,1)} %multiply_bitcast_fusion) | data formatting | bytes 8388608 | tf_op jit(solution)/shard_map/vmap()/transpose | solution.py:29
  135.4 14.2 %reshape.182 = bf16[8,32,64,128]{3,2,1,0:T(8,128)(2,1)} reshape(bf16[8,32,64,2,64]{4,3,2,1,0:T(2,128)(2,1)} %copy.23) | data formatting | bytes 8388608 | tf_op jit(solution)/shard_map/vmap()/reshape | solution.py:30
  149.6 8.9 %convolution_convert_fusion = bf16[8,32,64,64]{3,2,1,0:T(8,128)(2,1)} fusion(bf16[8,32,64,128]{3,2,1,0:T(8,128)(2,1)} %reshape.182, bf16[8,32,128,64]{3,2,1,0:T(8,128)(2,1)} %reshape.184), kind=kOutput, calls=%fused_computation.6 | convolution fusion | flops 269484032 | bytes 10485760 | tf_op jit(solution)/shard_map/vmap(sak,skb->sab)/dot_general | solution.py:34
  158.5 6.7 %convert_element_type.30 = bf16[8,2,16,4096]{3,2,1,0:T(8,128)(2,1)} reshape(bf16[8,32,64,64]{3,2,1,0:T(8,128)(2,1)} %convolution_convert_fusion) | data formatting | bytes 4194304 | tf_op jit(solution)/shard_map/convert_element_type | solution.py:60
  166.1 0.7 dynamic-slice_add_fusion
  166.8 0.7 minimum_bitcast_fusion
  168.6 0.7 fusion.21
  169.3 37.1 %reduce-scatter.2.cloned.1.call-done = bf16[1,2,16,4096]{3,2,1,0:T(8,128)(2,1)} async-done(((bf16[8,2,16,4096]{3,2,1,0:T(8,128)(2,1)}), bf16[1,2,16,4096]{3,2,1,0:T(8,128)(2,1)}) %reduce-scatter.2.cloned.1.call-update) | async-done | bytes 262160 | tf_op jit(solution)/shard_map/reduce_scatter | solution.py:59
  206.4 2.6 fusion.6
  209.0 6.2 %fusion.2 = f32[6]{0:T(128)S(1)} fusion(bf16[6,2,16,4096]{3,2,1,0:T(8,128)(2,1)S(1)} %bitcast.66, f32[2,16,4096,1]{2,1,0,3:T(8,128)S(1)} %get-tuple-element.32), kind=kOutput, calls=%fused_computation.10 | convolution fusion | flops 9437184 | bytes 2097176 | tf_op jit(solution)/shard_map/hijsx,ijsx->h/dot_general | solution.py:86
  215.2 39.6 %all-reduce = (f32[]{:T(128)}, f32[6]{0:T(128)S(1)}) all-reduce(f32[]{:T(128)} %get-tuple-element.33, f32[6]{0:T(128)S(1)} %fusion.2), channel_id=1, replica_groups=mesh['reorder'=4,'pair'=8] {'reorder','pair'}, use_global_device_ids=true, to_apply=%region_4.5 | all-reduce | flops 7 | bytes 56 | tf_op jit(solution)/shard_map/psum | solution.py:94
  (52 shorter events, 4.4 us)
Async XLA Ops:
  7.2 201.8 %copy-start = (bf16[6,1,2,16,4096]{4,3,2,1,0:T(8,128)(2,1)S(1)}, bf16[6,1,2,16,4096]{4,3,2,1,0:T(8,128)(2,1)}, u32[]{:S(2)}) copy-start(bf16[6,1,2,16,4096]{4,3,2,1,0:T(8,128)(2,1)} %param.12) | copy-start | bytes 4718596
  7.2 33.1 %all-gather.2.cloned.1.call-start = ((), (), s32[]{:S(2)}) async-start(), calls=%async_computation.2 | async-start | bytes 1310720 | tf_op jit(solution)/shard_map/all_gather | solution.py:43
  40.2 38.1 %all-to-all-start = ((bf16[1,8,16,4096]{3,2,0,1:T(8,128)(2,1)}), bf16[1,8,16,4096]{3,2,0,1:T(8,128)(2,1)S(1)}, u32[]{:S(2)}, u32[]{:S(2)}) async-start(bf16[1,8,16,4096]{3,2,0,1:T(8,128)(2,1)} %all-gather.2.cloned.1.call-done), calls=%async_computation | async-start | bytes 2097152 | tf_op jit(solution)/shard_map/all_to_all | solution.py:44
  43.9 162.5 %reduce-scatter.2.cloned.1.call-start = ((), (), s32[]{:S(2)}) async-start(), calls=%async_computation.3 | async-start | bytes 2359296 | tf_op jit(solution)/shard_map/reduce_scatter | solution.py:59
  78.3 1.1 copy-start.1
  158.5 6.7 %copy-start.4 = (f32[200]{0:T(256)S(1)}, f32[200]{0:T(256)}, u32[]{:S(2)}) copy-start(f32[200]{0:T(256)} %param.14) | copy-start | bytes 2404
  158.5 6.7 %copy-start.5 = (s32[8]{0:T(128)S(1)}, s32[8]{0:T(128)}, u32[]{:S(2)}) copy-start(s32[8]{0:T(128)} %param.13) | copy-start | bytes 100
  158.5 7.5 %copy-start.3 = (f32[1600]{0:T(1024)S(1)}, f32[1600]{0:T(1024)}, u32[]{:S(2)}) copy-start(f32[1600]{0:T(1024)} %param.15) | copy-start | bytes 19204
  158.5 47.9 %copy-start.2 = (bf16[1,2,16,4096]{3,2,1,0:T(8,128)(2,1)S(1)}, bf16[1,2,16,4096]{3,2,1,0:T(8,128)(2,1)}, u32[]{:S(2)}) copy-start(bf16[1,2,16,4096]{3,2,1,0:T(8,128)(2,1)} %param.8) | copy-start | bytes 786436
Sparse Core Ops, SparseCore 0:
  9.6 30.6 all-gather.1
  165.4 40.9 reduce-scatter.1
where the time goes:
time: 264 us; the launch traced here: 263 us
  local copies, waits for them, and re-layouts  108 us (41%)
  waiting for transfers between devices  67.1 us (25%)
  blocking collectives  39.6 us (15%)
  matrix products  15.7 us (6%)
  between operations  15 us (6%)
  other arithmetic  14.2 us (5%)
  starting transfers between devices  3.73 us (1%)
    psum x1, blocking collectives, local(): cross, square = lax.psum((cross, square), ('reorder', 'pair'))  39.6 us
    reduce_scatter x1, waiting for transfers between devices, local(): lax.psum_scatter(jax.vmap(full_row)(jnp.arange(occ_dev * lax.axis_size('p...  37.1 us
    gather x4, local copies, waits for them, and re-layouts, cycle_block(): left = tiles[picks] * present[..., None].astype(tiles.dtype)  30.9 us
    all_gather x1, waiting for transfers between devices, local(): rows_here = lax.all_gather(amps, 'reorder', axis=1, tiled=True)  29.3 us
    gather x4, local copies, waits for them, and re-layouts, cycle_block(): right = ints_k[out_pair[:, None], cols_in[picks], cols_out[:, None]]  20.9 us
    transpose x1, local copies, waits for them, and re-layouts, cycle_block(): left = left.reshape(slots, ROWCAP, TILE, TILE).transpose(0, 2, 1, 3).resh...  16.3 us
    reshape x1, local copies, waits for them, and re-layouts, cycle_block(): left = left.reshape(slots, ROWCAP, TILE, TILE).transpose(0, 2, 1, 3).resh...  14.2 us
    reshape x1, local copies, waits for them, and re-layouts, cycle_block(): right = right.reshape(slots, ROWCAP * TILE, TILE)  12.6 us
  transfers between devices with their start and end apart: 3, of which 2 were waited for; matrix products, arithmetic and copies ran while one was open for 16% of the time, Pallas kernels for 0%

commit v1 on v0

v1 whole, which is shorter than its diff:
```python
import functools

import jax
import jax.numpy as jnp
from jax import lax
from jax.experimental import pallas as pl
from jax.experimental.pallas import tpu as pltpu
from jax.sharding import PartitionSpec as P

TILE = 64
ROWS = 32
LANES = 128
LIVE2 = 24
F32 = jnp.float32
BF16 = jnp.bfloat16
SMEM = pl.BlockSpec(memory_space=pltpu.SMEM)
VMEM = pl.BlockSpec(memory_space=pltpu.VMEM)


def count_live(ti_ref, i, j, capt, dead):
    total = jnp.int32(0)
    for s in range(capt):
        total = total + (ti_ref[i, j, s] < dead).astype(jnp.int32)
    return total


def row_of(idx, across):
    factor = -(-(1 << 17) // across)
    assert all((n * factor) >> 17 == n // across for n in range(across * across + 1))
    return lax.shift_right_logical(idx * factor, 17)


def pack_kernel(capt, across, ti_ref, amps_ref, out_ref, flat_ref, turned_ref):
    first = lax.axis_index("pair")
    second = lax.axis_index("reorder") * 2
    live1 = count_live(ti_ref, first, second + 1, capt, across * across)
    for jj in range(2):
        for p in range(ROWS):
            chunk = amps_ref[0, jj, :, p * LANES : (p + 1) * LANES].astype(F32)
            for g in range(capt // 8):
                start = (jj * capt + g * 8) * ROWS + p
                flat_ref[pl.ds(start, 8, stride=ROWS), :] = chunk[g * 8 : (g + 1) * 8]
    old = lax.broadcasted_iota(jnp.int32, (LANES, LANES), 0)
    new = lax.broadcasted_iota(jnp.int32, (LANES, LANES), 1)
    source = (new // 64) * 64 + (new % 32) * 2 + (new % 64) // 32
    turn = (old == source).astype(F32).astype(BF16)
    turned_ref[...] = jnp.dot(
        flat_ref[...].astype(BF16), turn, preferred_element_type=F32
    ).astype(BF16)
    out_ref[0:capt] = turned_ref[0 : capt * ROWS].reshape(capt, ROWS, LANES)
    out_ref[capt:LIVE2] = jnp.zeros((LIVE2 - capt, ROWS, LANES), BF16)

    def place(s, carry):
        start = pl.multiple_of((capt + s) * ROWS, ROWS)
        out_ref[LIVE2 - live1 + s] = turned_ref[pl.ds(start, ROWS), :]
        return carry

    lax.fori_loop(0, live1, place, 0)


def pack(amps, ti, capt, across):
    return pl.pallas_call(
        functools.partial(pack_kernel, capt, across),
        in_specs=[SMEM, VMEM],
        out_specs=VMEM,
        scratch_shapes=[
            pltpu.VMEM((2 * capt * ROWS, LANES), F32),
            pltpu.VMEM((2 * capt * ROWS, LANES), BF16),
        ],
        out_shape=jax.ShapeDtypeStruct((LIVE2, ROWS, LANES), BF16),
        cost_estimate=pl.CostEstimate(flops=10**8, bytes_accessed=500000, transcendentals=0),
        name="pack_amps",
    )(ti, amps)


def prep_kernel(
    capt, across, nq, nmax, ti_ref, slab_ref, occ_ref, ints_ref, row_ref, col_ref,
    meta_ref, mine_ref, send_ref, inv_ref, wide_ref, den_ref, tab_ref,
):
    dead = across * across
    me = lax.axis_index("pair")
    sibling = me ^ 1
    plane = lax.axis_index("reorder")
    second = plane * 2

    def build(which, who, k):
        def field(f):
            return (which * 5 + f) * nmax

        parity = lax.rem(k, 2)

        def one_first(q, cnt):
            i = (plane ^ q) * 2 + (who & 1)
            out = (lax.shift_right_logical(who, 1) ^ plane ^ q) * LIVE2
            for a in range(across + 1):
                tab_ref[a] = -1
            live_in = jnp.int32(0)
            for t in range(capt):
                idx = ti_ref[i, k, t]
                live_in = live_in + (idx < dead).astype(jnp.int32)
                a = row_of(idx, across)
                held = t * 32 + idx - a * across
                old = tab_ref[a]
                tab_ref[a] = jnp.where(old < 0, held, old)
                tab_ref[32 + a] = jnp.where(old < 0, -1, held)
            shift = q * LIVE2 + jnp.where(parity == 1, LIVE2 - live_in, 0)
            live1 = count_live(ti_ref, i, second + 1, capt, dead)
            for jj in range(2):
                for s in range(capt):
                    idx = ti_ref[i, second + jj, s]
                    a = row_of(idx, across)
                    b = idx - a * across
                    h0 = tab_ref[a]
                    h1 = tab_ref[32 + a]
                    hit = (idx < dead) & (h0 >= 0)
                    both = h1 >= 0
                    if which < 2:
                        place = out + (s if jj == 0 else LIVE2 - live1 + s)
                        meta_ref[field(0) + cnt] = place
                        t0 = shift + lax.shift_right_arithmetic(h0, 5)
                        t1 = shift + lax.shift_right_arithmetic(h1, 5)
                        meta_ref[field(1) + cnt] = t0
                        meta_ref[field(2) + cnt] = jnp.where(both, t1, t0)
                    if which != 1:
                        w0 = ((h0 & 31) * across + b) * 2 + jj
                        w1 = ((h1 & 31) * across + b) * 2 + jj
                        meta_ref[field(3) + cnt] = w0
                        meta_ref[field(4) + cnt] = jnp.where(both, w1, -1)
                    cnt = cnt + hit.astype(jnp.int32)
            return cnt

        total = lax.fori_loop(0, nq, one_first, jnp.int32(0))
        meta_ref[15 * nmax + which] = total
        return total

    def gather(which, total, tiles_ref):
        def fetch(step, carry):
            for u in range(4):
                e = jnp.minimum(step * 4 + u, total - 1)
                for m in range(2):
                    at = jnp.maximum(meta_ref[(which * 5 + 3 + m) * nmax + e], 0)
                    wide_ref[2 * u + m] = ints_ref[lax.shift_right_logical(at, 1)].astype(F32)
            for u in range(4):
                e = jnp.minimum(step * 4 + u, total - 1)
                for m in range(2):
                    at = meta_ref[(which * 5 + 3 + m) * nmax + e]
                    jj = jnp.maximum(at, 0) & 1
                    tile = wide_ref[2 * u + m, pl.ds(jj, ROWS, stride=2), :]
                    if m == 1:
                        tile = jnp.where(at >= 0, tile, 0.0)
                    tiles_ref[e, m * ROWS : (m + 1) * ROWS] = tile.astype(BF16)
            return carry

        lax.fori_loop(0, (total + 3) // 4, fetch, 0)

    gather(2, build(2, sibling, me), send_ref)
    gather(0, build(0, me, me), mine_ref)
    build(1, me, sibling)

    occ_i = occ_ref[slab_ref[me]]
    for jj in range(2):
        occ = occ_i + occ_ref[slab_ref[second + jj]]

        def denom(s, carry):
            idx = ti_ref[me, second + jj, s]
            row = row_of(idx, across)
            a = jnp.minimum(row, across - 1)
            b = idx - row * across
            at = pl.multiple_of((jj * capt + s) * ROWS, ROWS)
            den_ref[pl.ds(at, ROWS), :] = 1.0 / ((occ - row_ref[a]) - col_ref[b])
            return carry

        lax.fori_loop(0, capt, denom, 0)
        for p in range(ROWS):
            for g in range(capt // 8):
                inv_ref[jj, g * 8 : (g + 1) * 8, p * LANES : (p + 1) * LANES] = den_ref[
                    pl.ds((jj * capt + g * 8) * ROWS + p, 8, stride=ROWS), :
                ]


def prep(cycle_ints, ti, slab, eps_occ, eps_vir, capt, across, nq):
    nmax = nq * LIVE2 + 8
    vir = eps_vir.reshape(across, ROWS, 2, 1)
    row_table = jnp.broadcast_to(vir, (across, ROWS, 2, 64)).reshape(across, ROWS, LANES)
    col_table = jnp.broadcast_to(
        eps_vir.reshape(across, 1, 1, 64), (across, 1, 2, 64)
    ).reshape(across, 1, LANES)
    ints = cycle_ints[0].transpose(1, 2, 0, 3).reshape(across, across, 2, ROWS, LANES)
    ints = ints.transpose(0, 1, 3, 2, 4).reshape(across * across, 2 * ROWS, LANES)
    tiles = jax.ShapeDtypeStruct((nq * LIVE2, 2 * ROWS, LANES), BF16)
    return pl.pallas_call(
        functools.partial(prep_kernel, capt, across, nq, nmax),
        in_specs=[SMEM, SMEM, SMEM, VMEM, VMEM, VMEM],
        out_specs=[SMEM, VMEM, VMEM, VMEM],
        scratch_shapes=[
            pltpu.VMEM((8, 2 * ROWS, LANES), F32),
            pltpu.VMEM((2 * capt * ROWS, LANES), F32),
            pltpu.SMEM((64,), jnp.int32),
        ],
        out_shape=[
            jax.ShapeDtypeStruct((15 * nmax + 8,), jnp.int32),
            tiles,
            tiles,
            jax.ShapeDtypeStruct((2, capt, TILE * TILE), F32),
        ],
        compiler_params=pltpu.CompilerParams(vmem_limit_bytes=32 * 1024 * 1024),
        cost_estimate=pl.CostEstimate(flops=10**9, bytes_accessed=40 * 10**6, transcendentals=0),
        name="prep_integrals",
    )(ti, slab, eps_occ, ints, row_table, col_table)


def multiply_kernel(which, nq, nmax, unroll, meta_ref, tiles_ref, *refs):
    amps_refs, refs = refs[:nq], refs[nq:]
    if which == 0:
        sum_ref, amps_ref = refs
        sum_ref[...] = jnp.zeros(sum_ref.shape, F32)
    else:
        sum_ref, out_refs, amps_ref = refs[0], refs[1:-1], refs[-1]
    for q in range(nq):
        amps_ref[q * LIVE2 : (q + 1) * LIVE2] = amps_refs[q][...]
    low = lax.broadcasted_iota(jnp.int32, (ROWS, LANES), 1) < 64

    def spread(w):
        w = w.astype(F32)
        r = pltpu.roll(w, 64, 1)
        zero = jnp.zeros_like(w)
        parts = [
            jnp.where(low, w, zero),
            jnp.where(low, r, zero),
            jnp.where(low, zero, r),
            jnp.where(low, zero, w),
        ]
        return jnp.concatenate(parts, axis=0).astype(BF16)

    total = meta_ref[15 * nmax + which]

    def several(step, carry):
        results = []
        for u in range(unroll):
            e = jnp.minimum(step * unroll + u, total - 1)
            at = which * 5 * nmax + e
            left = jnp.concatenate(
                [amps_ref[meta_ref[nmax + at]], amps_ref[meta_ref[2 * nmax + at]]], axis=1
            )
            right = jnp.concatenate(
                [spread(tiles_ref[e, 0:ROWS]), spread(tiles_ref[e, ROWS : 2 * ROWS])], axis=0
            )
            place = jnp.where(step * unroll + u < total, meta_ref[at], nq * LIVE2)
            results.append((place, jnp.dot(left, right, preferred_element_type=F32)))
        for place, value in results:
            if which == 0:
                sum_ref[place] = value
            else:
                sum_ref[place] += value
        return carry

    lax.fori_loop(0, (total + unroll - 1) // unroll, several, 0)
    if which == 1:
        for q in range(nq):
            out_refs[q][...] = sum_ref[q * LIVE2 : (q + 1) * LIVE2].astype(BF16)


def multiply(which, meta, tiles, amps, sums, nq):
    block = jax.ShapeDtypeStruct((LIVE2, ROWS, LANES), BF16)
    scratch = [pltpu.VMEM((nq * LIVE2, ROWS, LANES), BF16)]
    if which == 0:
        out = jax.ShapeDtypeStruct((nq * LIVE2 + 1, ROWS, LANES), F32)
    else:
        out = [block] * nq
    return pl.pallas_call(
        functools.partial(multiply_kernel, which, nq, nq * LIVE2 + 8, 8),
        in_specs=[SMEM] + [VMEM] * (1 + nq + len(sums)),
        out_specs=jax.tree.map(lambda _: VMEM, out),
        out_shape=out,
        scratch_shapes=scratch,
        compiler_params=pltpu.CompilerParams(vmem_limit_bytes=24 * 1024 * 1024),
        cost_estimate=pl.CostEstimate(flops=10**9, bytes_accessed=10**7, transcendentals=0),
        name="multiply_own" if which == 0 else "multiply_sibling",
    )(meta, tiles, *amps, *sums)


def update_kernel(
    capt, across, nq, ti_ref, amps_ref, ovov_ref, hist_ref, inv_ref, *refs
):
    part_refs, (new_ref, gram_ref, sum_ref) = refs[:nq], refs[nq:]
    nhist = hist_ref.shape[0]
    first = lax.axis_index("pair")
    second = lax.axis_index("reorder") * 2

    def add(s, carry):
        acc = part_refs[0][s].astype(F32)
        for part_ref in part_refs[1:]:
            acc = acc + part_ref[s].astype(F32)
        sum_ref[pl.ds(pl.multiple_of(s * ROWS, ROWS), ROWS), :] = acc
        return carry

    lax.fori_loop(0, LIVE2, add, 0, unroll=4)
    slot = lax.broadcasted_iota(jnp.int32, (8, LANES), 0)
    accs = [jnp.zeros((8, LANES), F32) for _ in range(nhist + 1)]
    for jj in range(2):
        count = count_live(ti_ref, first, second + jj, capt, across * across)
        start = 0 if jj == 0 else (LIVE2 - count) * ROWS
        for g in range(capt // 8):
            alive = slot + g * 8 < count
            rows = slice(g * 8, (g + 1) * 8)

            def chunk(p, accs):
                here = pl.ds(pl.multiple_of(p * LANES, LANES), LANES)
                cycle = sum_ref[pl.ds(start + g * 8 * ROWS + p, 8, stride=ROWS), :]
                resid = jnp.where(alive, ovov_ref[0, jj, rows, here].astype(F32) + cycle, 0.0)
                moved = amps_ref[0, jj, rows, here].astype(F32) + resid * inv_ref[jj, rows, here]
                new_ref[0, jj, rows, here] = jnp.where(alive, moved, 0.0).astype(BF16)
                out = [
                    accs[m] + hist_ref[m, 0, jj, rows, here].astype(F32) * resid
                    for m in range(nhist)
                ]
                out.append(accs[nhist] + resid * resid)
                return out

            accs = lax.fori_loop(0, ROWS, chunk, accs, unroll=8)
    for m in range(8):
        if m <= nhist:
            gram_ref[m : m + 1] = jnp.sum(accs[m], axis=0, keepdims=True)
        else:
            gram_ref[m : m + 1] = jnp.zeros((1, LANES), F32)


def update(ti, amps, ovov, history, inv, parts, capt, across):
    nq = len(parts)
    return pl.pallas_call(
        functools.partial(update_kernel, capt, across, nq),
        in_specs=[SMEM] + [VMEM] * (4 + nq),
        out_specs=[VMEM, VMEM],
        out_shape=[
            jax.ShapeDtypeStruct(amps.shape, BF16),
            jax.ShapeDtypeStruct((8, LANES), F32),
        ],
        scratch_shapes=[pltpu.VMEM(((LIVE2 + capt) * ROWS, LANES), F32)],
        compiler_params=pltpu.CompilerParams(vmem_limit_bytes=24 * 1024 * 1024),
        cost_estimate=pl.CostEstimate(flops=10**8, bytes_accessed=6 * 10**6, transcendentals=0),
        name="update_amps",
    )(ti, amps, ovov, history, inv, *parts)


def finish_kernel(nhist, scale, *refs):
    total = refs[0][...]
    for ref in refs[1:-1]:
        total = total + ref[...]
    total = jnp.sum(total, axis=1, keepdims=True)
    row = lax.broadcasted_iota(jnp.int32, total.shape, 0)
    total = jnp.where(row == nhist, jnp.sqrt(jnp.maximum(total, 0.0)), total) * scale
    for m in range(nhist + 1):
        refs[-1][m] = total[m, 0]


def finish(sums, nhist, scale):
    return pl.pallas_call(
        functools.partial(finish_kernel, nhist, scale),
        in_specs=[VMEM] * len(sums),
        out_specs=SMEM,
        out_shape=jax.ShapeDtypeStruct((nhist + 1,), F32),
        name="finish_gram",
    )(*sums)


def swap(x, axis, size, step):
    return lax.ppermute(x, axis, [(n, n ^ step) for n in range(size)])


def spread_perm(npair, nq, m):
    pairs = []
    for plane in range(nq):
        for pair in range(npair):
            to = ((pair // 2) ^ m) * npair + 2 * plane + pair % 2
            pairs.append((plane * npair + pair, to))
    return pairs


def local(npair, nq, amps, tile_index, ovov, cycle_ints, history, slab, eps_occ, eps_vir):
    occ_dev, jdev, capt, tile_area = amps.shape
    ns = tile_index.shape[0]
    across = cycle_ints.shape[2]
    nhist = history.shape[0]
    assert occ_dev == 1 and jdev == 2 and tile_area == TILE * TILE and capt == 16
    assert ns == npair == 2 * nq
    packed = pack(amps, tile_index, capt, across)
    turned = [
        lax.ppermute(packed, ("reorder", "pair"), spread_perm(npair, nq, m)) for m in range(nq)
    ]
    late = lax.optimization_barrier((packed, cycle_ints, tile_index, slab, eps_occ, eps_vir))
    meta, mine, send, inv = prep(*late[1:], capt, across, nq)
    turned, send = lax.optimization_barrier((turned, send))
    theirs = swap(send, "pair", npair, 1)
    sums = multiply(0, meta, mine, turned, [], nq)
    partial = multiply(1, meta, theirs, turned, [sums], nq)
    parts = [partial[0]] + [swap(partial[e], "pair", npair, 2 * e) for e in range(1, nq)]
    new_amps, gram = update(tile_index, amps, ovov, history, inv, parts, capt, across)
    gram = sum([swap(gram, "pair", npair, n) for n in range(1, npair)], gram)
    sums = [gram] + [swap(gram, "reorder", nq, n) for n in range(1, nq)]
    return (new_amps, finish(sums, nhist, 1.0 / (TILE * ns)))


def solution(mesh):
    in_specs = (
        P("pair", "reorder", None, None),
        P(),
        P("pair", "reorder", None, None),
        P("pair", "reorder", None, None, None),
        P(None, "pair", "reorder", None, None),
        P(),
        P(),
        P(),
    )
    out_specs = (P("pair", "reorder", None, None), P())
    body = functools.partial(local, mesh.shape["pair"], mesh.shape["reorder"])
    return jax.shard_map(body, mesh=mesh, in_specs=in_specs, out_specs=out_specs, check_vma=False)
```

time: 264 us -> 71.7 us (0.27)
  local copies, waits for them, and re-layouts: 108 us -> 7.9 us
  waiting for transfers between devices: 67.1 us -> 16.4 us
  blocking collectives: 39.6 us -> 0 us
  starting transfers between devices: 3.73 us -> 26.2 us
  Pallas kernels: 0 us -> 20.1 us
  matrix products: 15.7 us -> 0 us
  other arithmetic: 14.2 us -> 0.01 us
  between operations: 15 us -> 0.84 us
    gather x10 -> x0, local copies, waits for them, and re-layouts: 54.9 us -> none  [the longest x4 30.9 us: cycle_block(): left = tiles[picks] * present[..., None].astype(tiles.dtype)]
    psum x1 -> x0, blocking collectives: 39.6 us -> none  [local(): cross, square = lax.psum((cross, square), ('reorder', 'pair'))]
    reduce_scatter x1 -> x0, waiting for transfers between devices: 37.1 us -> none  [local(): lax.psum_scatter(jax.vmap(full_row)(jnp.arange(occ_dev * lax.axis_size('p...]
    all_gather x1 -> x0, waiting for transfers between devices: 29.3 us -> none  [local(): rows_here = lax.all_gather(amps, 'reorder', axis=1, tiled=True)]
    reshape x4 -> x1, local copies, waits for them, and re-layouts: 26.9 us -> 0.45 us  [prep(): jnp.broadcast_to(vir, (across, ROWS, 2, 64)).reshape(across, ROWS, LANES)]
    ppermute x0 -> x18, starting transfers between devices: none -> 26.2 us  [the longest x14 14.3 us: swap(): return lax.ppermute(x, axis, [(n, n ^ step) for n in range(size)])]
    pallas_call x0 -> x6, Pallas kernels: none -> 20.1 us  [the longest x1 8.62 us: prep(): pl.pallas_call(functools.partial(prep_kernel, capt, across, nq, nmax), in...]
    ppermute x0 -> x18, waiting for transfers between devices: none -> 16.4 us  [the longest x14 16.4 us: swap(): return lax.ppermute(x, axis, [(n, n ^ step) for n in range(size)])]
  transfers between devices with their start and end apart: 3 -> 18, of which waited for: 2 -> 9; matrix products, arithmetic and copies ran while one was open for 16% -> 5% of each run, Pallas kernels for 0% -> 15%
where the time goes in v1:
time: 71.7 us; the launch traced here: 71.5 us
  starting transfers between devices  26.2 us (37%)
  Pallas kernels  20.1 us (28%)
  waiting for transfers between devices  16.4 us (23%)
  local copies, waits for them, and re-layouts  7.9 us (11%)
  between operations  0.84 us (1%)
    ppermute x14, waiting for transfers between devices, swap(): return lax.ppermute(x, axis, [(n, n ^ step) for n in range(size)])  16.4 us
    ppermute x14, starting transfers between devices, swap(): return lax.ppermute(x, axis, [(n, n ^ step) for n in range(size)])  14.3 us
    ppermute x4, starting transfers between devices, local(): lax.ppermute(packed, ('reorder', 'pair'), spread_perm(npair, nq, m))  11.9 us
    pallas_call x1, Pallas kernels, prep(): pl.pallas_call(functools.partial(prep_kernel, capt, across, nq, nmax), in...  8.62 us
    pallas_call x2, Pallas kernels, multiply(): pl.pallas_call(functools.partial(multiply_kernel, which, nq, nq * LIVE2 +...  4.87 us
    unnamed x22, local copies, waits for them, and re-layouts  4.53 us
    pallas_call x1, Pallas kernels, update(): pl.pallas_call(functools.partial(update_kernel, capt, across, nq), in_spe...  2.82 us
    pallas_call x1, Pallas kernels, pack(): pl.pallas_call(functools.partial(pack_kernel, capt, across), in_specs=[SM...  2.43 us
  transfers between devices with their start and end apart: 18, of which 9 were waited for; matrix products, arithmetic and copies ran while one was open for 5% of the time, Pallas kernels for 15%

profile of v1, /device:TPU:0, one launch (start us, length us, event | category | flops | bytes accessed | tf_op | source)
XLA Modules:
  0.0 71.5 jit_solution(10573856390201760970)
XLA Ops:
  0.6 2.4 %pack_amps.1 = bf16[24,32,128]{2,1,0:T(8,128)(2,1)} custom-call(s32[8,8,16]{2,1,0:T(8,128)} %ti_ref.4, bf16[1,2,16,4096]{3,2,1,0:T(8,128)(2,1)} %amps_ref.3), custom_call_target="tpu_custom_call" | custom-call | flops 100000000 | bytes 500000 | tf_op jit(solution)/shard_map/pack_amps/pallas_call | solution.py:62
  3.1 1.7 %collective-permute-start = (bf16[24,32,128]{2,1,0:T(8,128)(2,1)}, bf16[24,32,128]{2,1,0:T(8,128)(2,1)S(1)}, u32[]{:S(2)}, u32[]{:S(2)}) collective-permute-start(bf16[24,32,128]{2,1,0:T(8,128)(2,1)} %pack_amps.1), channel_id=1, source_target_pairs={{0,0},{1,1},{2,8},{3,9},{4,16},{5,17},{6,24},{7,25},{8,2},{9,3},{1... | collective-permute-start | bytes 589832 | tf_op jit(solution)/shard_map/ppermute | solution.py:388
  4.8 4.8 %collective-permute-start.1 = (bf16[24,32,128]{2,1,0:T(8,128)(2,1)}, bf16[24,32,128]{2,1,0:T(8,128)(2,1)S(1)}, u32[]{:S(2)}, u32[]{:S(2)}) collective-permute-start(bf16[24,32,128]{2,1,0:T(8,128)(2,1)} %pack_amps.1), channel_id=1, source_target_pairs={{0,8},{1,9},{2,0},{3,1},{4,24},{5,25},{6,16},{7,17},{8,10},{9,11},... | collective-permute-start | bytes 589832 | tf_op jit(solution)/shard_map/ppermute | solution.py:388
  9.6 3.5 %collective-permute-start.2 = (bf16[24,32,128]{2,1,0:T(8,128)(2,1)}, bf16[24,32,128]{2,1,0:T(8,128)(2,1)S(1)}, u32[]{:S(2)}, u32[]{:S(2)}) collective-permute-start(bf16[24,32,128]{2,1,0:T(8,128)(2,1)} %pack_amps.1), channel_id=1, source_target_pairs={{0,16},{1,17},{2,24},{3,25},{4,0},{5,1},{6,8},{7,9},{8,18},{9,19},... | collective-permute-start | bytes 589832 | tf_op jit(solution)/shard_map/ppermute | solution.py:388
  13.0 1.9 %collective-permute-start.3 = (bf16[24,32,128]{2,1,0:T(8,128)(2,1)}, bf16[24,32,128]{2,1,0:T(8,128)(2,1)S(1)}, u32[]{:S(2)}, u32[]{:S(2)}) collective-permute-start(bf16[24,32,128]{2,1,0:T(8,128)(2,1)} %pack_amps.1), channel_id=1, source_target_pairs={{0,24},{1,25},{2,16},{3,17},{4,8},{5,9},{6,0},{7,1},{8,26},{9,27},... | collective-permute-start | bytes 589832 | tf_op jit(solution)/shard_map/ppermute | solution.py:388
  14.9 1.1 %broadcast_in_dim.16 = f32[25,32,2]{2,1,0:T(8,128)S(1)} reshape(f32[1600]{0:T(1024)} %param.15) | data formatting | bytes 12800 | tf_op jit(solution)/shard_map/broadcast_in_dim | solution.py:184
  18.4 3.9 %copy-done = bf16[1,2,25,25,4096]{4,1,3,2,0:T(2,128)(2,1)S(1)} copy-done((bf16[1,2,25,25,4096]{4,1,3,2,0:T(2,128)(2,1)S(1)}, bf16[1,2,25,25,4096]{4,1,3,2,0:T(2,128)(2,1)}, u32[]{:S(2)}) %copy-start) | copy-done | bytes 10240024
  22.3 8.6 %prep_integrals.1 = (s32[1568]{0:T(1024)S(1)}, bf16[96,64,128]{2,1,0:T(8,128)(2,1)S(1)}, bf16[96,64,128]{2,1,0:T(8,128)(2,1)S(1)}, f32[2,16,4096]{2,1,0:T(8,128)S(1)}) custom-call(s32[8,8,16]{2,1,0:T(8,128)S(1)} %copy-done.3, s32[8]{0:T(128)S(1)} %copy-done.6, f32[200]{0:T(256)S(1)} %copy-done.5, bf16[625,64,128]{2,1,0:T(8,128)(2,1)S(1)} %bitcast.9, ...), custom_call_target="tpu_custom_call" | custom-call | flops 1000000000 | bytes 40000000 | tf_op jit(solution)/shard_map/prep_integrals/pallas_call | solution.py:191
  31.0 2.4 %multiply_own.1.refs_4_ = f32[97,32,128]{2,1,0:T(8,128)S(1)} custom-call(s32[1568]{0:T(1024)S(1)} %get-tuple-element.28.meta_ref, bf16[96,64,128]{2,1,0:T(8,128)(2,1)S(1)} %get-tuple-element.35.tiles_ref, bf16[24,32,128]{2,1,0:T(8,128)(2,1)S(1)} %collective-permute-done.refs_0_, bf16[24,32,128]{2,1,0:T(8,128)(2,1)S(1)} %collective-permute-done.1.refs_1_, ...), custom_call_target="tpu_custom_call" | custom-call | flops 1000000000 | bytes 10000000 | tf_op jit(solution)/shard_map/multiply_own/pallas_call | solution.py:270
  34.4 2.4 %multiply_sibling.1 = (bf16[24,32,128]{2,1,0:T(8,128)(2,1)S(1)}, bf16[24,32,128]{2,1,0:T(8,128)(2,1)S(1)}, bf16[24,32,128]{2,1,0:T(8,128)(2,1)S(1)}, bf16[24,32,128]{2,1,0:T(8,128)(2,1)S(1)}) custom-call(s32[1568]{0:T(1024)S(1)} %get-tuple-element.28.meta_ref, bf16[96,64,128]{2,1,0:T(8,128)(2,1)S(1)} %collective-permute-done.4.tiles_ref, ...), custom_call_target="tpu_custom_call" | custom-call | flops 1000000000 | bytes 10000000 | tf_op jit(solution)/shard_map/multiply_sibling/pallas_call | solution.py:270
  36.9 1.6 %collective-permute-start.6 = (bf16[24,32,128]{2,1,0:T(8,128)(2,1)S(1)}, bf16[24,32,128]{2,1,0:T(8,128)(2,1)S(1)}, u32[]{:S(2)}, u32[]{:S(2)}) collective-permute-start(bf16[24,32,128]{2,1,0:T(8,128)(2,1)S(1)} %get-tuple-element.38), channel_id=1, source_target_pairs={{0,4},{1,5},{2,6},{3,7},{4,0},{5,1},{6,2},{7,3},{8,12},{9,13},{10,... | collective-permute-start | bytes 589832 | tf_op jit(solution)/shard_map/ppermute | solution.py:367
  38.6 1.9 %collective-permute-start.7 = (bf16[24,32,128]{2,1,0:T(8,128)(2,1)S(1)}, bf16[24,32,128]{2,1,0:T(8,128)(2,1)S(1)}, u32[]{:S(2)}, u32[]{:S(2)}) collective-permute-start(bf16[24,32,128]{2,1,0:T(8,128)(2,1)S(1)} %get-tuple-element.39), channel_id=1, source_target_pairs={{0,6},{1,7},{2,4},{3,5},{4,2},{5,3},{6,0},{7,1},{8,14},{9,15},{10,... | collective-permute-start | bytes 589832 | tf_op jit(solution)/shard_map/ppermute | solution.py:367
  40.4 4.3 %collective-permute-done.5.refs_1_ = bf16[24,32,128]{2,1,0:T(8,128)(2,1)S(1)} collective-permute-done((bf16[24,32,128]{2,1,0:T(8,128)(2,1)S(1)}, bf16[24,32,128]{2,1,0:T(8,128)(2,1)S(1)}, u32[]{:S(2)}, u32[]{:S(2)}) %collective-permute-start.5) | collective-permute-done | bytes 196640 | tf_op jit(solution)/shard_map/ppermute | solution.py:367
  44.7 2.9 %collective-permute-done.6.refs_2_ = bf16[24,32,128]{2,1,0:T(8,128)(2,1)S(1)} collective-permute-done((bf16[24,32,128]{2,1,0:T(8,128)(2,1)S(1)}, bf16[24,32,128]{2,1,0:T(8,128)(2,1)S(1)}, u32[]{:S(2)}, u32[]{:S(2)}) %collective-permute-start.6) | collective-permute-done | bytes 196640 | tf_op jit(solution)/shard_map/ppermute | solution.py:367
  47.6 1.8 %collective-permute-done.7.refs_3_ = bf16[24,32,128]{2,1,0:T(8,128)(2,1)S(1)} collective-permute-done((bf16[24,32,128]{2,1,0:T(8,128)(2,1)S(1)}, bf16[24,32,128]{2,1,0:T(8,128)(2,1)S(1)}, u32[]{:S(2)}, u32[]{:S(2)}) %collective-permute-start.7) | collective-permute-done | bytes 196640 | tf_op jit(solution)/shard_map/ppermute | solution.py:367
  49.4 2.8 %update_amps.1 = (bf16[1,2,16,4096]{3,2,1,0:T(8,128)(2,1)}, f32[8,128]{1,0:T(8,128)S(1)}) custom-call(s32[8,8,16]{2,1,0:T(8,128)S(1)} %copy-done.3, bf16[1,2,16,4096]{3,2,1,0:T(8,128)(2,1)S(1)} %copy-done.2, bf16[1,2,16,4096]{3,2,1,0:T(8,128)(2,1)S(1)} %copy-done.4, bf16[6,1,2,16,4096]{4,3,2,1,0:T(8,128)(2,1)S(1)} %copy-done.1, ...), custom_call_target="tpu_custom_call" | custom-call | flops 100000000 | bytes 6000000 | tf_op jit(solution)/shard_map/update_amps/pallas_call | solution.py:330
  52.9 1.5 %collective-permute-start.13 = (f32[8,128]{1,0:T(8,128)S(1)}, f32[8,128]{1,0:T(8,128)S(1)}, u32[]{:S(2)}, u32[]{:S(2)}) collective-permute-start(f32[8,128]{1,0:T(8,128)S(1)} %get-tuple-element.41), channel_id=1, source_target_pairs={{0,6},{1,7},{2,4},{3,5},{4,2},{5,3},{6,0},{7,1},{8,14},{9,15},{10,... | collective-permute-start | bytes 12296 | tf_op jit(solution)/shard_map/ppermute | solution.py:367
  55.2 1.4 %collective-permute-start.11 = (f32[8,128]{1,0:T(8,128)S(1)}, f32[8,128]{1,0:T(8,128)S(1)}, u32[]{:S(2)}, u32[]{:S(2)}) collective-permute-start(f32[8,128]{1,0:T(8,128)S(1)} %get-tuple-element.41), channel_id=1, source_target_pairs={{0,4},{1,5},{2,6},{3,7},{4,0},{5,1},{6,2},{7,3},{8,12},{9,13},{10,... | collective-permute-start | bytes 12296 | tf_op jit(solution)/shard_map/ppermute | solution.py:367
  56.6 1.2 %collective-permute-start.9 = (f32[8,128]{1,0:T(8,128)S(1)}, f32[8,128]{1,0:T(8,128)S(1)}, u32[]{:S(2)}, u32[]{:S(2)}) collective-permute-start(f32[8,128]{1,0:T(8,128)S(1)} %get-tuple-element.41), channel_id=1, source_target_pairs={{0,2},{1,3},{2,0},{3,1},{4,6},{5,7},{6,4},{7,5},{8,10},{9,11},{10,... | collective-permute-start | bytes 12296 | tf_op jit(solution)/shard_map/ppermute | solution.py:367
  60.3 1.0 %collective-permute-start.15 = (f32[8,128]{1,0:T(8,128)S(1)}, f32[8,128]{1,0:T(8,128)S(1)}, u32[]{:S(2)}, u32[]{:S(2)}) collective-permute-start(f32[8,128]{1,0:T(8,128)S(1)} %add_add_fusion.refs_0_), channel_id=1, source_target_pairs={{0,8},{8,0},{16,24},{24,16},{1,9},{9,1},{17,25},{25,17},{2,10},{10... | collective-permute-start | bytes 12296 | tf_op jit(solution)/shard_map/ppermute | solution.py:367
  61.3 2.8 %collective-permute-start.16 = (f32[8,128]{1,0:T(8,128)S(1)}, f32[8,128]{1,0:T(8,128)S(1)}, u32[]{:S(2)}, u32[]{:S(2)}) collective-permute-start(f32[8,128]{1,0:T(8,128)S(1)} %add_add_fusion.refs_0_), channel_id=1, source_target_pairs={{0,16},{8,24},{16,0},{24,8},{1,17},{9,25},{17,1},{25,9},{2,18},{10... | collective-permute-start | bytes 12296 | tf_op jit(solution)/shard_map/ppermute | solution.py:367
  64.7 1.1 %collective-permute-done.16.refs_2_ = f32[8,128]{1,0:T(8,128)S(1)} collective-permute-done((f32[8,128]{1,0:T(8,128)S(1)}, f32[8,128]{1,0:T(8,128)S(1)}, u32[]{:S(2)}, u32[]{:S(2)}) %collective-permute-start.16) | collective-permute-done | bytes 4128 | tf_op jit(solution)/shard_map/ppermute | solution.py:367
  65.8 3.7 %collective-permute-done.17.refs_3_ = f32[8,128]{1,0:T(8,128)S(1)} collective-permute-done((f32[8,128]{1,0:T(8,128)S(1)}, f32[8,128]{1,0:T(8,128)S(1)}, u32[]{:S(2)}, u32[]{:S(2)}) %collective-permute-start.17) | collective-permute-done | bytes 4128 | tf_op jit(solution)/shard_map/ppermute | solution.py:367
  70.1 1.4 %finish_gram.1 = f32[7]{0:T(128)} custom-call(f32[8,128]{1,0:T(8,128)} %copy-done.7, f32[8,128]{1,0:T(8,128)} %copy-done.8, f32[8,128]{1,0:T(8,128)} %copy-done.9, f32[8,128]{1,0:T(8,128)} %copy-done.10), custom_call_target="tpu_custom_call" | custom-call | tf_op jit(solution)/shard_map/finish_gram/pallas_call | solution.py:357
  (47 shorter events, 8.6 us)
Async XLA Ops:
  3.1 15.3 %copy-start.3 = (s32[8,8,16]{2,1,0:T(8,128)S(1)}, s32[8,8,16]{2,1,0:T(8,128)}, u32[]{:S(2)}) copy-start(s32[8,8,16]{2,1,0:T(8,128)} %ti_ref.4) | copy-start | bytes 12292
  3.1 15.3 %copy-start.5 = (f32[200]{0:T(256)S(1)}, f32[200]{0:T(256)}, u32[]{:S(2)}) copy-start(f32[200]{0:T(256)} %occ_ref) | copy-start | bytes 2404
  3.1 15.3 %copy-start.6 = (s32[8]{0:T(128)S(1)}, s32[8]{0:T(128)}, u32[]{:S(2)}) copy-start(s32[8]{0:T(128)} %slab_ref) | copy-start | bytes 100
  3.1 27.9 %collective-permute-start = (bf16[24,32,128]{2,1,0:T(8,128)(2,1)}, bf16[24,32,128]{2,1,0:T(8,128)(2,1)S(1)}, u32[]{:S(2)}, u32[]{:S(2)}) collective-permute-start(bf16[24,32,128]{2,1,0:T(8,128)(2,1)} %pack_amps.1), channel_id=1, source_target_pairs={{0,0},{1,1},{2,8},{3,9},{4,16},{5,17},{6,24},{7,25},{8,2},{9,3},{1... | collective-permute-start | bytes 589832 | tf_op jit(solution)/shard_map/ppermute | solution.py:388
  4.8 26.2 %collective-permute-start.1 = (bf16[24,32,128]{2,1,0:T(8,128)(2,1)}, bf16[24,32,128]{2,1,0:T(8,128)(2,1)S(1)}, u32[]{:S(2)}, u32[]{:S(2)}) collective-permute-start(bf16[24,32,128]{2,1,0:T(8,128)(2,1)} %pack_amps.1), channel_id=1, source_target_pairs={{0,8},{1,9},{2,0},{3,1},{4,24},{5,25},{6,16},{7,17},{8,10},{9,11},... | collective-permute-start | bytes 589832 | tf_op jit(solution)/shard_map/ppermute | solution.py:388
  9.6 21.4 %collective-permute-start.2 = (bf16[24,32,128]{2,1,0:T(8,128)(2,1)}, bf16[24,32,128]{2,1,0:T(8,128)(2,1)S(1)}, u32[]{:S(2)}, u32[]{:S(2)}) collective-permute-start(bf16[24,32,128]{2,1,0:T(8,128)(2,1)} %pack_amps.1), channel_id=1, source_target_pairs={{0,16},{1,17},{2,24},{3,25},{4,0},{5,1},{6,8},{7,9},{8,18},{9,19},... | collective-permute-start | bytes 589832 | tf_op jit(solution)/shard_map/ppermute | solution.py:388
  13.0 17.9 %collective-permute-start.3 = (bf16[24,32,128]{2,1,0:T(8,128)(2,1)}, bf16[24,32,128]{2,1,0:T(8,128)(2,1)S(1)}, u32[]{:S(2)}, u32[]{:S(2)}) collective-permute-start(bf16[24,32,128]{2,1,0:T(8,128)(2,1)} %pack_amps.1), channel_id=1, source_target_pairs={{0,24},{1,25},{2,16},{3,17},{4,8},{5,9},{6,0},{7,1},{8,26},{9,27},... | collective-permute-start | bytes 589832 | tf_op jit(solution)/shard_map/ppermute | solution.py:388
  31.0 3.5 %collective-permute-start.4 = (bf16[96,64,128]{2,1,0:T(8,128)(2,1)S(1)}, bf16[96,64,128]{2,1,0:T(8,128)(2,1)S(1)}, u32[]{:S(2)}, u32[]{:S(2)}) collective-permute-start(bf16[96,64,128]{2,1,0:T(8,128)(2,1)S(1)} %get-tuple-element.30), channel_id=1, source_target_pairs={{0,1},{1,0},{2,3},{3,2},{4,5},{5,4},{6,7},{7,6},{8,9},{9,8},{10,11... | collective-permute-start | bytes 4718600 | tf_op jit(solution)/shard_map/ppermute | solution.py:367
  33.5 15.9 %copy-start.1 = (bf16[6,1,2,16,4096]{4,3,2,1,0:T(8,128)(2,1)S(1)}, bf16[6,1,2,16,4096]{4,3,2,1,0:T(8,128)(2,1)}, u32[]{:S(2)}) copy-start(bf16[6,1,2,16,4096]{4,3,2,1,0:T(8,128)(2,1)} %hist_ref.1) | copy-start | bytes 4718596
  33.5 15.9 %copy-start.2 = (bf16[1,2,16,4096]{3,2,1,0:T(8,128)(2,1)S(1)}, bf16[1,2,16,4096]{3,2,1,0:T(8,128)(2,1)}, u32[]{:S(2)}) copy-start(bf16[1,2,16,4096]{3,2,1,0:T(8,128)(2,1)} %amps_ref.3) | copy-start | bytes 786436
  33.5 15.9 %copy-start.4 = (bf16[1,2,16,4096]{3,2,1,0:T(8,128)(2,1)S(1)}, bf16[1,2,16,4096]{3,2,1,0:T(8,128)(2,1)}, u32[]{:S(2)}) copy-start(bf16[1,2,16,4096]{3,2,1,0:T(8,128)(2,1)} %ovov_ref.1) | copy-start | bytes 786436
  36.9 7.8 %collective-permute-start.5 = (bf16[24,32,128]{2,1,0:T(8,128)(2,1)S(1)}, bf16[24,32,128]{2,1,0:T(8,128)(2,1)S(1)}, u32[]{:S(2)}, u32[]{:S(2)}) collective-permute-start(bf16[24,32,128]{2,1,0:T(8,128)(2,1)S(1)} %get-tuple-element.37), channel_id=1, source_target_pairs={{0,2},{1,3},{2,0},{3,1},{4,6},{5,7},{6,4},{7,5},{8,10},{9,11},{10,... | collective-permute-start | bytes 589832 | tf_op jit(solution)/shard_map/ppermute | solution.py:367
  36.9 10.6 %collective-permute-start.6 = (bf16[24,32,128]{2,1,0:T(8,128)(2,1)S(1)}, bf16[24,32,128]{2,1,0:T(8,128)(2,1)S(1)}, u32[]{:S(2)}, u32[]{:S(2)}) collective-permute-start(bf16[24,32,128]{2,1,0:T(8,128)(2,1)S(1)} %get-tuple-element.38), channel_id=1, source_target_pairs={{0,4},{1,5},{2,6},{3,7},{4,0},{5,1},{6,2},{7,3},{8,12},{9,13},{10,... | collective-permute-start | bytes 589832 | tf_op jit(solution)/shard_map/ppermute | solution.py:367
  38.6 10.8 %collective-permute-start.7 = (bf16[24,32,128]{2,1,0:T(8,128)(2,1)S(1)}, bf16[24,32,128]{2,1,0:T(8,128)(2,1)S(1)}, u32[]{:S(2)}, u32[]{:S(2)}) collective-permute-start(bf16[24,32,128]{2,1,0:T(8,128)(2,1)S(1)} %get-tuple-element.39), channel_id=1, source_target_pairs={{0,6},{1,7},{2,4},{3,5},{4,2},{5,3},{6,0},{7,1},{8,14},{9,15},{10,... | collective-permute-start | bytes 589832 | tf_op jit(solution)/shard_map/ppermute | solution.py:367
  52.2 4.4 %collective-permute-start.14 = (f32[8,128]{1,0:T(8,128)S(1)}, f32[8,128]{1,0:T(8,128)S(1)}, u32[]{:S(2)}, u32[]{:S(2)}) collective-permute-start(f32[8,128]{1,0:T(8,128)S(1)} %get-tuple-element.41), channel_id=1, source_target_pairs={{0,7},{1,6},{2,5},{3,4},{4,3},{5,2},{6,1},{7,0},{8,15},{9,14},{10,... | collective-permute-start | bytes 12296 | tf_op jit(solution)/shard_map/ppermute | solution.py:367
  52.9 5.0 %collective-permute-start.13 = (f32[8,128]{1,0:T(8,128)S(1)}, f32[8,128]{1,0:T(8,128)S(1)}, u32[]{:S(2)}, u32[]{:S(2)}) collective-permute-start(f32[8,128]{1,0:T(8,128)S(1)} %get-tuple-element.41), channel_id=1, source_target_pairs={{0,6},{1,7},{2,4},{3,5},{4,2},{5,3},{6,0},{7,1},{8,14},{9,15},{10,... | collective-permute-start | bytes 12296 | tf_op jit(solution)/shard_map/ppermute | solution.py:367
  54.4 4.1 %collective-permute-start.12 = (f32[8,128]{1,0:T(8,128)S(1)}, f32[8,128]{1,0:T(8,128)S(1)}, u32[]{:S(2)}, u32[]{:S(2)}) collective-permute-start(f32[8,128]{1,0:T(8,128)S(1)} %get-tuple-element.41), channel_id=1, source_target_pairs={{0,5},{1,4},{2,7},{3,6},{4,1},{5,0},{6,3},{7,2},{8,13},{9,12},{10,... | collective-permute-start | bytes 12296 | tf_op jit(solution)/shard_map/ppermute | solution.py:367
  55.2 3.6 %collective-permute-start.11 = (f32[8,128]{1,0:T(8,128)S(1)}, f32[8,128]{1,0:T(8,128)S(1)}, u32[]{:S(2)}, u32[]{:S(2)}) collective-permute-start(f32[8,128]{1,0:T(8,128)S(1)} %get-tuple-element.41), channel_id=1, source_target_pairs={{0,4},{1,5},{2,6},{3,7},{4,0},{5,1},{6,2},{7,3},{8,12},{9,13},{10,... | collective-permute-start | bytes 12296 | tf_op jit(solution)/shard_map/ppermute | solution.py:367
  56.6 3.0 %collective-permute-start.10 = (f32[8,128]{1,0:T(8,128)S(1)}, f32[8,128]{1,0:T(8,128)S(1)}, u32[]{:S(2)}, u32[]{:S(2)}) collective-permute-start(f32[8,128]{1,0:T(8,128)S(1)} %get-tuple-element.41), channel_id=1, source_target_pairs={{0,3},{1,2},{2,1},{3,0},{4,7},{5,6},{6,5},{7,4},{8,11},{9,10},{10,... | collective-permute-start | bytes 12296 | tf_op jit(solution)/shard_map/ppermute | solution.py:367
  56.6 3.6 %collective-permute-start.9 = (f32[8,128]{1,0:T(8,128)S(1)}, f32[8,128]{1,0:T(8,128)S(1)}, u32[]{:S(2)}, u32[]{:S(2)}) collective-permute-start(f32[8,128]{1,0:T(8,128)S(1)} %get-tuple-element.41), channel_id=1, source_target_pairs={{0,2},{1,3},{2,0},{3,1},{4,6},{5,7},{6,4},{7,5},{8,10},{9,11},{10,... | collective-permute-start | bytes 12296 | tf_op jit(solution)/shard_map/ppermute | solution.py:367
  57.9 2.4 %collective-permute-start.8 = (f32[8,128]{1,0:T(8,128)S(1)}, f32[8,128]{1,0:T(8,128)S(1)}, u32[]{:S(2)}, u32[]{:S(2)}) collective-permute-start(f32[8,128]{1,0:T(8,128)S(1)} %get-tuple-element.41), channel_id=1, source_target_pairs={{0,1},{1,0},{2,3},{3,2},{4,5},{5,4},{6,7},{7,6},{8,9},{9,8},{10,11... | collective-permute-start | bytes 12296 | tf_op jit(solution)/shard_map/ppermute | solution.py:367
  60.3 4.5 %collective-permute-start.15 = (f32[8,128]{1,0:T(8,128)S(1)}, f32[8,128]{1,0:T(8,128)S(1)}, u32[]{:S(2)}, u32[]{:S(2)}) collective-permute-start(f32[8,128]{1,0:T(8,128)S(1)} %add_add_fusion.refs_0_), channel_id=1, source_target_pairs={{0,8},{8,0},{16,24},{24,16},{1,9},{9,1},{17,25},{25,17},{2,10},{10... | collective-permute-start | bytes 12296 | tf_op jit(solution)/shard_map/ppermute | solution.py:367
  61.3 4.5 %collective-permute-start.16 = (f32[8,128]{1,0:T(8,128)S(1)}, f32[8,128]{1,0:T(8,128)S(1)}, u32[]{:S(2)}, u32[]{:S(2)}) collective-permute-start(f32[8,128]{1,0:T(8,128)S(1)} %add_add_fusion.refs_0_), channel_id=1, source_target_pairs={{0,16},{8,24},{16,0},{24,8},{1,17},{9,25},{17,1},{25,9},{2,18},{10... | collective-permute-start | bytes 12296 | tf_op jit(solution)/shard_map/ppermute | solution.py:367
  64.1 5.4 %collective-permute-start.17 = (f32[8,128]{1,0:T(8,128)S(1)}, f32[8,128]{1,0:T(8,128)S(1)}, u32[]{:S(2)}, u32[]{:S(2)}) collective-permute-start(f32[8,128]{1,0:T(8,128)S(1)} %add_add_fusion.refs_0_), channel_id=1, source_target_pairs={{0,24},{8,16},{16,8},{24,0},{1,25},{9,17},{17,9},{25,1},{2,26},{10... | collective-permute-start | bytes 12296 | tf_op jit(solution)/shard_map/ppermute | solution.py:367
  (5 other events, 22.2 us)

commit v2 on v1

--- a/solution.py
+++ b/solution.py
@@ -74,9 +74,11 @@
 
 
 def prep_kernel(
-    capt, across, nq, nmax, ti_ref, slab_ref, occ_ref, ints_ref, row_ref, col_ref,
-    meta_ref, mine_ref, send_ref, inv_ref, wide_ref, den_ref, tab_ref,
+    capt, across, nq, nmax, ti_ref, hbm_ref,
+    meta_ref, mine_ref, send_ref, ints_ref, wide_ref, tab_ref, sem,
 ):
+    fetch_ints = pltpu.make_async_copy(hbm_ref, ints_ref, sem)
+    fetch_ints.start()
     dead = across * across
     me = lax.axis_index("pair")
     sibling = me ^ 1
@@ -90,8 +92,8 @@
         parity = lax.rem(k, 2)
 
         def one_first(q, cnt):
-            i = (plane ^ q) * 2 + (who & 1)
-            out = (lax.shift_right_logical(who, 1) ^ plane ^ q) * LIVE2
+            i = who ^ (q * 2)
+            out = q * LIVE2
             for a in range(across + 1):
                 tab_ref[a] = -1
             live_in = jnp.int32(0)
@@ -153,60 +155,74 @@
 
         lax.fori_loop(0, (total + 3) // 4, fetch, 0)
 
-    gather(2, build(2, sibling, me), send_ref)
-    gather(0, build(0, me, me), mine_ref)
+    total_send = build(2, sibling, me)
+    total_mine = build(0, me, me)
     build(1, me, sibling)
-
-    occ_i = occ_ref[slab_ref[me]]
+    fetch_ints.wait()
+    gather(2, total_send, send_ref)
+    gather(0, total_mine, mine_ref)
+
+
+def prep(cycle_ints, ti, capt, across, nq):
+    nmax = nq * LIVE2 + 8
+    ints = cycle_ints[0].transpose(1, 2, 0, 3).reshape(across, across, 2, ROWS, LANES)
+    ints = ints.transpose(0, 1, 3, 2, 4).reshape(across * across, 2 * ROWS, LANES)
+    tiles = jax.ShapeDtypeStruct((nq * LIVE2, 2 * ROWS, LANES), BF16)
+    return pl.pallas_call(
+        functools.partial(prep_kernel, capt, across, nq, nmax),
+        in_specs=[SMEM, pl.BlockSpec(memory_space=pltpu.HBM)],
+        out_specs=[SMEM, VMEM, VMEM],
+        scratch_shapes=[
+            pltpu.VMEM(ints.shape, BF16),
+            pltpu.VMEM((8, 2 * ROWS, LANES), F32),
+            pltpu.SMEM((64,), jnp.int32),
+            pltpu.SemaphoreType.DMA,
+        ],
+        out_shape=[jax.ShapeDtypeStruct((15 * nmax + 8,), jnp.int32), tiles, tiles],
+        compiler_params=pltpu.CompilerParams(vmem_limit_bytes=53 * 1024 * 1024),
+        cost_estimate=pl.CostEstimate(flops=10**9, bytes_accessed=40 * 10**6, transcendentals=0),
+        name="prep_integrals",
+    )(ti, ints)
+
+
+def denom_kernel(capt, across, ti_ref, slab_ref, occ_ref, vir_ref, inv_ref, row_ref, col_ref):
+    first = lax.axis_index("pair")
+    second = lax.axis_index("reorder") * 2
+    occ_i = occ_ref[slab_ref[first]]
+    low = lax.broadcasted_iota(jnp.int32, (8, LANES), 1) < 64
     for jj in range(2):
-        occ = occ_i + occ_ref[slab_ref[second + jj]]
-
-        def denom(s, carry):
-            idx = ti_ref[me, second + jj, s]
+        for s in range(capt):
+            idx = ti_ref[first, second + jj, s]
             row = row_of(idx, across)
             a = jnp.minimum(row, across - 1)
             b = idx - row * across
-            at = pl.multiple_of((jj * capt + s) * ROWS, ROWS)
-            den_ref[pl.ds(at, ROWS), :] = 1.0 / ((occ - row_ref[a]) - col_ref[b])
-            return carry
-
-        lax.fori_loop(0, capt, denom, 0)
-        for p in range(ROWS):
-            for g in range(capt // 8):
-                inv_ref[jj, g * 8 : (g + 1) * 8, p * LANES : (p + 1) * LANES] = den_ref[
-                    pl.ds((jj * capt + g * 8) * ROWS + p, 8, stride=ROWS), :
-                ]
-
-
-def prep(cycle_ints, ti, slab, eps_occ, eps_vir, capt, across, nq):
-    nmax = nq * LIVE2 + 8
-    vir = eps_vir.reshape(across, ROWS, 2, 1)
-    row_table = jnp.broadcast_to(vir, (across, ROWS, 2, 64)).reshape(across, ROWS, LANES)
-    col_table = jnp.broadcast_to(
-        eps_vir.reshape(across, 1, 1, 64), (across, 1, 2, 64)
-    ).reshape(across, 1, LANES)
-    ints = cycle_ints[0].transpose(1, 2, 0, 3).reshape(across, across, 2, ROWS, LANES)
-    ints = ints.transpose(0, 1, 3, 2, 4).reshape(across * across, 2 * ROWS, LANES)
-    tiles = jax.ShapeDtypeStruct((nq * LIVE2, 2 * ROWS, LANES), BF16)
-    return pl.pallas_call(
-        functools.partial(prep_kernel, capt, across, nq, nmax),
-        in_specs=[SMEM, SMEM, SMEM, VMEM, VMEM, VMEM],
-        out_specs=[SMEM, VMEM, VMEM, VMEM],
-        scratch_shapes=[
-            pltpu.VMEM((8, 2 * ROWS, LANES), F32),
-            pltpu.VMEM((2 * capt * ROWS, LANES), F32),
-            pltpu.SMEM((64,), jnp.int32),
-        ],
-        out_shape=[
-            jax.ShapeDtypeStruct((15 * nmax + 8,), jnp.int32),
-            tiles,
-            tiles,
-            jax.ShapeDtypeStruct((2, capt, TILE * TILE), F32),
-        ],
-        compiler_params=pltpu.CompilerParams(vmem_limit_bytes=32 * 1024 * 1024),
-        cost_estimate=pl.CostEstimate(flops=10**9, bytes_accessed=40 * 10**6, transcendentals=0),
-        name="prep_integrals",
-    )(ti, slab, eps_occ, ints, row_table, col_table)
+            row_ref[jj * capt + s] = vir_ref[a]
+            col_ref[jj * capt + s] = vir_ref[b]
+    for jj in range(2):
+        occ = occ_i + occ_ref[slab_ref[second + jj]]
+        for g in range(capt // 8):
+            here = pl.ds(jj * capt + g * 8, 8)
+            rows = occ - row_ref[here]
+            col = col_ref[here]
+            cols = jnp.concatenate([col, col], axis=1)
+            for p in range(ROWS):
+                even = jnp.broadcast_to(rows[:, 2 * p : 2 * p + 1], (8, LANES))
+                odd = jnp.broadcast_to(rows[:, 2 * p + 1 : 2 * p + 2], (8, LANES))
+                inv_ref[jj, g * 8 : (g + 1) * 8, p * LANES : (p + 1) * LANES] = 1.0 / (
+                    jnp.where(low, even, odd) - cols
+                )
+
+
+def denominators(ti, slab, eps_occ, eps_vir, capt, across):
+    return pl.pallas_call(
+        functools.partial(denom_kernel, capt, across),
+        in_specs=[SMEM, SMEM, SMEM, VMEM],
+        out_specs=VMEM,
+        scratch_shapes=[pltpu.VMEM((2 * capt, 64), F32)] * 2,
+        out_shape=jax.ShapeDtypeStruct((2, capt, TILE * TILE), F32),
+        cost_estimate=pl.CostEstimate(flops=10**7, bytes_accessed=10**6, transcendentals=0),
+        name="denominators",
+    )(ti, slab, eps_occ, eps_vir.reshape(across, 64))
 
 
 def multiply_kernel(which, nq, nmax, unroll, meta_ref, tiles_ref, *refs):
@@ -319,13 +335,14 @@
 
             accs = lax.fori_loop(0, ROWS, chunk, accs, unroll=8)
     for m in range(8):
+        row = jnp.zeros((1, LANES), F32)
         if m <= nhist:
-            gram_ref[m : m + 1] = jnp.sum(accs[m], axis=0, keepdims=True)
-        else:
-            gram_ref[m : m + 1] = jnp.zeros((1, LANES), F32)
-
-
-def update(ti, amps, ovov, history, inv, parts, capt, across):
+            row = jnp.sum(accs[m], axis=0, keepdims=True)
+        for n in range(gram_ref.shape[0]):
+            gram_ref[n, m : m + 1] = row
+
+
+def update(ti, amps, ovov, history, inv, parts, copies, capt, across):
     nq = len(parts)
     return pl.pallas_call(
         functools.partial(update_kernel, capt, across, nq),
@@ -333,7 +350,7 @@
         out_specs=[VMEM, VMEM],
         out_shape=[
             jax.ShapeDtypeStruct(amps.shape, BF16),
-            jax.ShapeDtypeStruct((8, LANES), F32),
+            jax.ShapeDtypeStruct((copies, 8, LANES), F32),
         ],
         scratch_shapes=[pltpu.VMEM(((LIVE2 + capt) * ROWS, LANES), F32)],
         compiler_params=pltpu.CompilerParams(vmem_limit_bytes=24 * 1024 * 1024),
@@ -343,9 +360,7 @@
 
 
 def finish_kernel(nhist, scale, *refs):
-    total = refs[0][...]
-    for ref in refs[1:-1]:
-        total = total + ref[...]
+    total = jnp.sum(refs[0][...], axis=0)
     total = jnp.sum(total, axis=1, keepdims=True)
     row = lax.broadcasted_iota(jnp.int32, total.shape, 0)
     total = jnp.where(row == nhist, jnp.sqrt(jnp.maximum(total, 0.0)), total) * scale
@@ -356,24 +371,15 @@
 def finish(sums, nhist, scale):
     return pl.pallas_call(
         functools.partial(finish_kernel, nhist, scale),
-        in_specs=[VMEM] * len(sums),
+        in_specs=[VMEM],
         out_specs=SMEM,
         out_shape=jax.ShapeDtypeStruct((nhist + 1,), F32),
         name="finish_gram",
-    )(*sums)
+    )(sums)
 
 
 def swap(x, axis, size, step):
     return lax.ppermute(x, axis, [(n, n ^ step) for n in range(size)])
-
-
-def spread_perm(npair, nq, m):
-    pairs = []
-    for plane in range(nq):
-        for pair in range(npair):
-            to = ((pair // 2) ^ m) * npair + 2 * plane + pair % 2
-            pairs.append((plane * npair + pair, to))
-    return pairs
 
 
 def local(npair, nq, amps, tile_index, ovov, cycle_ints, history, slab, eps_occ, eps_vir):
@@ -384,19 +390,26 @@
     assert occ_dev == 1 and jdev == 2 and tile_area == TILE * TILE and capt == 16
     assert ns == npair == 2 * nq
     packed = pack(amps, tile_index, capt, across)
+    blocks = lax.all_gather(packed, "reorder")
+    late = lax.optimization_barrier((blocks, cycle_ints, tile_index))
+    meta, mine, send = prep(*late[1:], capt, across, nq)
+    chip = lax.axis_index("pair") // 2
     turned = [
-        lax.ppermute(packed, ("reorder", "pair"), spread_perm(npair, nq, m)) for m in range(nq)
+        lax.dynamic_index_in_dim(blocks, chip ^ e, 0, keepdims=False) for e in range(nq)
     ]
-    late = lax.optimization_barrier((packed, cycle_ints, tile_index, slab, eps_occ, eps_vir))
-    meta, mine, send, inv = prep(*late[1:], capt, across, nq)
+    turned = [turned[0]] + [swap(turned[e], "pair", npair, 2 * e) for e in range(1, nq)]
     turned, send = lax.optimization_barrier((turned, send))
     theirs = swap(send, "pair", npair, 1)
     sums = multiply(0, meta, mine, turned, [], nq)
     partial = multiply(1, meta, theirs, turned, [sums], nq)
     parts = [partial[0]] + [swap(partial[e], "pair", npair, 2 * e) for e in range(1, nq)]
-    new_amps, gram = update(tile_index, amps, ovov, history, inv, parts, capt, across)
-    gram = sum([swap(gram, "pair", npair, n) for n in range(1, npair)], gram)
-    sums = [gram] + [swap(gram, "reorder", nq, n) for n in range(1, nq)]
+    late = lax.optimization_barrier((partial[0], tile_index, slab, eps_occ, eps_vir))
+    inv = denominators(*late[1:], capt, across)
+    new_amps, gram = update(
+        tile_index, amps, ovov, history, inv, parts, npair, capt, across
+    )
+    gram = lax.all_to_all(gram, "pair", split_axis=0, concat_axis=0, tiled=True)
+    sums = lax.all_gather(jnp.sum(gram, axis=0), "reorder")
     return (new_amps, finish(sums, nhist, 1.0 / (TILE * ns)))
 
 

time: 71.7 us -> 82.1 us (1.15)
  blocking collectives: 0 us -> 42.7 us
  starting transfers between devices: 26.2 us -> 7.17 us
  waiting for transfers between devices: 16.4 us -> 4.84 us
  local copies, waits for them, and re-layouts: 7.9 us -> 3.2 us
  Pallas kernels: 20.1 us -> 23.1 us
    all_gather x0 -> x2, blocking collectives: none -> 35.1 us  [the longest x1 21.5 us: local(): blocks = lax.all_gather(packed, 'reorder')]
    ppermute x4 -> x0, starting transfers between devices: 11.9 us -> none  [local(): lax.ppermute(packed, ('reorder', 'pair'), spread_perm(npair, nq, m))]
    ppermute x14 -> x7, waiting for transfers between devices: 16.4 us -> 4.84 us  [swap(): return lax.ppermute(x, axis, [(n, n ^ step) for n in range(size)])]
    all_to_all x0 -> x1, blocking collectives: none -> 7.57 us  [local(): gram = lax.all_to_all(gram, 'pair', split_axis=0, concat_axis=0, tiled=True)]
    ppermute x14 -> x7, starting transfers between devices: 14.3 us -> 7.17 us  [swap(): return lax.ppermute(x, axis, [(n, n ^ step) for n in range(size)])]
    broadcast_in_dim x5 -> x0, local copies, waits for them, and re-layouts: 2.91 us -> none  [the longest x2 2.04 us: prep(): jnp.broadcast_to(vir, (across, ROWS, 2, 64)).reshape(across, ROWS, LANES)]
    pallas_call x0 -> x1, Pallas kernels: none -> 2.6 us  [denominators(): pl.pallas_call(functools.partial(denom_kernel, capt, across), in_specs=[S...]
    unnamed x22 -> x16, local copies, waits for them, and re-layouts: 4.53 us -> 2.47 us
  transfers between devices with their start and end apart: 18 -> 7, of which waited for: 9 -> 2; matrix products, arithmetic and copies ran while one was open for 5% -> 1% of each run, Pallas kernels for 15% -> 18%
where the time goes in v2:
time: 82.1 us; the launch traced here: 81.9 us
  blocking collectives  42.7 us (52%)
  Pallas kernels  23.1 us (28%)
  starting transfers between devices  7.17 us (9%)
  waiting for transfers between devices  4.84 us (6%)
  local copies, waits for them, and re-layouts  3.2 us (4%)
  between operations  0.83 us (1%)
    all_gather x1, blocking collectives, local(): blocks = lax.all_gather(packed, 'reorder')  21.5 us
    all_gather x1, blocking collectives, local(): sums = lax.all_gather(jnp.sum(gram, axis=0), 'reorder')  13.7 us
    pallas_call x1, Pallas kernels, prep(): pl.pallas_call(functools.partial(prep_kernel, capt, across, nq, nmax), in...  9.03 us
    all_to_all x1, blocking collectives, local(): gram = lax.all_to_all(gram, 'pair', split_axis=0, concat_axis=0, tiled=True)  7.57 us
    ppermute x7, starting transfers between devices, swap(): return lax.ppermute(x, axis, [(n, n ^ step) for n in range(size)])  7.17 us
    pallas_call x2, Pallas kernels, multiply(): pl.pallas_call(functools.partial(multiply_kernel, which, nq, nq * LIVE2 +...  4.87 us
    ppermute x7, waiting for transfers between devices, swap(): return lax.ppermute(x, axis, [(n, n ^ step) for n in range(size)])  4.84 us
    pallas_call x1, Pallas kernels, update(): pl.pallas_call(functools.partial(update_kernel, capt, across, nq), in_spe...  2.81 us
  transfers between devices with their start and end apart: 7, of which 2 were waited for; matrix products, arithmetic and copies ran while one was open for 1% of the time, Pallas kernels for 18%

profile of v2, /device:TPU:0, one launch (start us, length us, event | category | flops | bytes accessed | tf_op | source)
XLA Modules:
  0.0 81.9 jit_solution(11982955877556398851)
XLA Ops:
  0.7 2.4 %pack_amps.1 = bf16[24,32,128]{2,1,0:T(8,128)(2,1)} custom-call(s32[8,8,16]{2,1,0:T(8,128)} %ti_ref.5, bf16[1,2,16,4096]{3,2,1,0:T(8,128)(2,1)} %amps_ref.3), custom_call_target="tpu_custom_call" | custom-call | flops 100000000 | bytes 500000 | tf_op jit(solution)/shard_map/pack_amps/pallas_call | solution.py:62
  3.1 21.5 %all-gather = bf16[96,32,128]{2,1,0:T(8,128)(2,1)S(1)} all-gather(bf16[24,32,128]{2,1,0:T(8,128)(2,1)} %pack_amps.1), channel_id=2, replica_groups=mesh['reorder'=4,'pair'=8] {'reorder'}, dimensions={0}, use_global_device_ids=true | all-gather | bytes 983040 | tf_op jit(solution)/shard_map/all_gather | solution.py:393
  24.6 0.1 dynamic-slice_bitcast_fusion
  24.6 1.6 %collective-permute-start = (bf16[24,32,128]{2,1,0:T(8,128)(2,1)S(1)}, bf16[24,32,128]{2,1,0:T(8,128)(2,1)S(1)}, u32[]{:S(2)}, u32[]{:S(2)}) collective-permute-start(bf16[24,32,128]{2,1,0:T(8,128)(2,1)S(1)} %get-tuple-element.44), channel_id=1, source_target_pairs={{0,2},{1,3},{2,0},{3,1},{4,6},{5,7},{6,4},{7,5},{8,10},{9,11},{10,... | collective-permute-start | bytes 589832 | tf_op jit(solution)/shard_map/ppermute | solution.py:382
  26.3 1.5 %collective-permute-start.1 = (bf16[24,32,128]{2,1,0:T(8,128)(2,1)S(1)}, bf16[24,32,128]{2,1,0:T(8,128)(2,1)S(1)}, u32[]{:S(2)}, u32[]{:S(2)}) collective-permute-start(bf16[24,32,128]{2,1,0:T(8,128)(2,1)S(1)} %get-tuple-element.43), channel_id=1, source_target_pairs={{0,4},{1,5},{2,6},{3,7},{4,0},{5,1},{6,2},{7,3},{8,12},{9,13},{10,... | collective-permute-start | bytes 589832 | tf_op jit(solution)/shard_map/ppermute | solution.py:382
  27.7 0.5 collective-permute-start.2
  28.2 9.0 %prep_integrals.1 = (s32[1568]{0:T(1024)S(1)}, bf16[96,64,128]{2,1,0:T(8,128)(2,1)}, bf16[96,64,128]{2,1,0:T(8,128)(2,1)}) custom-call(s32[8,8,16]{2,1,0:T(8,128)S(1)} %copy-done.4, bf16[625,64,128]{2,1,0:T(8,128)(2,1)} %bitcast.19), custom_call_target="tpu_custom_call" | custom-call | flops 1000000000 | bytes 40000000 | tf_op jit(solution)/shard_map/prep_integrals/pallas_call | solution.py:171
  37.3 0.1 collective-permute-start.3
  37.4 1.4 %copy-done.2 = bf16[96,64,128]{2,1,0:T(8,128)(2,1)S(1)} copy-done((bf16[96,64,128]{2,1,0:T(8,128)(2,1)S(1)}, bf16[96,64,128]{2,1,0:T(8,128)(2,1)}, u32[]{:S(2)}) %copy-start.2) | copy-done | bytes 1572888
  38.8 2.7 %multiply_own.1.refs_4_ = f32[97,32,128]{2,1,0:T(8,128)S(1)} custom-call(s32[1568]{0:T(1024)S(1)} %get-tuple-element.24.meta_ref, bf16[96,64,128]{2,1,0:T(8,128)(2,1)S(1)} %copy-done.2, bf16[24,32,128]{2,1,0:T(8,128)(2,1)S(1)} %get-tuple-element.27.refs_0_, bf16[24,32,128]{2,1,0:T(8,128)(2,1)S(1)} %collective-permute-done.refs_1_, ...), custom_call_target="tpu_custom_call" | custom-call | flops 1000000000 | bytes 10000000 | tf_op jit(solution)/shard_map/multiply_own/pallas_call | solution.py:286
  41.5 0.0 copy-start.1
  41.6 2.2 %multiply_sibling.1 = (bf16[24,32,128]{2,1,0:T(8,128)(2,1)S(1)}, bf16[24,32,128]{2,1,0:T(8,128)(2,1)S(1)}, bf16[24,32,128]{2,1,0:T(8,128)(2,1)S(1)}, bf16[24,32,128]{2,1,0:T(8,128)(2,1)S(1)}) custom-call(s32[1568]{0:T(1024)S(1)} %get-tuple-element.24.meta_ref, bf16[96,64,128]{2,1,0:T(8,128)(2,1)S(1)} %collective-permute-done.3.tiles_ref, ...), custom_call_target="tpu_custom_call" | custom-call | flops 1000000000 | bytes 10000000 | tf_op jit(solution)/shard_map/multiply_sibling/pallas_call | solution.py:286
  43.7 0.1 collective-permute-start.4
  43.8 0.7 collective-permute-start.5
  44.5 2.8 %collective-permute-start.6 = (bf16[24,32,128]{2,1,0:T(8,128)(2,1)S(1)}, bf16[24,32,128]{2,1,0:T(8,128)(2,1)S(1)}, u32[]{:S(2)}, u32[]{:S(2)}) collective-permute-start(bf16[24,32,128]{2,1,0:T(8,128)(2,1)S(1)} %get-tuple-element.39), channel_id=1, source_target_pairs={{0,6},{1,7},{2,4},{3,5},{4,2},{5,3},{6,0},{7,1},{8,14},{9,15},{10,... | collective-permute-start | bytes 589832 | tf_op jit(solution)/shard_map/ppermute | solution.py:382
  47.3 0.7 reshape.15.vir_ref
  47.9 2.6 %denominators.1.inv_ref = f32[2,16,4096]{2,1,0:T(8,128)} custom-call(s32[8,8,16]{2,1,0:T(8,128)} %ti_ref.5, s32[8]{0:T(128)} %slab_ref, f32[200]{0:T(256)} %occ_ref, f32[25,64]{1,0:T(8,128)} %reshape.15.vir_ref), custom_call_target="tpu_custom_call" | custom-call | flops 10000000 | bytes 1000000 | tf_op jit(solution)/shard_map/denominators/pallas_call | solution.py:217
  50.6 0.9 %collective-permute-done.4.refs_1_ = bf16[24,32,128]{2,1,0:T(8,128)(2,1)S(1)} collective-permute-done((bf16[24,32,128]{2,1,0:T(8,128)(2,1)S(1)}, bf16[24,32,128]{2,1,0:T(8,128)(2,1)S(1)}, u32[]{:S(2)}, u32[]{:S(2)}) %collective-permute-start.4) | collective-permute-done | bytes 196640 | tf_op jit(solution)/shard_map/ppermute | solution.py:382
  51.5 3.9 %collective-permute-done.5.refs_2_ = bf16[24,32,128]{2,1,0:T(8,128)(2,1)S(1)} collective-permute-done((bf16[24,32,128]{2,1,0:T(8,128)(2,1)S(1)}, bf16[24,32,128]{2,1,0:T(8,128)(2,1)S(1)}, u32[]{:S(2)}, u32[]{:S(2)}) %collective-permute-start.5) | collective-permute-done | bytes 196640 | tf_op jit(solution)/shard_map/ppermute | solution.py:382
  55.4 1.0 %copy-done = f32[2,16,4096]{2,1,0:T(8,128)S(1)} copy-done((f32[2,16,4096]{2,1,0:T(8,128)S(1)}, f32[2,16,4096]{2,1,0:T(8,128)}, u32[]{:S(2)}) %copy-start) | copy-done | bytes 524312
  56.5 2.8 %update_amps.1 = (bf16[1,2,16,4096]{3,2,1,0:T(8,128)(2,1)}, f32[8,8,128]{2,1,0:T(8,128)S(1)}) custom-call(s32[8,8,16]{2,1,0:T(8,128)S(1)} %copy-done.5, bf16[1,2,16,4096]{3,2,1,0:T(8,128)(2,1)S(1)} %copy-done.3, bf16[1,2,16,4096]{3,2,1,0:T(8,128)(2,1)S(1)} %copy-done.6, bf16[6,1,2,16,4096]{4,3,2,1,0:T(8,128)(2,1)S(1)} %copy-done.1, ...), custom_call_target="tpu_custom_call" | custom-call | flops 100000000 | bytes 6000000 | tf_op jit(solution)/shard_map/update_amps/pallas_call | solution.py:347
  59.3 7.6 %all_to_all.5 = f32[8,8,128]{2,1,0:T(8,128)S(1)} all-to-all(f32[8,8,128]{2,1,0:T(8,128)S(1)} %get-tuple-element.41), channel_id=1, replica_groups=mesh['reorder'=4,'pair'=8] {'pair'}, dimensions={0} | all-to-all | bytes 65536 | tf_op jit(solution)/shard_map/all_to_all | solution.py:411
  66.9 13.7 %all-gather.1 = f32[32,128]{1,0:T(8,128)} all-gather(f32[8,128]{1,0:T(8,128)S(1)} %reduce_sum.9), channel_id=3, replica_groups=mesh['reorder'=4,'pair'=8] {'reorder'}, dimensions={0}, use_global_device_ids=true | all-gather | bytes 20480 | tf_op jit(solution)/shard_map/all_gather | solution.py:412
  80.5 1.4 %finish_gram.1 = f32[7]{0:T(128)} custom-call(f32[4,8,128]{2,1,0:T(8,128)} %bitcast.21), custom_call_target="tpu_custom_call" | custom-call | tf_op jit(solution)/shard_map/finish_gram/pallas_call | solution.py:372
  (19 shorter events, 0.1 us)
Async XLA Ops:
  0.6 27.6 %copy-start.4 = (s32[8,8,16]{2,1,0:T(8,128)S(1)}, s32[8,8,16]{2,1,0:T(8,128)}, u32[]{:S(2)}) copy-start(s32[8,8,16]{2,1,0:T(8,128)} %ti_ref.5) | copy-start | bytes 12292
  24.6 12.6 %collective-permute-start = (bf16[24,32,128]{2,1,0:T(8,128)(2,1)S(1)}, bf16[24,32,128]{2,1,0:T(8,128)(2,1)S(1)}, u32[]{:S(2)}, u32[]{:S(2)}) collective-permute-start(bf16[24,32,128]{2,1,0:T(8,128)(2,1)S(1)} %get-tuple-element.44), channel_id=1, source_target_pairs={{0,2},{1,3},{2,0},{3,1},{4,6},{5,7},{6,4},{7,5},{8,10},{9,11},{10,... | collective-permute-start | bytes 589832 | tf_op jit(solution)/shard_map/ppermute | solution.py:382
  26.3 11.0 %collective-permute-start.1 = (bf16[24,32,128]{2,1,0:T(8,128)(2,1)S(1)}, bf16[24,32,128]{2,1,0:T(8,128)(2,1)S(1)}, u32[]{:S(2)}, u32[]{:S(2)}) collective-permute-start(bf16[24,32,128]{2,1,0:T(8,128)(2,1)S(1)} %get-tuple-element.43), channel_id=1, source_target_pairs={{0,4},{1,5},{2,6},{3,7},{4,0},{5,1},{6,2},{7,3},{8,12},{9,13},{10,... | collective-permute-start | bytes 589832 | tf_op jit(solution)/shard_map/ppermute | solution.py:382
  27.7 9.5 %collective-permute-start.2 = (bf16[24,32,128]{2,1,0:T(8,128)(2,1)S(1)}, bf16[24,32,128]{2,1,0:T(8,128)(2,1)S(1)}, u32[]{:S(2)}, u32[]{:S(2)}) collective-permute-start(bf16[24,32,128]{2,1,0:T(8,128)(2,1)S(1)} %get-tuple-element.42), channel_id=1, source_target_pairs={{0,6},{1,7},{2,4},{3,5},{4,2},{5,3},{6,0},{7,1},{8,14},{9,15},{10,... | collective-permute-start | bytes 589832 | tf_op jit(solution)/shard_map/ppermute | solution.py:382
  37.3 4.3 %collective-permute-start.3 = (bf16[96,64,128]{2,1,0:T(8,128)(2,1)}, bf16[96,64,128]{2,1,0:T(8,128)(2,1)S(1)}, u32[]{:S(2)}, u32[]{:S(2)}) collective-permute-start(bf16[96,64,128]{2,1,0:T(8,128)(2,1)} %get-tuple-element.26), channel_id=1, source_target_pairs={{0,1},{1,0},{2,3},{3,2},{4,5},{5,4},{6,7},{7,6},{8,9},{9,8},{10,11... | collective-permute-start | bytes 4718600 | tf_op jit(solution)/shard_map/ppermute | solution.py:382
  37.3 1.4 %copy-start.2 = (bf16[96,64,128]{2,1,0:T(8,128)(2,1)S(1)}, bf16[96,64,128]{2,1,0:T(8,128)(2,1)}, u32[]{:S(2)}) copy-start(bf16[96,64,128]{2,1,0:T(8,128)(2,1)} %get-tuple-element.31.tiles_ref) | copy-start | bytes 4718596
  41.5 5.8 %copy-start.7 = (f32[1600]{0:T(1024)S(1)}, f32[1600]{0:T(1024)}, u32[]{:S(2)}) copy-start(f32[1600]{0:T(1024)} %param.15) | copy-start | bytes 19204
  41.5 13.9 %copy-start.1 = (bf16[6,1,2,16,4096]{4,3,2,1,0:T(8,128)(2,1)S(1)}, bf16[6,1,2,16,4096]{4,3,2,1,0:T(8,128)(2,1)}, u32[]{:S(2)}) copy-start(bf16[6,1,2,16,4096]{4,3,2,1,0:T(8,128)(2,1)} %hist_ref.1) | copy-start | bytes 4718596
  41.5 13.9 %copy-start.3 = (bf16[1,2,16,4096]{3,2,1,0:T(8,128)(2,1)S(1)}, bf16[1,2,16,4096]{3,2,1,0:T(8,128)(2,1)}, u32[]{:S(2)}) copy-start(bf16[1,2,16,4096]{3,2,1,0:T(8,128)(2,1)} %amps_ref.3) | copy-start | bytes 786436
  41.5 13.9 %copy-start.5 = (s32[8,8,16]{2,1,0:T(8,128)S(1)}, s32[8,8,16]{2,1,0:T(8,128)}, u32[]{:S(2)}) copy-start(s32[8,8,16]{2,1,0:T(8,128)} %ti_ref.5) | copy-start | bytes 12292
  41.5 13.9 %copy-start.6 = (bf16[1,2,16,4096]{3,2,1,0:T(8,128)(2,1)S(1)}, bf16[1,2,16,4096]{3,2,1,0:T(8,128)(2,1)}, u32[]{:S(2)}) copy-start(bf16[1,2,16,4096]{3,2,1,0:T(8,128)(2,1)} %ovov_ref.1) | copy-start | bytes 786436
  43.7 7.8 %collective-permute-start.4 = (bf16[24,32,128]{2,1,0:T(8,128)(2,1)S(1)}, bf16[24,32,128]{2,1,0:T(8,128)(2,1)S(1)}, u32[]{:S(2)}, u32[]{:S(2)}) collective-permute-start(bf16[24,32,128]{2,1,0:T(8,128)(2,1)S(1)} %get-tuple-element.37), channel_id=1, source_target_pairs={{0,2},{1,3},{2,0},{3,1},{4,6},{5,7},{6,4},{7,5},{8,10},{9,11},{10,... | collective-permute-start | bytes 589832 | tf_op jit(solution)/shard_map/ppermute | solution.py:382
  43.8 11.6 %collective-permute-start.5 = (bf16[24,32,128]{2,1,0:T(8,128)(2,1)S(1)}, bf16[24,32,128]{2,1,0:T(8,128)(2,1)S(1)}, u32[]{:S(2)}, u32[]{:S(2)}) collective-permute-start(bf16[24,32,128]{2,1,0:T(8,128)(2,1)S(1)} %get-tuple-element.38), channel_id=1, source_target_pairs={{0,4},{1,5},{2,6},{3,7},{4,0},{5,1},{6,2},{7,3},{8,12},{9,13},{10,... | collective-permute-start | bytes 589832 | tf_op jit(solution)/shard_map/ppermute | solution.py:382
  44.5 10.9 %collective-permute-start.6 = (bf16[24,32,128]{2,1,0:T(8,128)(2,1)S(1)}, bf16[24,32,128]{2,1,0:T(8,128)(2,1)S(1)}, u32[]{:S(2)}, u32[]{:S(2)}) collective-permute-start(bf16[24,32,128]{2,1,0:T(8,128)(2,1)S(1)} %get-tuple-element.39), channel_id=1, source_target_pairs={{0,6},{1,7},{2,4},{3,5},{4,2},{5,3},{6,0},{7,1},{8,14},{9,15},{10,... | collective-permute-start | bytes 589832 | tf_op jit(solution)/shard_map/ppermute | solution.py:382
  55.4 1.0 %copy-start = (f32[2,16,4096]{2,1,0:T(8,128)S(1)}, f32[2,16,4096]{2,1,0:T(8,128)}, u32[]{:S(2)}) copy-start(f32[2,16,4096]{2,1,0:T(8,128)} %denominators.1.inv_ref) | copy-start | bytes 1572868

commit v3 on v2

--- a/solution.py
+++ b/solution.py
@@ -92,8 +92,8 @@
         parity = lax.rem(k, 2)
 
         def one_first(q, cnt):
-            i = who ^ (q * 2)
-            out = q * LIVE2
+            i = (plane ^ q) * 2 + (who & 1)
+            out = (lax.shift_right_logical(who, 1) ^ plane ^ q) * LIVE2
             for a in range(across + 1):
                 tab_ref[a] = -1
             live_in = jnp.int32(0)
@@ -278,20 +278,17 @@
 
 def multiply(which, meta, tiles, amps, sums, nq):
     block = jax.ShapeDtypeStruct((LIVE2, ROWS, LANES), BF16)
-    scratch = [pltpu.VMEM((nq * LIVE2, ROWS, LANES), BF16)]
-    if which == 0:
-        out = jax.ShapeDtypeStruct((nq * LIVE2 + 1, ROWS, LANES), F32)
-    else:
-        out = [block] * nq
+    total = jax.ShapeDtypeStruct((nq * LIVE2 + 1, ROWS, LANES), F32)
+    out = [block] * nq if which == 1 else total
     return pl.pallas_call(
         functools.partial(multiply_kernel, which, nq, nq * LIVE2 + 8, 8),
-        in_specs=[SMEM] + [VMEM] * (1 + nq + len(sums)),
+        in_specs=[SMEM] + [VMEM] * (1 + len(amps) + len(sums)),
         out_specs=jax.tree.map(lambda _: VMEM, out),
         out_shape=out,
-        scratch_shapes=scratch,
+        scratch_shapes=[pltpu.VMEM((nq * LIVE2, ROWS, LANES), BF16)],
         compiler_params=pltpu.CompilerParams(vmem_limit_bytes=24 * 1024 * 1024),
-        cost_estimate=pl.CostEstimate(flops=10**9, bytes_accessed=10**7, transcendentals=0),
-        name="multiply_own" if which == 0 else "multiply_sibling",
+        cost_estimate=pl.CostEstimate(flops=10**9, bytes_accessed=6 * 10**6, transcendentals=0),
+        name=("multiply_own", "multiply_sibling")[which],
     )(meta, tiles, *amps, *sums)
 
 
@@ -311,38 +308,40 @@
         return carry
 
     lax.fori_loop(0, LIVE2, add, 0, unroll=4)
-    slot = lax.broadcasted_iota(jnp.int32, (8, LANES), 0)
-    accs = [jnp.zeros((8, LANES), F32) for _ in range(nhist + 1)]
+    slot = lax.broadcasted_iota(jnp.int32, (capt, LANES), 0)
+    accs = [jnp.zeros((capt, LANES), F32) for _ in range(nhist + 1)]
     for jj in range(2):
         count = count_live(ti_ref, first, second + jj, capt, across * across)
         start = 0 if jj == 0 else (LIVE2 - count) * ROWS
-        for g in range(capt // 8):
-            alive = slot + g * 8 < count
-            rows = slice(g * 8, (g + 1) * 8)
-
-            def chunk(p, accs):
-                here = pl.ds(pl.multiple_of(p * LANES, LANES), LANES)
-                cycle = sum_ref[pl.ds(start + g * 8 * ROWS + p, 8, stride=ROWS), :]
-                resid = jnp.where(alive, ovov_ref[0, jj, rows, here].astype(F32) + cycle, 0.0)
-                moved = amps_ref[0, jj, rows, here].astype(F32) + resid * inv_ref[jj, rows, here]
-                new_ref[0, jj, rows, here] = jnp.where(alive, moved, 0.0).astype(BF16)
-                out = [
-                    accs[m] + hist_ref[m, 0, jj, rows, here].astype(F32) * resid
-                    for m in range(nhist)
-                ]
-                out.append(accs[nhist] + resid * resid)
-                return out
-
-            accs = lax.fori_loop(0, ROWS, chunk, accs, unroll=8)
+        alive = slot < count
+
+        def chunk(p, accs):
+            here = pl.ds(pl.multiple_of(p * LANES, LANES), LANES)
+            cycle = jnp.concatenate(
+                [
+                    sum_ref[pl.ds(start + g * ROWS + p, 8, stride=ROWS), :]
+                    for g in range(0, capt, 8)
+                ],
+                axis=0,
+            )
+            resid = jnp.where(alive, ovov_ref[0, jj, :, here].astype(F32) + cycle, 0.0)
+            moved = amps_ref[0, jj, :, here].astype(F32) + resid * inv_ref[jj, :, here]
+            new_ref[0, jj, :, here] = jnp.where(alive, moved, 0.0).astype(BF16)
+            out = [
+                accs[m] + hist_ref[m, 0, jj, :, here].astype(F32) * resid for m in range(nhist)
+            ]
+            out.append(accs[nhist] + resid * resid)
+            return out
+
+        accs = lax.fori_loop(0, ROWS, chunk, accs, unroll=4)
     for m in range(8):
         row = jnp.zeros((1, LANES), F32)
         if m <= nhist:
             row = jnp.sum(accs[m], axis=0, keepdims=True)
-        for n in range(gram_ref.shape[0]):
-            gram_ref[n, m : m + 1] = row
-
-
-def update(ti, amps, ovov, history, inv, parts, copies, capt, across):
+        gram_ref[m : m + 1] = row
+
+
+def update(ti, amps, ovov, history, inv, parts, capt, across):
     nq = len(parts)
     return pl.pallas_call(
         functools.partial(update_kernel, capt, across, nq),
@@ -350,7 +349,7 @@
         out_specs=[VMEM, VMEM],
         out_shape=[
             jax.ShapeDtypeStruct(amps.shape, BF16),
-            jax.ShapeDtypeStruct((copies, 8, LANES), F32),
+            jax.ShapeDtypeStruct((8, LANES), F32),
         ],
         scratch_shapes=[pltpu.VMEM(((LIVE2 + capt) * ROWS, LANES), F32)],
         compiler_params=pltpu.CompilerParams(vmem_limit_bytes=24 * 1024 * 1024),
@@ -360,7 +359,7 @@
 
 
 def finish_kernel(nhist, scale, *refs):
-    total = jnp.sum(refs[0][...], axis=0)
+    total = refs[0][...] + refs[1][...]
     total = jnp.sum(total, axis=1, keepdims=True)
     row = lax.broadcasted_iota(jnp.int32, total.shape, 0)
     total = jnp.where(row == nhist, jnp.sqrt(jnp.maximum(total, 0.0)), total) * scale
@@ -371,15 +370,23 @@
 def finish(sums, nhist, scale):
     return pl.pallas_call(
         functools.partial(finish_kernel, nhist, scale),
-        in_specs=[VMEM],
+        in_specs=[VMEM] * len(sums),
         out_specs=SMEM,
         out_shape=jax.ShapeDtypeStruct((nhist + 1,), F32),
         name="finish_gram",
-    )(sums)
+    )(*sums)
 
 
 def swap(x, axis, size, step):
     return lax.ppermute(x, axis, [(n, n ^ step) for n in range(size)])
+
+
+def spread_perm(npair, nq, m):
+    return [
+        (z * npair + p, ((p // 2) ^ m) * npair + 2 * z + p % 2)
+        for z in range(nq)
+        for p in range(npair)
+    ]
 
 
 def local(npair, nq, amps, tile_index, ovov, cycle_ints, history, slab, eps_occ, eps_vir):
@@ -390,26 +397,26 @@
     assert occ_dev == 1 and jdev == 2 and tile_area == TILE * TILE and capt == 16
     assert ns == npair == 2 * nq
     packed = pack(amps, tile_index, capt, across)
-    blocks = lax.all_gather(packed, "reorder")
-    late = lax.optimization_barrier((blocks, cycle_ints, tile_index))
-    meta, mine, send = prep(*late[1:], capt, across, nq)
-    chip = lax.axis_index("pair") // 2
-    turned = [
-        lax.dynamic_index_in_dim(blocks, chip ^ e, 0, keepdims=False) for e in range(nq)
-    ]
-    turned = [turned[0]] + [swap(turned[e], "pair", npair, 2 * e) for e in range(1, nq)]
-    turned, send = lax.optimization_barrier((turned, send))
+    axes = ("reorder", "pair")
+    turned = [lax.ppermute(packed, axes, spread_perm(npair, nq, m)) for m in range(nq)]
+    late = lax.optimization_barrier((packed, cycle_ints, tile_index, slab, eps_occ, eps_vir))
+    meta, mine, send = prep(*late[1:3], capt, across, nq)
+    inv = denominators(*late[2:], capt, across)
+    turned, send, inv = lax.optimization_barrier((turned, send, inv))
     theirs = swap(send, "pair", npair, 1)
     sums = multiply(0, meta, mine, turned, [], nq)
     partial = multiply(1, meta, theirs, turned, [sums], nq)
     parts = [partial[0]] + [swap(partial[e], "pair", npair, 2 * e) for e in range(1, nq)]
-    late = lax.optimization_barrier((partial[0], tile_index, slab, eps_occ, eps_vir))
-    inv = denominators(*late[1:], capt, across)
-    new_amps, gram = update(
-        tile_index, amps, ovov, history, inv, parts, npair, capt, across
-    )
-    gram = lax.all_to_all(gram, "pair", split_axis=0, concat_axis=0, tiled=True)
-    sums = lax.all_gather(jnp.sum(gram, axis=0), "reorder")
+    new_amps, gram = update(tile_index, amps, ovov, history, inv, parts, capt, across)
+    step = 1
+    while step < npair:
+        gram = gram + swap(gram, "pair", npair, step)
+        step *= 2
+    step = 1
+    while 2 * step < nq:
+        gram = gram + swap(gram, "reorder", nq, step)
+        step *= 2
+    sums = [gram, swap(gram, "reorder", nq, step)]
     return (new_amps, finish(sums, nhist, 1.0 / (TILE * ns)))
 
 

time: 82.1 us -> 71.3 us (0.87)
  blocking collectives: 42.7 us -> 0 us
  waiting for transfers between devices: 4.84 us -> 20.5 us
  starting transfers between devices: 7.17 us -> 21.2 us
  local copies, waits for them, and re-layouts: 3.2 us -> 4.14 us
  Pallas kernels: 23.1 us -> 24 us
    all_gather x2 -> x0, blocking collectives: 35.1 us -> none  [the longest x1 21.5 us: local(): blocks = lax.all_gather(packed, 'reorder')]
    ppermute x7 -> x9, waiting for transfers between devices: 4.84 us -> 20.5 us  [swap(): return lax.ppermute(x, axis, [(n, n ^ step) for n in range(size)])]
    ppermute x0 -> x4, starting transfers between devices: none -> 11.7 us  [local(): lax.ppermute(packed, axes, spread_perm(npair, nq, m))]
    all_to_all x1 -> x0, blocking collectives: 7.57 us -> none  [local(): gram = lax.all_to_all(gram, 'pair', split_axis=0, concat_axis=0, tiled=True)]
    ppermute x7 -> x9, starting transfers between devices: 7.17 us -> 9.54 us  [swap(): return lax.ppermute(x, axis, [(n, n ^ step) for n in range(size)])]
    pallas_call x2, Pallas kernels: 4.87 us -> 5.7 us  [multiply(): pl.pallas_call(functools.partial(multiply_kernel, which, nq, nq * LIVE2 +...]
  transfers between devices with their start and end apart: 7 -> 13, of which waited for: 2 -> 8; matrix products, arithmetic and copies ran while one was open for 1% -> 2% of each run, Pallas kernels for 18% -> 20%
where the time goes in v3:
time: 71.3 us; the launch traced here: 70.7 us
  Pallas kernels  24 us (34%)
  starting transfers between devices  21.2 us (30%)
  waiting for transfers between devices  20.5 us (29%)
  local copies, waits for them, and re-layouts  4.14 us (6%)
  between operations  0.78 us (1%)
    ppermute x9, waiting for transfers between devices, swap(): return lax.ppermute(x, axis, [(n, n ^ step) for n in range(size)])  20.5 us
    ppermute x4, starting transfers between devices, local(): lax.ppermute(packed, axes, spread_perm(npair, nq, m))  11.7 us
    ppermute x9, starting transfers between devices, swap(): return lax.ppermute(x, axis, [(n, n ^ step) for n in range(size)])  9.54 us
    pallas_call x1, Pallas kernels, prep(): pl.pallas_call(functools.partial(prep_kernel, capt, across, nq, nmax), in...  8.85 us
    pallas_call x2, Pallas kernels, multiply(): pl.pallas_call(functools.partial(multiply_kernel, which, nq, nq * LIVE2 +...  5.7 us
    pallas_call x1, Pallas kernels, update(): pl.pallas_call(functools.partial(update_kernel, capt, across, nq), in_spe...  3.06 us
    unnamed x16, local copies, waits for them, and re-layouts  2.77 us
    pallas_call x1, Pallas kernels, denominators(): pl.pallas_call(functools.partial(denom_kernel, capt, across), in_specs=[S...  2.59 us
  transfers between devices with their start and end apart: 13, of which 8 were waited for; matrix products, arithmetic and copies ran while one was open for 2% of the time, Pallas kernels for 20%

profile of v3, /device:TPU:0, one launch (start us, length us, event | category | flops | bytes accessed | tf_op | source)
XLA Modules:
  0.0 70.7 jit_solution(10920007440544162056)
XLA Ops:
  0.6 2.5 %pack_amps.1 = bf16[24,32,128]{2,1,0:T(8,128)(2,1)} custom-call(s32[8,8,16]{2,1,0:T(8,128)} %ti_ref.5, bf16[1,2,16,4096]{3,2,1,0:T(8,128)(2,1)} %amps_ref.3), custom_call_target="tpu_custom_call" | custom-call | flops 100000000 | bytes 500000 | tf_op jit(solution)/shard_map/pack_amps/pallas_call | solution.py:62
  3.1 1.6 %collective-permute-start = (bf16[24,32,128]{2,1,0:T(8,128)(2,1)}, bf16[24,32,128]{2,1,0:T(8,128)(2,1)S(1)}, u32[]{:S(2)}, u32[]{:S(2)}) collective-permute-start(bf16[24,32,128]{2,1,0:T(8,128)(2,1)} %pack_amps.1), channel_id=1, source_target_pairs={{0,0},{1,1},{2,8},{3,9},{4,16},{5,17},{6,24},{7,25},{8,2},{9,3},{1... | collective-permute-start | bytes 589832 | tf_op jit(solution)/shard_map/ppermute | solution.py:401
  4.7 4.7 %collective-permute-start.1 = (bf16[24,32,128]{2,1,0:T(8,128)(2,1)}, bf16[24,32,128]{2,1,0:T(8,128)(2,1)S(1)}, u32[]{:S(2)}, u32[]{:S(2)}) collective-permute-start(bf16[24,32,128]{2,1,0:T(8,128)(2,1)} %pack_amps.1), channel_id=1, source_target_pairs={{0,8},{1,9},{2,0},{3,1},{4,24},{5,25},{6,16},{7,17},{8,10},{9,11},... | collective-permute-start | bytes 589832 | tf_op jit(solution)/shard_map/ppermute | solution.py:401
  9.4 3.5 %collective-permute-start.2 = (bf16[24,32,128]{2,1,0:T(8,128)(2,1)}, bf16[24,32,128]{2,1,0:T(8,128)(2,1)S(1)}, u32[]{:S(2)}, u32[]{:S(2)}) collective-permute-start(bf16[24,32,128]{2,1,0:T(8,128)(2,1)} %pack_amps.1), channel_id=1, source_target_pairs={{0,16},{1,17},{2,24},{3,25},{4,0},{5,1},{6,8},{7,9},{8,18},{9,19},... | collective-permute-start | bytes 589832 | tf_op jit(solution)/shard_map/ppermute | solution.py:401
  12.9 1.9 %collective-permute-start.3 = (bf16[24,32,128]{2,1,0:T(8,128)(2,1)}, bf16[24,32,128]{2,1,0:T(8,128)(2,1)S(1)}, u32[]{:S(2)}, u32[]{:S(2)}) collective-permute-start(bf16[24,32,128]{2,1,0:T(8,128)(2,1)} %pack_amps.1), channel_id=1, source_target_pairs={{0,24},{1,25},{2,16},{3,17},{4,8},{5,9},{6,0},{7,1},{8,26},{9,27},... | collective-permute-start | bytes 589832 | tf_op jit(solution)/shard_map/ppermute | solution.py:401
  14.8 1.4 %reshape.15.vir_ref = f32[25,64]{1,0:T(8,128)} reshape(f32[1600]{0:T(1024)} %param.15) | data formatting | bytes 12800 | tf_op jit(solution)/shard_map/reshape | solution.py:225
  16.2 2.6 %denominators.1.inv_ref = f32[2,16,4096]{2,1,0:T(8,128)} custom-call(s32[8,8,16]{2,1,0:T(8,128)} %ti_ref.5, s32[8]{0:T(128)} %slab_ref, f32[200]{0:T(256)} %occ_ref, f32[25,64]{1,0:T(8,128)} %reshape.15.vir_ref), custom_call_target="tpu_custom_call" | custom-call | flops 10000000 | bytes 1000000 | tf_op jit(solution)/shard_map/denominators/pallas_call | solution.py:217
  19.5 8.9 %prep_integrals.1 = (s32[1568]{0:T(1024)S(1)}, bf16[96,64,128]{2,1,0:T(8,128)(2,1)}, bf16[96,64,128]{2,1,0:T(8,128)(2,1)}) custom-call(s32[8,8,16]{2,1,0:T(8,128)S(1)} %copy-done.4, bf16[625,64,128]{2,1,0:T(8,128)(2,1)} %bitcast.9), custom_call_target="tpu_custom_call" | custom-call | flops 1000000000 | bytes 40000000 | tf_op jit(solution)/shard_map/prep_integrals/pallas_call | solution.py:171
  28.5 1.4 %copy-done.2 = bf16[96,64,128]{2,1,0:T(8,128)(2,1)S(1)} copy-done((bf16[96,64,128]{2,1,0:T(8,128)(2,1)S(1)}, bf16[96,64,128]{2,1,0:T(8,128)(2,1)}, u32[]{:S(2)}) %copy-start.2) | copy-done | bytes 1572888
  29.9 3.0 %multiply_own.1.refs_4_ = f32[97,32,128]{2,1,0:T(8,128)S(1)} custom-call(s32[1568]{0:T(1024)S(1)} %get-tuple-element.29.meta_ref, bf16[96,64,128]{2,1,0:T(8,128)(2,1)S(1)} %copy-done.2, bf16[24,32,128]{2,1,0:T(8,128)(2,1)S(1)} %collective-permute-done.refs_0_, bf16[24,32,128]{2,1,0:T(8,128)(2,1)S(1)} %collective-permute-done.1.refs_1_, ...), custom_call_target="tpu_custom_call" | custom-call | flops 1000000000 | bytes 6000000 | tf_op jit(solution)/shard_map/multiply_own/pallas_call | solution.py:283
  33.0 2.7 %multiply_sibling.1 = (bf16[24,32,128]{2,1,0:T(8,128)(2,1)S(1)}, bf16[24,32,128]{2,1,0:T(8,128)(2,1)S(1)}, bf16[24,32,128]{2,1,0:T(8,128)(2,1)S(1)}, bf16[24,32,128]{2,1,0:T(8,128)(2,1)S(1)}) custom-call(s32[1568]{0:T(1024)S(1)} %get-tuple-element.29.meta_ref, bf16[96,64,128]{2,1,0:T(8,128)(2,1)S(1)} %collective-permute-done.4.tiles_ref, ...), custom_call_target="tpu_custom_call" | custom-call | flops 1000000000 | bytes 6000000 | tf_op jit(solution)/shard_map/multiply_sibling/pallas_call | solution.py:283
  35.8 3.2 %collective-permute-start.6 = (bf16[24,32,128]{2,1,0:T(8,128)(2,1)S(1)}, bf16[24,32,128]{2,1,0:T(8,128)(2,1)S(1)}, u32[]{:S(2)}, u32[]{:S(2)}) collective-permute-start(bf16[24,32,128]{2,1,0:T(8,128)(2,1)S(1)} %get-tuple-element.38), channel_id=1, source_target_pairs={{0,4},{1,5},{2,6},{3,7},{4,0},{5,1},{6,2},{7,3},{8,12},{9,13},{10,... | collective-permute-start | bytes 589832 | tf_op jit(solution)/shard_map/ppermute | solution.py:381
  38.9 1.4 %collective-permute-start.7 = (bf16[24,32,128]{2,1,0:T(8,128)(2,1)S(1)}, bf16[24,32,128]{2,1,0:T(8,128)(2,1)S(1)}, u32[]{:S(2)}, u32[]{:S(2)}) collective-permute-start(bf16[24,32,128]{2,1,0:T(8,128)(2,1)S(1)} %get-tuple-element.39), channel_id=1, source_target_pairs={{0,6},{1,7},{2,4},{3,5},{4,2},{5,3},{6,0},{7,1},{8,14},{9,15},{10,... | collective-permute-start | bytes 589832 | tf_op jit(solution)/shard_map/ppermute | solution.py:381
  40.3 1.4 %collective-permute-done.5.refs_1_ = bf16[24,32,128]{2,1,0:T(8,128)(2,1)S(1)} collective-permute-done((bf16[24,32,128]{2,1,0:T(8,128)(2,1)S(1)}, bf16[24,32,128]{2,1,0:T(8,128)(2,1)S(1)}, u32[]{:S(2)}, u32[]{:S(2)}) %collective-permute-start.5) | collective-permute-done | bytes 196640 | tf_op jit(solution)/shard_map/ppermute | solution.py:381
  41.7 5.6 %collective-permute-done.6.refs_2_ = bf16[24,32,128]{2,1,0:T(8,128)(2,1)S(1)} collective-permute-done((bf16[24,32,128]{2,1,0:T(8,128)(2,1)S(1)}, bf16[24,32,128]{2,1,0:T(8,128)(2,1)S(1)}, u32[]{:S(2)}, u32[]{:S(2)}) %collective-permute-start.6) | collective-permute-done | bytes 196640 | tf_op jit(solution)/shard_map/ppermute | solution.py:381
  47.3 1.8 %collective-permute-done.7.refs_3_ = bf16[24,32,128]{2,1,0:T(8,128)(2,1)S(1)} collective-permute-done((bf16[24,32,128]{2,1,0:T(8,128)(2,1)S(1)}, bf16[24,32,128]{2,1,0:T(8,128)(2,1)S(1)}, u32[]{:S(2)}, u32[]{:S(2)}) %collective-permute-start.7) | collective-permute-done | bytes 196640 | tf_op jit(solution)/shard_map/ppermute | solution.py:381
  49.2 3.1 %update_amps.1 = (bf16[1,2,16,4096]{3,2,1,0:T(8,128)(2,1)}, f32[8,128]{1,0:T(8,128)S(1)}) custom-call(s32[8,8,16]{2,1,0:T(8,128)S(1)} %copy-done.4, bf16[1,2,16,4096]{3,2,1,0:T(8,128)(2,1)S(1)} %copy-done.3, bf16[1,2,16,4096]{3,2,1,0:T(8,128)(2,1)S(1)} %copy-done.5, bf16[6,1,2,16,4096]{4,3,2,1,0:T(8,128)(2,1)S(1)} %copy-done.1, f32[2,16,4096]{2,1,0:T(8,128)S(1)} %copy-done, ...), custom_call_target="tpu_custom_call" | custom-call | flops 100000000 | bytes 6000000 | tf_op jit(solution)/shard_map/update_amps/pallas_call | solution.py:346
  54.0 3.0 %collective-permute-done.9 = f32[8,128]{1,0:T(8,128)S(1)} collective-permute-done((f32[8,128]{1,0:T(8,128)S(1)}, f32[8,128]{1,0:T(8,128)S(1)}, u32[]{:S(2)}, u32[]{:S(2)}) %collective-permute-start.9) | collective-permute-done | bytes 4128 | tf_op jit(solution)/shard_map/ppermute | solution.py:381
  57.7 3.0 %collective-permute-done.10 = f32[8,128]{1,0:T(8,128)S(1)} collective-permute-done((f32[8,128]{1,0:T(8,128)S(1)}, f32[8,128]{1,0:T(8,128)S(1)}, u32[]{:S(2)}, u32[]{:S(2)}) %collective-permute-start.10) | collective-permute-done | bytes 4128 | tf_op jit(solution)/shard_map/ppermute | solution.py:381
  60.7 1.3 %collective-permute-start.11 = (f32[8,128]{1,0:T(8,128)S(1)}, f32[8,128]{1,0:T(8,128)S(1)}, u32[]{:S(2)}, u32[]{:S(2)}) collective-permute-start(f32[8,128]{1,0:T(8,128)S(1)} %add.14), channel_id=1, source_target_pairs={{0,8},{8,0},{16,24},{24,16},{1,9},{9,1},{17,25},{25,17},{2,10},{10... | collective-permute-start | bytes 12296 | tf_op jit(solution)/shard_map/ppermute | solution.py:381
  62.0 2.3 %collective-permute-done.11 = f32[8,128]{1,0:T(8,128)S(1)} collective-permute-done((f32[8,128]{1,0:T(8,128)S(1)}, f32[8,128]{1,0:T(8,128)S(1)}, u32[]{:S(2)}, u32[]{:S(2)}) %collective-permute-start.11) | collective-permute-done | bytes 4128 | tf_op jit(solution)/shard_map/ppermute | solution.py:381
  64.3 2.3 %collective-permute-start.12 = (f32[8,128]{1,0:T(8,128)S(1)}, f32[8,128]{1,0:T(8,128)S(1)}, u32[]{:S(2)}, u32[]{:S(2)}) collective-permute-start(f32[8,128]{1,0:T(8,128)S(1)} %add.15.refs_0_), channel_id=1, source_target_pairs={{0,16},{8,24},{16,0},{24,8},{1,17},{9,25},{17,1},{25,9},{2,18},{10... | collective-permute-start | bytes 12296 | tf_op jit(solution)/shard_map/ppermute | solution.py:381
  66.5 2.2 %collective-permute-done.12.refs_1_ = f32[8,128]{1,0:T(8,128)S(1)} collective-permute-done((f32[8,128]{1,0:T(8,128)S(1)}, f32[8,128]{1,0:T(8,128)S(1)}, u32[]{:S(2)}, u32[]{:S(2)}) %collective-permute-start.12) | collective-permute-done | bytes 4128 | tf_op jit(solution)/shard_map/ppermute | solution.py:381
  69.4 1.3 %finish_gram.1 = f32[7]{0:T(128)} custom-call(f32[8,128]{1,0:T(8,128)} %copy-done.6, f32[8,128]{1,0:T(8,128)} %copy-done.7), custom_call_target="tpu_custom_call" | custom-call | tf_op jit(solution)/shard_map/finish_gram/pallas_call | solution.py:371
  (30 shorter events, 3.9 us)
Async XLA Ops:
  3.1 25.3 %collective-permute-start = (bf16[24,32,128]{2,1,0:T(8,128)(2,1)}, bf16[24,32,128]{2,1,0:T(8,128)(2,1)S(1)}, u32[]{:S(2)}, u32[]{:S(2)}) collective-permute-start(bf16[24,32,128]{2,1,0:T(8,128)(2,1)} %pack_amps.1), channel_id=1, source_target_pairs={{0,0},{1,1},{2,8},{3,9},{4,16},{5,17},{6,24},{7,25},{8,2},{9,3},{1... | collective-permute-start | bytes 589832 | tf_op jit(solution)/shard_map/ppermute | solution.py:401
  4.7 23.7 %collective-permute-start.1 = (bf16[24,32,128]{2,1,0:T(8,128)(2,1)}, bf16[24,32,128]{2,1,0:T(8,128)(2,1)S(1)}, u32[]{:S(2)}, u32[]{:S(2)}) collective-permute-start(bf16[24,32,128]{2,1,0:T(8,128)(2,1)} %pack_amps.1), channel_id=1, source_target_pairs={{0,8},{1,9},{2,0},{3,1},{4,24},{5,25},{6,16},{7,17},{8,10},{9,11},... | collective-permute-start | bytes 589832 | tf_op jit(solution)/shard_map/ppermute | solution.py:401
  9.4 19.0 %collective-permute-start.2 = (bf16[24,32,128]{2,1,0:T(8,128)(2,1)}, bf16[24,32,128]{2,1,0:T(8,128)(2,1)S(1)}, u32[]{:S(2)}, u32[]{:S(2)}) collective-permute-start(bf16[24,32,128]{2,1,0:T(8,128)(2,1)} %pack_amps.1), channel_id=1, source_target_pairs={{0,16},{1,17},{2,24},{3,25},{4,0},{5,1},{6,8},{7,9},{8,18},{9,19},... | collective-permute-start | bytes 589832 | tf_op jit(solution)/shard_map/ppermute | solution.py:401
  12.9 15.5 %collective-permute-start.3 = (bf16[24,32,128]{2,1,0:T(8,128)(2,1)}, bf16[24,32,128]{2,1,0:T(8,128)(2,1)S(1)}, u32[]{:S(2)}, u32[]{:S(2)}) collective-permute-start(bf16[24,32,128]{2,1,0:T(8,128)(2,1)} %pack_amps.1), channel_id=1, source_target_pairs={{0,24},{1,25},{2,16},{3,17},{4,8},{5,9},{6,0},{7,1},{8,26},{9,27},... | collective-permute-start | bytes 589832 | tf_op jit(solution)/shard_map/ppermute | solution.py:401
  18.8 0.8 %copy-start.4 = (s32[8,8,16]{2,1,0:T(8,128)S(1)}, s32[8,8,16]{2,1,0:T(8,128)}, u32[]{:S(2)}) copy-start(s32[8,8,16]{2,1,0:T(8,128)} %ti_ref.5) | copy-start | bytes 12292
  28.4 4.5 %collective-permute-start.4 = (bf16[96,64,128]{2,1,0:T(8,128)(2,1)}, bf16[96,64,128]{2,1,0:T(8,128)(2,1)S(1)}, u32[]{:S(2)}, u32[]{:S(2)}) collective-permute-start(bf16[96,64,128]{2,1,0:T(8,128)(2,1)} %get-tuple-element.30), channel_id=1, source_target_pairs={{0,1},{1,0},{2,3},{3,2},{4,5},{5,4},{6,7},{7,6},{8,9},{9,8},{10,11... | collective-permute-start | bytes 4718600 | tf_op jit(solution)/shard_map/ppermute | solution.py:381
  28.5 1.4 %copy-start.2 = (bf16[96,64,128]{2,1,0:T(8,128)(2,1)S(1)}, bf16[96,64,128]{2,1,0:T(8,128)(2,1)}, u32[]{:S(2)}) copy-start(bf16[96,64,128]{2,1,0:T(8,128)(2,1)} %get-tuple-element.35.tiles_ref) | copy-start | bytes 4718596
  32.9 16.3 %copy-start = (f32[2,16,4096]{2,1,0:T(8,128)S(1)}, f32[2,16,4096]{2,1,0:T(8,128)}, u32[]{:S(2)}) copy-start(f32[2,16,4096]{2,1,0:T(8,128)} %denominators.1.inv_ref) | copy-start | bytes 1572868
  32.9 16.3 %copy-start.1 = (bf16[6,1,2,16,4096]{4,3,2,1,0:T(8,128)(2,1)S(1)}, bf16[6,1,2,16,4096]{4,3,2,1,0:T(8,128)(2,1)}, u32[]{:S(2)}) copy-start(bf16[6,1,2,16,4096]{4,3,2,1,0:T(8,128)(2,1)} %hist_ref.1) | copy-start | bytes 4718596
  32.9 16.3 %copy-start.3 = (bf16[1,2,16,4096]{3,2,1,0:T(8,128)(2,1)S(1)}, bf16[1,2,16,4096]{3,2,1,0:T(8,128)(2,1)}, u32[]{:S(2)}) copy-start(bf16[1,2,16,4096]{3,2,1,0:T(8,128)(2,1)} %amps_ref.3) | copy-start | bytes 786436
  33.0 16.2 %copy-start.5 = (bf16[1,2,16,4096]{3,2,1,0:T(8,128)(2,1)S(1)}, bf16[1,2,16,4096]{3,2,1,0:T(8,128)(2,1)}, u32[]{:S(2)}) copy-start(bf16[1,2,16,4096]{3,2,1,0:T(8,128)(2,1)} %ovov_ref.1) | copy-start | bytes 786436
  35.7 6.0 %collective-permute-start.5 = (bf16[24,32,128]{2,1,0:T(8,128)(2,1)S(1)}, bf16[24,32,128]{2,1,0:T(8,128)(2,1)S(1)}, u32[]{:S(2)}, u32[]{:S(2)}) collective-permute-start(bf16[24,32,128]{2,1,0:T(8,128)(2,1)S(1)} %get-tuple-element.37), channel_id=1, source_target_pairs={{0,2},{1,3},{2,0},{3,1},{4,6},{5,7},{6,4},{7,5},{8,10},{9,11},{10,... | collective-permute-start | bytes 589832 | tf_op jit(solution)/shard_map/ppermute | solution.py:381
  35.8 11.6 %collective-permute-start.6 = (bf16[24,32,128]{2,1,0:T(8,128)(2,1)S(1)}, bf16[24,32,128]{2,1,0:T(8,128)(2,1)S(1)}, u32[]{:S(2)}, u32[]{:S(2)}) collective-permute-start(bf16[24,32,128]{2,1,0:T(8,128)(2,1)S(1)} %get-tuple-element.38), channel_id=1, source_target_pairs={{0,4},{1,5},{2,6},{3,7},{4,0},{5,1},{6,2},{7,3},{8,12},{9,13},{10,... | collective-permute-start | bytes 589832 | tf_op jit(solution)/shard_map/ppermute | solution.py:381
  38.9 10.2 %collective-permute-start.7 = (bf16[24,32,128]{2,1,0:T(8,128)(2,1)S(1)}, bf16[24,32,128]{2,1,0:T(8,128)(2,1)S(1)}, u32[]{:S(2)}, u32[]{:S(2)}) collective-permute-start(bf16[24,32,128]{2,1,0:T(8,128)(2,1)S(1)} %get-tuple-element.39), channel_id=1, source_target_pairs={{0,6},{1,7},{2,4},{3,5},{4,2},{5,3},{6,0},{7,1},{8,14},{9,15},{10,... | collective-permute-start | bytes 589832 | tf_op jit(solution)/shard_map/ppermute | solution.py:381
  52.3 1.2 %collective-permute-start.8 = (f32[8,128]{1,0:T(8,128)S(1)}, f32[8,128]{1,0:T(8,128)S(1)}, u32[]{:S(2)}, u32[]{:S(2)}) collective-permute-start(f32[8,128]{1,0:T(8,128)S(1)} %get-tuple-element.41), channel_id=1, source_target_pairs={{0,1},{1,0},{2,3},{3,2},{4,5},{5,4},{6,7},{7,6},{8,9},{9,8},{10,11... | collective-permute-start | bytes 12296 | tf_op jit(solution)/shard_map/ppermute | solution.py:381
  53.4 3.6 %collective-permute-start.9 = (f32[8,128]{1,0:T(8,128)S(1)}, f32[8,128]{1,0:T(8,128)S(1)}, u32[]{:S(2)}, u32[]{:S(2)}) collective-permute-start(f32[8,128]{1,0:T(8,128)S(1)} %add.12), channel_id=1, source_target_pairs={{0,2},{1,3},{2,0},{3,1},{4,6},{5,7},{6,4},{7,5},{8,10},{9,11},{10,... | collective-permute-start | bytes 12296 | tf_op jit(solution)/shard_map/ppermute | solution.py:381
  57.0 3.6 %collective-permute-start.10 = (f32[8,128]{1,0:T(8,128)S(1)}, f32[8,128]{1,0:T(8,128)S(1)}, u32[]{:S(2)}, u32[]{:S(2)}) collective-permute-start(f32[8,128]{1,0:T(8,128)S(1)} %add.13), channel_id=1, source_target_pairs={{0,4},{1,5},{2,6},{3,7},{4,0},{5,1},{6,2},{7,3},{8,12},{9,13},{10,... | collective-permute-start | bytes 12296 | tf_op jit(solution)/shard_map/ppermute | solution.py:381
  60.7 3.6 %collective-permute-start.11 = (f32[8,128]{1,0:T(8,128)S(1)}, f32[8,128]{1,0:T(8,128)S(1)}, u32[]{:S(2)}, u32[]{:S(2)}) collective-permute-start(f32[8,128]{1,0:T(8,128)S(1)} %add.14), channel_id=1, source_target_pairs={{0,8},{8,0},{16,24},{24,16},{1,9},{9,1},{17,25},{25,17},{2,10},{10... | collective-permute-start | bytes 12296 | tf_op jit(solution)/shard_map/ppermute | solution.py:381
  64.3 4.5 %copy-start.6 = (f32[8,128]{1,0:T(8,128)}, f32[8,128]{1,0:T(8,128)S(1)}, u32[]{:S(2)}) copy-start(f32[8,128]{1,0:T(8,128)S(1)} %add.15.refs_0_) | copy-start | bytes 12292
  64.3 4.5 %collective-permute-start.12 = (f32[8,128]{1,0:T(8,128)S(1)}, f32[8,128]{1,0:T(8,128)S(1)}, u32[]{:S(2)}, u32[]{:S(2)}) collective-permute-start(f32[8,128]{1,0:T(8,128)S(1)} %add.15.refs_0_), channel_id=1, source_target_pairs={{0,16},{8,24},{16,0},{24,8},{1,17},{9,25},{17,1},{25,9},{2,18},{10... | collective-permute-start | bytes 12296 | tf_op jit(solution)/shard_map/ppermute | solution.py:381
  68.8 0.6 copy-start.7

commit v4 on v3

--- a/solution.py
+++ b/solution.py
@@ -179,7 +179,7 @@
             pltpu.SemaphoreType.DMA,
         ],
         out_shape=[jax.ShapeDtypeStruct((15 * nmax + 8,), jnp.int32), tiles, tiles],
-        compiler_params=pltpu.CompilerParams(vmem_limit_bytes=53 * 1024 * 1024),
+        compiler_params=pltpu.CompilerParams(vmem_limit_bytes=50 * 1024 * 1024),
         cost_estimate=pl.CostEstimate(flops=10**9, bytes_accessed=40 * 10**6, transcendentals=0),
         name="prep_integrals",
     )(ti, ints)
@@ -295,7 +295,7 @@
 def update_kernel(
     capt, across, nq, ti_ref, amps_ref, ovov_ref, hist_ref, inv_ref, *refs
 ):
-    part_refs, (new_ref, gram_ref, sum_ref) = refs[:nq], refs[nq:]
+    part_refs, (new_ref, gram_ref, sum_ref, total_ref) = refs[:nq], refs[nq:]
     nhist = hist_ref.shape[0]
     first = lax.axis_index("pair")
     second = lax.axis_index("reorder") * 2
@@ -338,10 +338,11 @@
         row = jnp.zeros((1, LANES), F32)
         if m <= nhist:
             row = jnp.sum(accs[m], axis=0, keepdims=True)
-        gram_ref[m : m + 1] = row
-
-
-def update(ti, amps, ovov, history, inv, parts, capt, across):
+        total_ref[m : m + 1] = row
+    gram_ref[...] = jnp.broadcast_to(total_ref[...][None], gram_ref.shape)
+
+
+def update(ti, amps, ovov, history, inv, parts, copies, capt, across):
     nq = len(parts)
     return pl.pallas_call(
         functools.partial(update_kernel, capt, across, nq),
@@ -349,32 +350,35 @@
         out_specs=[VMEM, VMEM],
         out_shape=[
             jax.ShapeDtypeStruct(amps.shape, BF16),
-            jax.ShapeDtypeStruct((8, LANES), F32),
+            jax.ShapeDtypeStruct((copies, 8, LANES), F32),
         ],
-        scratch_shapes=[pltpu.VMEM(((LIVE2 + capt) * ROWS, LANES), F32)],
+        scratch_shapes=[
+            pltpu.VMEM(((LIVE2 + capt) * ROWS, LANES), F32),
+            pltpu.VMEM((8, LANES), F32),
+        ],
         compiler_params=pltpu.CompilerParams(vmem_limit_bytes=24 * 1024 * 1024),
         cost_estimate=pl.CostEstimate(flops=10**8, bytes_accessed=6 * 10**6, transcendentals=0),
         name="update_amps",
     )(ti, amps, ovov, history, inv, *parts)
 
 
-def finish_kernel(nhist, scale, *refs):
-    total = refs[0][...] + refs[1][...]
+def finish_kernel(nhist, scale, sums_ref, out_ref):
+    total = jnp.sum(sums_ref[...], axis=0)
     total = jnp.sum(total, axis=1, keepdims=True)
     row = lax.broadcasted_iota(jnp.int32, total.shape, 0)
     total = jnp.where(row == nhist, jnp.sqrt(jnp.maximum(total, 0.0)), total) * scale
     for m in range(nhist + 1):
-        refs[-1][m] = total[m, 0]
+        out_ref[m] = total[m, 0]
 
 
 def finish(sums, nhist, scale):
     return pl.pallas_call(
         functools.partial(finish_kernel, nhist, scale),
-        in_specs=[VMEM] * len(sums),
+        in_specs=[VMEM],
         out_specs=SMEM,
         out_shape=jax.ShapeDtypeStruct((nhist + 1,), F32),
         name="finish_gram",
-    )(*sums)
+    )(sums)
 
 
 def swap(x, axis, size, step):
@@ -407,16 +411,10 @@
     sums = multiply(0, meta, mine, turned, [], nq)
     partial = multiply(1, meta, theirs, turned, [sums], nq)
     parts = [partial[0]] + [swap(partial[e], "pair", npair, 2 * e) for e in range(1, nq)]
-    new_amps, gram = update(tile_index, amps, ovov, history, inv, parts, capt, across)
-    step = 1
-    while step < npair:
-        gram = gram + swap(gram, "pair", npair, step)
-        step *= 2
-    step = 1
-    while 2 * step < nq:
-        gram = gram + swap(gram, "reorder", nq, step)
-        step *= 2
-    sums = [gram, swap(gram, "reorder", nq, step)]
+    new_amps, gram = update(
+        tile_index, amps, ovov, history, inv, parts, npair * nq, capt, across
+    )
+    sums = lax.all_to_all(gram, axes, split_axis=0, concat_axis=0, tiled=True)
     return (new_amps, finish(sums, nhist, 1.0 / (TILE * ns)))
 
 

time: 71.3 us -> 66.1 us (0.927)
  blocking collectives: 0 us -> 11.8 us
  waiting for transfers between devices: 20.5 us -> 10.9 us
  Pallas kernels: 24 us -> 20.7 us
  starting transfers between devices: 21.2 us -> 19.2 us
  local copies, waits for them, and re-layouts: 4.14 us -> 2.15 us
    all_to_all x0 -> x1, blocking collectives: none -> 11.8 us  [local(): sums = lax.all_to_all(gram, axes, split_axis=0, concat_axis=0, tiled=True)]
    ppermute x9 -> x4, waiting for transfers between devices: 20.5 us -> 10.9 us  [swap(): return lax.ppermute(x, axis, [(n, n ^ step) for n in range(size)])]
    pallas_call x2, Pallas kernels: 5.7 us -> 3.49 us  [multiply(): pl.pallas_call(functools.partial(multiply_kernel, which, nq, nq * LIVE2 +...]
    ppermute x9 -> x4, starting transfers between devices: 9.54 us -> 7.46 us  [swap(): return lax.ppermute(x, axis, [(n, n ^ step) for n in range(size)])]
    unnamed x16 -> x10, local copies, waits for them, and re-layouts: 2.77 us -> 0.78 us
    pallas_call x1, Pallas kernels: 8.85 us -> 7.58 us  [prep(): pl.pallas_call(functools.partial(prep_kernel, capt, across, nq, nmax), in...]
  transfers between devices with their start and end apart: 13 -> 8, of which waited for: 8 -> 4; matrix products, arithmetic and copies ran while one was open for 2% -> 2% of each run, Pallas kernels for 20% -> 18%
where the time goes in v4:
time: 66.1 us; the launch traced here: 65.5 us
  Pallas kernels  20.7 us (31%)
  starting transfers between devices  19.2 us (29%)
  blocking collectives  11.8 us (18%)
  waiting for transfers between devices  10.9 us (16%)
  local copies, waits for them, and re-layouts  2.15 us (3%)
  between operations  0.75 us (1%)
    all_to_all x1, blocking collectives, local(): sums = lax.all_to_all(gram, axes, split_axis=0, concat_axis=0, tiled=True)  11.8 us
    ppermute x4, starting transfers between devices, local(): lax.ppermute(packed, axes, spread_perm(npair, nq, m))  11.8 us
    ppermute x4, waiting for transfers between devices, swap(): return lax.ppermute(x, axis, [(n, n ^ step) for n in range(size)])  10.9 us
    pallas_call x1, Pallas kernels, prep(): pl.pallas_call(functools.partial(prep_kernel, capt, across, nq, nmax), in...  7.58 us
    ppermute x4, starting transfers between devices, swap(): return lax.ppermute(x, axis, [(n, n ^ step) for n in range(size)])  7.46 us
    pallas_call x2, Pallas kernels, multiply(): pl.pallas_call(functools.partial(multiply_kernel, which, nq, nq * LIVE2 +...  3.49 us
    pallas_call x1, Pallas kernels, update(): pl.pallas_call(functools.partial(update_kernel, capt, across, nq), in_spe...  3.06 us
    pallas_call x1, Pallas kernels, denominators(): pl.pallas_call(functools.partial(denom_kernel, capt, across), in_specs=[S...  2.6 us
  transfers between devices with their start and end apart: 8, of which 4 were waited for; matrix products, arithmetic and copies ran while one was open for 2% of the time, Pallas kernels for 18%

profile of v4, /device:TPU:0, one launch (start us, length us, event | category | flops | bytes accessed | tf_op | source)
XLA Modules:
  0.0 65.5 jit_solution(3955379032801762877)
XLA Ops:
  0.6 2.4 %pack_amps.1 = bf16[24,32,128]{2,1,0:T(8,128)(2,1)} custom-call(s32[8,8,16]{2,1,0:T(8,128)} %ti_ref.5, bf16[1,2,16,4096]{3,2,1,0:T(8,128)(2,1)} %amps_ref.3), custom_call_target="tpu_custom_call" | custom-call | flops 100000000 | bytes 500000 | tf_op jit(solution)/shard_map/pack_amps/pallas_call | solution.py:62
  3.0 1.6 %collective-permute-start = (bf16[24,32,128]{2,1,0:T(8,128)(2,1)}, bf16[24,32,128]{2,1,0:T(8,128)(2,1)S(1)}, u32[]{:S(2)}, u32[]{:S(2)}) collective-permute-start(bf16[24,32,128]{2,1,0:T(8,128)(2,1)} %pack_amps.1), channel_id=1, source_target_pairs={{0,0},{1,1},{2,8},{3,9},{4,16},{5,17},{6,24},{7,25},{8,2},{9,3},{1... | collective-permute-start | bytes 589832 | tf_op jit(solution)/shard_map/ppermute | solution.py:405
  4.6 4.8 %collective-permute-start.1 = (bf16[24,32,128]{2,1,0:T(8,128)(2,1)}, bf16[24,32,128]{2,1,0:T(8,128)(2,1)S(1)}, u32[]{:S(2)}, u32[]{:S(2)}) collective-permute-start(bf16[24,32,128]{2,1,0:T(8,128)(2,1)} %pack_amps.1), channel_id=1, source_target_pairs={{0,8},{1,9},{2,0},{3,1},{4,24},{5,25},{6,16},{7,17},{8,10},{9,11},... | collective-permute-start | bytes 589832 | tf_op jit(solution)/shard_map/ppermute | solution.py:405
  9.4 3.5 %collective-permute-start.2 = (bf16[24,32,128]{2,1,0:T(8,128)(2,1)}, bf16[24,32,128]{2,1,0:T(8,128)(2,1)S(1)}, u32[]{:S(2)}, u32[]{:S(2)}) collective-permute-start(bf16[24,32,128]{2,1,0:T(8,128)(2,1)} %pack_amps.1), channel_id=1, source_target_pairs={{0,16},{1,17},{2,24},{3,25},{4,0},{5,1},{6,8},{7,9},{8,18},{9,19},... | collective-permute-start | bytes 589832 | tf_op jit(solution)/shard_map/ppermute | solution.py:405
  12.9 1.9 %collective-permute-start.3 = (bf16[24,32,128]{2,1,0:T(8,128)(2,1)}, bf16[24,32,128]{2,1,0:T(8,128)(2,1)S(1)}, u32[]{:S(2)}, u32[]{:S(2)}) collective-permute-start(bf16[24,32,128]{2,1,0:T(8,128)(2,1)} %pack_amps.1), channel_id=1, source_target_pairs={{0,24},{1,25},{2,16},{3,17},{4,8},{5,9},{6,0},{7,1},{8,26},{9,27},... | collective-permute-start | bytes 589832 | tf_op jit(solution)/shard_map/ppermute | solution.py:405
  14.8 1.4 %reshape.15.vir_ref = f32[25,64]{1,0:T(8,128)} reshape(f32[1600]{0:T(1024)} %param.15) | data formatting | bytes 12800 | tf_op jit(solution)/shard_map/reshape | solution.py:225
  16.2 2.6 %denominators.1.inv_ref = f32[2,16,4096]{2,1,0:T(8,128)} custom-call(s32[8,8,16]{2,1,0:T(8,128)} %ti_ref.5, s32[8]{0:T(128)} %slab_ref, f32[200]{0:T(256)} %occ_ref, f32[25,64]{1,0:T(8,128)} %reshape.15.vir_ref), custom_call_target="tpu_custom_call" | custom-call | flops 10000000 | bytes 1000000 | tf_op jit(solution)/shard_map/denominators/pallas_call | solution.py:217
  18.8 0.8 %copy-done.3 = s32[8,8,16]{2,1,0:T(8,128)S(1)} copy-done((s32[8,8,16]{2,1,0:T(8,128)S(1)}, s32[8,8,16]{2,1,0:T(8,128)}, u32[]{:S(2)}) %copy-start.3) | copy-done | bytes 4120
  19.5 7.6 %prep_integrals.1 = (s32[1568]{0:T(1024)S(1)}, bf16[96,64,128]{2,1,0:T(8,128)(2,1)S(1)}, bf16[96,64,128]{2,1,0:T(8,128)(2,1)S(1)}) custom-call(s32[8,8,16]{2,1,0:T(8,128)S(1)} %copy-done.3, bf16[625,64,128]{2,1,0:T(8,128)(2,1)} %bitcast.9), custom_call_target="tpu_custom_call" | custom-call | flops 1000000000 | bytes 40000000 | tf_op jit(solution)/shard_map/prep_integrals/pallas_call | solution.py:171
  27.1 0.1 collective-permute-start.4
  27.2 1.9 %multiply_own.1.refs_4_ = f32[97,32,128]{2,1,0:T(8,128)S(1)} custom-call(s32[1568]{0:T(1024)S(1)} %get-tuple-element.29.meta_ref, bf16[96,64,128]{2,1,0:T(8,128)(2,1)S(1)} %get-tuple-element.35.tiles_ref, bf16[24,32,128]{2,1,0:T(8,128)(2,1)S(1)} %collective-permute-done.refs_0_, bf16[24,32,128]{2,1,0:T(8,128)(2,1)S(1)} %collective-permute-done.1.refs_1_, ...), custom_call_target="tpu_custom_call" | custom-call | flops 1000000000 | bytes 6000000 | tf_op jit(solution)/shard_map/multiply_own/pallas_call | solution.py:283
  29.1 0.0 copy-start.1
  29.1 0.0 copy-start.2
  29.2 1.4 %collective-permute-done.4.tiles_ref = bf16[96,64,128]{2,1,0:T(8,128)(2,1)S(1)} collective-permute-done((bf16[96,64,128]{2,1,0:T(8,128)(2,1)S(1)}, bf16[96,64,128]{2,1,0:T(8,128)(2,1)S(1)}, u32[]{:S(2)}, u32[]{:S(2)}) %collective-permute-start.4) | collective-permute-done | bytes 1572896 | tf_op jit(solution)/shard_map/ppermute | solution.py:385
  30.6 1.6 %multiply_sibling.1 = (bf16[24,32,128]{2,1,0:T(8,128)(2,1)S(1)}, bf16[24,32,128]{2,1,0:T(8,128)(2,1)S(1)}, bf16[24,32,128]{2,1,0:T(8,128)(2,1)S(1)}, bf16[24,32,128]{2,1,0:T(8,128)(2,1)S(1)}) custom-call(s32[1568]{0:T(1024)S(1)} %get-tuple-element.29.meta_ref, bf16[96,64,128]{2,1,0:T(8,128)(2,1)S(1)} %collective-permute-done.4.tiles_ref, ...), custom_call_target="tpu_custom_call" | custom-call | flops 1000000000 | bytes 6000000 | tf_op jit(solution)/shard_map/multiply_sibling/pallas_call | solution.py:283
  32.2 0.6 collective-permute-start.5
  32.9 5.3 %collective-permute-start.6 = (bf16[24,32,128]{2,1,0:T(8,128)(2,1)S(1)}, bf16[24,32,128]{2,1,0:T(8,128)(2,1)S(1)}, u32[]{:S(2)}, u32[]{:S(2)}) collective-permute-start(bf16[24,32,128]{2,1,0:T(8,128)(2,1)S(1)} %get-tuple-element.38), channel_id=1, source_target_pairs={{0,4},{1,5},{2,6},{3,7},{4,0},{5,1},{6,2},{7,3},{8,12},{9,13},{10,... | collective-permute-start | bytes 589832 | tf_op jit(solution)/shard_map/ppermute | solution.py:385
  38.2 1.4 %collective-permute-start.7 = (bf16[24,32,128]{2,1,0:T(8,128)(2,1)S(1)}, bf16[24,32,128]{2,1,0:T(8,128)(2,1)S(1)}, u32[]{:S(2)}, u32[]{:S(2)}) collective-permute-start(bf16[24,32,128]{2,1,0:T(8,128)(2,1)S(1)} %get-tuple-element.39), channel_id=1, source_target_pairs={{0,6},{1,7},{2,4},{3,5},{4,2},{5,3},{6,0},{7,1},{8,14},{9,15},{10,... | collective-permute-start | bytes 589832 | tf_op jit(solution)/shard_map/ppermute | solution.py:385
  39.6 0.2 collective-permute-done.5.refs_1_
  39.8 7.4 %collective-permute-done.6.refs_2_ = bf16[24,32,128]{2,1,0:T(8,128)(2,1)S(1)} collective-permute-done((bf16[24,32,128]{2,1,0:T(8,128)(2,1)S(1)}, bf16[24,32,128]{2,1,0:T(8,128)(2,1)S(1)}, u32[]{:S(2)}, u32[]{:S(2)}) %collective-permute-start.6) | collective-permute-done | bytes 196640 | tf_op jit(solution)/shard_map/ppermute | solution.py:385
  47.2 1.8 %collective-permute-done.7.refs_3_ = bf16[24,32,128]{2,1,0:T(8,128)(2,1)S(1)} collective-permute-done((bf16[24,32,128]{2,1,0:T(8,128)(2,1)S(1)}, bf16[24,32,128]{2,1,0:T(8,128)(2,1)S(1)}, u32[]{:S(2)}, u32[]{:S(2)}) %collective-permute-start.7) | collective-permute-done | bytes 196640 | tf_op jit(solution)/shard_map/ppermute | solution.py:385
  49.0 3.1 %update_amps.1 = (bf16[1,2,16,4096]{3,2,1,0:T(8,128)(2,1)}, f32[32,8,128]{2,1,0:T(8,128)S(1)}) custom-call(s32[8,8,16]{2,1,0:T(8,128)S(1)} %copy-done.3, bf16[1,2,16,4096]{3,2,1,0:T(8,128)(2,1)S(1)} %copy-done.2, bf16[1,2,16,4096]{3,2,1,0:T(8,128)(2,1)S(1)} %copy-done.4, bf16[6,1,2,16,4096]{4,3,2,1,0:T(8,128)(2,1)S(1)} %copy-done.1, ...), custom_call_target="tpu_custom_call" | custom-call | flops 100000000 | bytes 6000000 | tf_op jit(solution)/shard_map/update_amps/pallas_call | solution.py:347
  52.1 11.8 %all_to_all.5.sums_ref = f32[32,8,128]{2,1,0:T(8,128)} all-to-all(f32[32,8,128]{2,1,0:T(8,128)S(1)} %get-tuple-element.41), channel_id=1, replica_groups=mesh['reorder'=4,'pair'=8] {'reorder','pair'}, dimensions={0} | all-to-all | bytes 262144 | tf_op jit(solution)/shard_map/all_to_all | solution.py:417
  63.9 1.6 %finish_gram.1 = f32[7]{0:T(128)} custom-call(f32[32,8,128]{2,1,0:T(8,128)} %all_to_all.5.sums_ref), custom_call_target="tpu_custom_call" | custom-call | tf_op jit(solution)/shard_map/finish_gram/pallas_call | solution.py:375
  (11 shorter events, 0.0 us)
Async XLA Ops:
  3.0 24.1 %collective-permute-start = (bf16[24,32,128]{2,1,0:T(8,128)(2,1)}, bf16[24,32,128]{2,1,0:T(8,128)(2,1)S(1)}, u32[]{:S(2)}, u32[]{:S(2)}) collective-permute-start(bf16[24,32,128]{2,1,0:T(8,128)(2,1)} %pack_amps.1), channel_id=1, source_target_pairs={{0,0},{1,1},{2,8},{3,9},{4,16},{5,17},{6,24},{7,25},{8,2},{9,3},{1... | collective-permute-start | bytes 589832 | tf_op jit(solution)/shard_map/ppermute | solution.py:405
  4.6 22.5 %collective-permute-start.1 = (bf16[24,32,128]{2,1,0:T(8,128)(2,1)}, bf16[24,32,128]{2,1,0:T(8,128)(2,1)S(1)}, u32[]{:S(2)}, u32[]{:S(2)}) collective-permute-start(bf16[24,32,128]{2,1,0:T(8,128)(2,1)} %pack_amps.1), channel_id=1, source_target_pairs={{0,8},{1,9},{2,0},{3,1},{4,24},{5,25},{6,16},{7,17},{8,10},{9,11},... | collective-permute-start | bytes 589832 | tf_op jit(solution)/shard_map/ppermute | solution.py:405
  9.4 17.7 %collective-permute-start.2 = (bf16[24,32,128]{2,1,0:T(8,128)(2,1)}, bf16[24,32,128]{2,1,0:T(8,128)(2,1)S(1)}, u32[]{:S(2)}, u32[]{:S(2)}) collective-permute-start(bf16[24,32,128]{2,1,0:T(8,128)(2,1)} %pack_amps.1), channel_id=1, source_target_pairs={{0,16},{1,17},{2,24},{3,25},{4,0},{5,1},{6,8},{7,9},{8,18},{9,19},... | collective-permute-start | bytes 589832 | tf_op jit(solution)/shard_map/ppermute | solution.py:405
  12.9 14.3 %collective-permute-start.3 = (bf16[24,32,128]{2,1,0:T(8,128)(2,1)}, bf16[24,32,128]{2,1,0:T(8,128)(2,1)S(1)}, u32[]{:S(2)}, u32[]{:S(2)}) collective-permute-start(bf16[24,32,128]{2,1,0:T(8,128)(2,1)} %pack_amps.1), channel_id=1, source_target_pairs={{0,24},{1,25},{2,16},{3,17},{4,8},{5,9},{6,0},{7,1},{8,26},{9,27},... | collective-permute-start | bytes 589832 | tf_op jit(solution)/shard_map/ppermute | solution.py:405
  18.7 0.8 %copy-start.3 = (s32[8,8,16]{2,1,0:T(8,128)S(1)}, s32[8,8,16]{2,1,0:T(8,128)}, u32[]{:S(2)}) copy-start(s32[8,8,16]{2,1,0:T(8,128)} %ti_ref.5) | copy-start | bytes 12292
  27.1 3.5 %collective-permute-start.4 = (bf16[96,64,128]{2,1,0:T(8,128)(2,1)S(1)}, bf16[96,64,128]{2,1,0:T(8,128)(2,1)S(1)}, u32[]{:S(2)}, u32[]{:S(2)}) collective-permute-start(bf16[96,64,128]{2,1,0:T(8,128)(2,1)S(1)} %get-tuple-element.30), channel_id=1, source_target_pairs={{0,1},{1,0},{2,3},{3,2},{4,5},{5,4},{6,7},{7,6},{8,9},{9,8},{10,11... | collective-permute-start | bytes 4718600 | tf_op jit(solution)/shard_map/ppermute | solution.py:385
  29.1 19.9 %copy-start = (f32[2,16,4096]{2,1,0:T(8,128)S(1)}, f32[2,16,4096]{2,1,0:T(8,128)}, u32[]{:S(2)}) copy-start(f32[2,16,4096]{2,1,0:T(8,128)} %denominators.1.inv_ref) | copy-start | bytes 1572868
  29.1 19.9 %copy-start.1 = (bf16[6,1,2,16,4096]{4,3,2,1,0:T(8,128)(2,1)S(1)}, bf16[6,1,2,16,4096]{4,3,2,1,0:T(8,128)(2,1)}, u32[]{:S(2)}) copy-start(bf16[6,1,2,16,4096]{4,3,2,1,0:T(8,128)(2,1)} %hist_ref.1) | copy-start | bytes 4718596
  29.1 19.9 %copy-start.2 = (bf16[1,2,16,4096]{3,2,1,0:T(8,128)(2,1)S(1)}, bf16[1,2,16,4096]{3,2,1,0:T(8,128)(2,1)}, u32[]{:S(2)}) copy-start(bf16[1,2,16,4096]{3,2,1,0:T(8,128)(2,1)} %amps_ref.3) | copy-start | bytes 786436
  29.2 19.9 %copy-start.4 = (bf16[1,2,16,4096]{3,2,1,0:T(8,128)(2,1)S(1)}, bf16[1,2,16,4096]{3,2,1,0:T(8,128)(2,1)}, u32[]{:S(2)}) copy-start(bf16[1,2,16,4096]{3,2,1,0:T(8,128)(2,1)} %ovov_ref.1) | copy-start | bytes 786436
  32.2 7.6 %collective-permute-start.5 = (bf16[24,32,128]{2,1,0:T(8,128)(2,1)S(1)}, bf16[24,32,128]{2,1,0:T(8,128)(2,1)S(1)}, u32[]{:S(2)}, u32[]{:S(2)}) collective-permute-start(bf16[24,32,128]{2,1,0:T(8,128)(2,1)S(1)} %get-tuple-element.37), channel_id=1, source_target_pairs={{0,2},{1,3},{2,0},{3,1},{4,6},{5,7},{6,4},{7,5},{8,10},{9,11},{10,... | collective-permute-start | bytes 589832 | tf_op jit(solution)/shard_map/ppermute | solution.py:385
  32.9 14.3 %collective-permute-start.6 = (bf16[24,32,128]{2,1,0:T(8,128)(2,1)S(1)}, bf16[24,32,128]{2,1,0:T(8,128)(2,1)S(1)}, u32[]{:S(2)}, u32[]{:S(2)}) collective-permute-start(bf16[24,32,128]{2,1,0:T(8,128)(2,1)S(1)} %get-tuple-element.38), channel_id=1, source_target_pairs={{0,4},{1,5},{2,6},{3,7},{4,0},{5,1},{6,2},{7,3},{8,12},{9,13},{10,... | collective-permute-start | bytes 589832 | tf_op jit(solution)/shard_map/ppermute | solution.py:385
  38.2 10.8 %collective-permute-start.7 = (bf16[24,32,128]{2,1,0:T(8,128)(2,1)S(1)}, bf16[24,32,128]{2,1,0:T(8,128)(2,1)S(1)}, u32[]{:S(2)}, u32[]{:S(2)}) collective-permute-start(bf16[24,32,128]{2,1,0:T(8,128)(2,1)S(1)} %get-tuple-element.39), channel_id=1, source_target_pairs={{0,6},{1,7},{2,4},{3,5},{4,2},{5,3},{6,0},{7,1},{8,14},{9,15},{10,... | collective-permute-start | bytes 589832 | tf_op jit(solution)/shard_map/ppermute | solution.py:385

commit v5 on v4

--- a/solution.py
+++ b/solution.py
@@ -295,7 +295,7 @@
 def update_kernel(
     capt, across, nq, ti_ref, amps_ref, ovov_ref, hist_ref, inv_ref, *refs
 ):
-    part_refs, (new_ref, gram_ref, sum_ref, total_ref) = refs[:nq], refs[nq:]
+    part_refs, (new_ref, gram_ref, sum_ref) = refs[:nq], refs[nq:]
     nhist = hist_ref.shape[0]
     first = lax.axis_index("pair")
     second = lax.axis_index("reorder") * 2
@@ -308,38 +308,35 @@
         return carry
 
     lax.fori_loop(0, LIVE2, add, 0, unroll=4)
-    slot = lax.broadcasted_iota(jnp.int32, (capt, LANES), 0)
-    accs = [jnp.zeros((capt, LANES), F32) for _ in range(nhist + 1)]
+    slot = lax.broadcasted_iota(jnp.int32, (8, LANES), 0)
+    accs = [jnp.zeros((8, LANES), F32) for _ in range(nhist + 1)]
     for jj in range(2):
         count = count_live(ti_ref, first, second + jj, capt, across * across)
         start = 0 if jj == 0 else (LIVE2 - count) * ROWS
-        alive = slot < count
-
-        def chunk(p, accs):
-            here = pl.ds(pl.multiple_of(p * LANES, LANES), LANES)
-            cycle = jnp.concatenate(
-                [
-                    sum_ref[pl.ds(start + g * ROWS + p, 8, stride=ROWS), :]
-                    for g in range(0, capt, 8)
-                ],
-                axis=0,
-            )
-            resid = jnp.where(alive, ovov_ref[0, jj, :, here].astype(F32) + cycle, 0.0)
-            moved = amps_ref[0, jj, :, here].astype(F32) + resid * inv_ref[jj, :, here]
-            new_ref[0, jj, :, here] = jnp.where(alive, moved, 0.0).astype(BF16)
-            out = [
-                accs[m] + hist_ref[m, 0, jj, :, here].astype(F32) * resid for m in range(nhist)
-            ]
-            out.append(accs[nhist] + resid * resid)
-            return out
-
-        accs = lax.fori_loop(0, ROWS, chunk, accs, unroll=4)
-    for m in range(8):
-        row = jnp.zeros((1, LANES), F32)
-        if m <= nhist:
-            row = jnp.sum(accs[m], axis=0, keepdims=True)
-        total_ref[m : m + 1] = row
-    gram_ref[...] = jnp.broadcast_to(total_ref[...][None], gram_ref.shape)
+        for g in range(capt // 8):
+            alive = slot + g * 8 < count
+            rows = slice(g * 8, (g + 1) * 8)
+
+            def chunk(p, accs):
+                here = pl.ds(pl.multiple_of(p * LANES, LANES), LANES)
+                cycle = sum_ref[pl.ds(start + g * 8 * ROWS + p, 8, stride=ROWS), :]
+                resid = jnp.where(alive, ovov_ref[0, jj, rows, here].astype(F32) + cycle, 0.0)
+                moved = amps_ref[0, jj, rows, here].astype(F32) + resid * inv_ref[jj, rows, here]
+                new_ref[0, jj, rows, here] = jnp.where(alive, moved, 0.0).astype(BF16)
+                out = [
+                    accs[m] + hist_ref[m, 0, jj, rows, here].astype(F32) * resid
+                    for m in range(nhist)
+                ]
+                out.append(accs[nhist] + resid * resid)
+                return out
+
+            accs = lax.fori_loop(0, ROWS, chunk, accs, unroll=8)
+    lane = lax.broadcasted_iota(jnp.int32, (1, LANES), 1)
+    row = jnp.zeros((1, LANES), F32)
+    for m in range(nhist + 1):
+        row = jnp.where(lane == m, jnp.sum(accs[m]), row)
+    for n in range(gram_ref.shape[0]):
+        gram_ref[n] = row
 
 
 def update(ti, amps, ovov, history, inv, parts, copies, capt, across):
@@ -350,11 +347,10 @@
         out_specs=[VMEM, VMEM],
         out_shape=[
             jax.ShapeDtypeStruct(amps.shape, BF16),
-            jax.ShapeDtypeStruct((copies, 8, LANES), F32),
+            jax.ShapeDtypeStruct((copies, 1, LANES), F32),
         ],
         scratch_shapes=[
             pltpu.VMEM(((LIVE2 + capt) * ROWS, LANES), F32),
-            pltpu.VMEM((8, LANES), F32),
         ],
         compiler_params=pltpu.CompilerParams(vmem_limit_bytes=24 * 1024 * 1024),
         cost_estimate=pl.CostEstimate(flops=10**8, bytes_accessed=6 * 10**6, transcendentals=0),
@@ -363,12 +359,13 @@
 
 
 def finish_kernel(nhist, scale, sums_ref, out_ref):
-    total = jnp.sum(sums_ref[...], axis=0)
-    total = jnp.sum(total, axis=1, keepdims=True)
-    row = lax.broadcasted_iota(jnp.int32, total.shape, 0)
-    total = jnp.where(row == nhist, jnp.sqrt(jnp.maximum(total, 0.0)), total) * scale
+    total = sums_ref[0]
+    for n in range(1, sums_ref.shape[0]):
+        total = total + sums_ref[n]
+    lane = lax.broadcasted_iota(jnp.int32, total.shape, 1)
+    total = jnp.where(lane == nhist, jnp.sqrt(jnp.maximum(total, 0.0)), total) * scale
     for m in range(nhist + 1):
-        out_ref[m] = total[m, 0]
+        out_ref[m] = total[0, m]
 
 
 def finish(sums, nhist, scale):

time: 66.1 us -> 64.4 us (0.974)
  blocking collectives: 11.8 us -> 10.8 us
    all_to_all x1, blocking collectives: 11.8 us -> 10.8 us  [local(): sums = lax.all_to_all(gram, axes, split_axis=0, concat_axis=0, tiled=True)]
  transfers between devices with their start and end apart: 8 -> 8, of which waited for: 4 -> 4; matrix products, arithmetic and copies ran while one was open for 2% -> 2% of each run, Pallas kernels for 18% -> 19%
where the time goes in v5:
time: 64.4 us; the launch traced here: 64 us
  Pallas kernels  20.9 us (32%)
  starting transfers between devices  18.8 us (29%)
  blocking collectives  10.8 us (17%)
  waiting for transfers between devices  10.6 us (16%)
  local copies, waits for them, and re-layouts  2.15 us (3%)
  between operations  0.75 us (1%)
    ppermute x4, starting transfers between devices, local(): lax.ppermute(packed, axes, spread_perm(npair, nq, m))  11.8 us
    all_to_all x1, blocking collectives, local(): sums = lax.all_to_all(gram, axes, split_axis=0, concat_axis=0, tiled=True)  10.8 us
    ppermute x4, waiting for transfers between devices, swap(): return lax.ppermute(x, axis, [(n, n ^ step) for n in range(size)])  10.6 us
    pallas_call x1, Pallas kernels, prep(): pl.pallas_call(functools.partial(prep_kernel, capt, across, nq, nmax), in...  7.67 us
    ppermute x4, starting transfers between devices, swap(): return lax.ppermute(x, axis, [(n, n ^ step) for n in range(size)])  7 us
    pallas_call x2, Pallas kernels, multiply(): pl.pallas_call(functools.partial(multiply_kernel, which, nq, nq * LIVE2 +...  4.04 us
    pallas_call x1, Pallas kernels, update(): pl.pallas_call(functools.partial(update_kernel, capt, across, nq), in_spe...  2.81 us
    pallas_call x1, Pallas kernels, denominators(): pl.pallas_call(functools.partial(denom_kernel, capt, across), in_specs=[S...  2.6 us
  transfers between devices with their start and end apart: 8, of which 4 were waited for; matrix products, arithmetic and copies ran while one was open for 2% of the time, Pallas kernels for 19%

profile of v5, /device:TPU:0, one launch (start us, length us, event | category | flops | bytes accessed | tf_op | source)
XLA Modules:
  0.0 64.0 jit_solution(16505429193152001616)
XLA Ops:
  0.6 2.4 %pack_amps.1 = bf16[24,32,128]{2,1,0:T(8,128)(2,1)} custom-call(s32[8,8,16]{2,1,0:T(8,128)} %ti_ref.5, bf16[1,2,16,4096]{3,2,1,0:T(8,128)(2,1)} %amps_ref.3), custom_call_target="tpu_custom_call" | custom-call | flops 100000000 | bytes 500000 | tf_op jit(solution)/shard_map/pack_amps/pallas_call | solution.py:62
  3.1 1.6 %collective-permute-start = (bf16[24,32,128]{2,1,0:T(8,128)(2,1)}, bf16[24,32,128]{2,1,0:T(8,128)(2,1)S(1)}, u32[]{:S(2)}, u32[]{:S(2)}) collective-permute-start(bf16[24,32,128]{2,1,0:T(8,128)(2,1)} %pack_amps.1), channel_id=1, source_target_pairs={{0,0},{1,1},{2,8},{3,9},{4,16},{5,17},{6,24},{7,25},{8,2},{9,3},{1... | collective-permute-start | bytes 589832 | tf_op jit(solution)/shard_map/ppermute | solution.py:402
  4.6 4.8 %collective-permute-start.1 = (bf16[24,32,128]{2,1,0:T(8,128)(2,1)}, bf16[24,32,128]{2,1,0:T(8,128)(2,1)S(1)}, u32[]{:S(2)}, u32[]{:S(2)}) collective-permute-start(bf16[24,32,128]{2,1,0:T(8,128)(2,1)} %pack_amps.1), channel_id=1, source_target_pairs={{0,8},{1,9},{2,0},{3,1},{4,24},{5,25},{6,16},{7,17},{8,10},{9,11},... | collective-permute-start | bytes 589832 | tf_op jit(solution)/shard_map/ppermute | solution.py:402
  9.4 3.5 %collective-permute-start.2 = (bf16[24,32,128]{2,1,0:T(8,128)(2,1)}, bf16[24,32,128]{2,1,0:T(8,128)(2,1)S(1)}, u32[]{:S(2)}, u32[]{:S(2)}) collective-permute-start(bf16[24,32,128]{2,1,0:T(8,128)(2,1)} %pack_amps.1), channel_id=1, source_target_pairs={{0,16},{1,17},{2,24},{3,25},{4,0},{5,1},{6,8},{7,9},{8,18},{9,19},... | collective-permute-start | bytes 589832 | tf_op jit(solution)/shard_map/ppermute | solution.py:402
  12.9 1.9 %collective-permute-start.3 = (bf16[24,32,128]{2,1,0:T(8,128)(2,1)}, bf16[24,32,128]{2,1,0:T(8,128)(2,1)S(1)}, u32[]{:S(2)}, u32[]{:S(2)}) collective-permute-start(bf16[24,32,128]{2,1,0:T(8,128)(2,1)} %pack_amps.1), channel_id=1, source_target_pairs={{0,24},{1,25},{2,16},{3,17},{4,8},{5,9},{6,0},{7,1},{8,26},{9,27},... | collective-permute-start | bytes 589832 | tf_op jit(solution)/shard_map/ppermute | solution.py:402
  14.9 1.4 %reshape.15.vir_ref = f32[25,64]{1,0:T(8,128)} reshape(f32[1600]{0:T(1024)} %param.15) | data formatting | bytes 12800 | tf_op jit(solution)/shard_map/reshape | solution.py:225
  16.2 2.6 %denominators.1.inv_ref = f32[2,16,4096]{2,1,0:T(8,128)} custom-call(s32[8,8,16]{2,1,0:T(8,128)} %ti_ref.5, s32[8]{0:T(128)} %slab_ref, f32[200]{0:T(256)} %occ_ref, f32[25,64]{1,0:T(8,128)} %reshape.15.vir_ref), custom_call_target="tpu_custom_call" | custom-call | flops 10000000 | bytes 1000000 | tf_op jit(solution)/shard_map/denominators/pallas_call | solution.py:217
  18.8 0.8 %copy-done.3 = s32[8,8,16]{2,1,0:T(8,128)S(1)} copy-done((s32[8,8,16]{2,1,0:T(8,128)S(1)}, s32[8,8,16]{2,1,0:T(8,128)}, u32[]{:S(2)}) %copy-start.3) | copy-done | bytes 4120
  19.6 7.7 %prep_integrals.1 = (s32[1568]{0:T(1024)S(1)}, bf16[96,64,128]{2,1,0:T(8,128)(2,1)S(1)}, bf16[96,64,128]{2,1,0:T(8,128)(2,1)S(1)}) custom-call(s32[8,8,16]{2,1,0:T(8,128)S(1)} %copy-done.3, bf16[625,64,128]{2,1,0:T(8,128)(2,1)} %bitcast.9), custom_call_target="tpu_custom_call" | custom-call | flops 1000000000 | bytes 40000000 | tf_op jit(solution)/shard_map/prep_integrals/pallas_call | solution.py:171
  27.3 0.1 collective-permute-start.4
  27.4 1.9 %multiply_own.1.refs_4_ = f32[97,32,128]{2,1,0:T(8,128)S(1)} custom-call(s32[1568]{0:T(1024)S(1)} %get-tuple-element.29.meta_ref, bf16[96,64,128]{2,1,0:T(8,128)(2,1)S(1)} %get-tuple-element.35.tiles_ref, bf16[24,32,128]{2,1,0:T(8,128)(2,1)S(1)} %collective-permute-done.refs_0_, bf16[24,32,128]{2,1,0:T(8,128)(2,1)S(1)} %collective-permute-done.1.refs_1_, ...), custom_call_target="tpu_custom_call" | custom-call | flops 1000000000 | bytes 6000000 | tf_op jit(solution)/shard_map/multiply_own/pallas_call | solution.py:283
  29.3 0.0 copy-start.1
  29.3 0.0 copy-start.4
  29.3 1.4 %collective-permute-done.4.tiles_ref = bf16[96,64,128]{2,1,0:T(8,128)(2,1)S(1)} collective-permute-done((bf16[96,64,128]{2,1,0:T(8,128)(2,1)S(1)}, bf16[96,64,128]{2,1,0:T(8,128)(2,1)S(1)}, u32[]{:S(2)}, u32[]{:S(2)}) %collective-permute-start.4) | collective-permute-done | bytes 1572896 | tf_op jit(solution)/shard_map/ppermute | solution.py:382
  30.8 2.1 %multiply_sibling.1 = (bf16[24,32,128]{2,1,0:T(8,128)(2,1)S(1)}, bf16[24,32,128]{2,1,0:T(8,128)(2,1)S(1)}, bf16[24,32,128]{2,1,0:T(8,128)(2,1)S(1)}, bf16[24,32,128]{2,1,0:T(8,128)(2,1)S(1)}) custom-call(s32[1568]{0:T(1024)S(1)} %get-tuple-element.29.meta_ref, bf16[96,64,128]{2,1,0:T(8,128)(2,1)S(1)} %collective-permute-done.4.tiles_ref, ...), custom_call_target="tpu_custom_call" | custom-call | flops 1000000000 | bytes 6000000 | tf_op jit(solution)/shard_map/multiply_sibling/pallas_call | solution.py:283
  32.9 0.2 collective-permute-start.5
  33.2 5.3 %collective-permute-start.6 = (bf16[24,32,128]{2,1,0:T(8,128)(2,1)S(1)}, bf16[24,32,128]{2,1,0:T(8,128)(2,1)S(1)}, u32[]{:S(2)}, u32[]{:S(2)}) collective-permute-start(bf16[24,32,128]{2,1,0:T(8,128)(2,1)S(1)} %get-tuple-element.38), channel_id=1, source_target_pairs={{0,4},{1,5},{2,6},{3,7},{4,0},{5,1},{6,2},{7,3},{8,12},{9,13},{10,... | collective-permute-start | bytes 589832 | tf_op jit(solution)/shard_map/ppermute | solution.py:382
  38.5 1.4 %collective-permute-start.7 = (bf16[24,32,128]{2,1,0:T(8,128)(2,1)S(1)}, bf16[24,32,128]{2,1,0:T(8,128)(2,1)S(1)}, u32[]{:S(2)}, u32[]{:S(2)}) collective-permute-start(bf16[24,32,128]{2,1,0:T(8,128)(2,1)S(1)} %get-tuple-element.39), channel_id=1, source_target_pairs={{0,6},{1,7},{2,4},{3,5},{4,2},{5,3},{6,0},{7,1},{8,14},{9,15},{10,... | collective-permute-start | bytes 589832 | tf_op jit(solution)/shard_map/ppermute | solution.py:382
  39.9 0.4 collective-permute-done.5.refs_1_
  40.2 6.9 %collective-permute-done.6.refs_2_ = bf16[24,32,128]{2,1,0:T(8,128)(2,1)S(1)} collective-permute-done((bf16[24,32,128]{2,1,0:T(8,128)(2,1)S(1)}, bf16[24,32,128]{2,1,0:T(8,128)(2,1)S(1)}, u32[]{:S(2)}, u32[]{:S(2)}) %collective-permute-start.6) | collective-permute-done | bytes 196640 | tf_op jit(solution)/shard_map/ppermute | solution.py:382
  47.1 1.8 %collective-permute-done.7.refs_3_ = bf16[24,32,128]{2,1,0:T(8,128)(2,1)S(1)} collective-permute-done((bf16[24,32,128]{2,1,0:T(8,128)(2,1)S(1)}, bf16[24,32,128]{2,1,0:T(8,128)(2,1)S(1)}, u32[]{:S(2)}, u32[]{:S(2)}) %collective-permute-start.7) | collective-permute-done | bytes 196640 | tf_op jit(solution)/shard_map/ppermute | solution.py:382
  49.0 2.8 %update_amps.1 = (bf16[1,2,16,4096]{3,2,1,0:T(8,128)(2,1)}, f32[32,1,128]{2,1,0:T(1,128)S(1)}) custom-call(s32[8,8,16]{2,1,0:T(8,128)S(1)} %copy-done.3, bf16[1,2,16,4096]{3,2,1,0:T(8,128)(2,1)S(1)} %copy-done.2, bf16[1,2,16,4096]{3,2,1,0:T(8,128)(2,1)S(1)} %copy-done.4, bf16[6,1,2,16,4096]{4,3,2,1,0:T(8,128)(2,1)S(1)} %copy-done.1, ...), custom_call_target="tpu_custom_call" | custom-call | flops 100000000 | bytes 6000000 | tf_op jit(solution)/shard_map/update_amps/pallas_call | solution.py:344
  51.8 10.8 %all_to_all.5.sums_ref = f32[32,1,128]{2,1,0:T(1,128)} all-to-all(f32[32,1,128]{2,1,0:T(1,128)S(1)} %get-tuple-element.41), channel_id=1, replica_groups=mesh['reorder'=4,'pair'=8] {'reorder','pair'}, dimensions={0} | all-to-all | bytes 32768 | tf_op jit(solution)/shard_map/all_to_all | solution.py:414
  62.6 1.4 %finish_gram.1 = f32[7]{0:T(128)} custom-call(f32[32,1,128]{2,1,0:T(1,128)} %all_to_all.5.sums_ref), custom_call_target="tpu_custom_call" | custom-call | tf_op jit(solution)/shard_map/finish_gram/pallas_call | solution.py:372
  (11 shorter events, 0.0 us)
Async XLA Ops:
  3.1 24.2 %collective-permute-start = (bf16[24,32,128]{2,1,0:T(8,128)(2,1)}, bf16[24,32,128]{2,1,0:T(8,128)(2,1)S(1)}, u32[]{:S(2)}, u32[]{:S(2)}) collective-permute-start(bf16[24,32,128]{2,1,0:T(8,128)(2,1)} %pack_amps.1), channel_id=1, source_target_pairs={{0,0},{1,1},{2,8},{3,9},{4,16},{5,17},{6,24},{7,25},{8,2},{9,3},{1... | collective-permute-start | bytes 589832 | tf_op jit(solution)/shard_map/ppermute | solution.py:402
  4.6 22.6 %collective-permute-start.1 = (bf16[24,32,128]{2,1,0:T(8,128)(2,1)}, bf16[24,32,128]{2,1,0:T(8,128)(2,1)S(1)}, u32[]{:S(2)}, u32[]{:S(2)}) collective-permute-start(bf16[24,32,128]{2,1,0:T(8,128)(2,1)} %pack_amps.1), channel_id=1, source_target_pairs={{0,8},{1,9},{2,0},{3,1},{4,24},{5,25},{6,16},{7,17},{8,10},{9,11},... | collective-permute-start | bytes 589832 | tf_op jit(solution)/shard_map/ppermute | solution.py:402
  9.4 17.9 %collective-permute-start.2 = (bf16[24,32,128]{2,1,0:T(8,128)(2,1)}, bf16[24,32,128]{2,1,0:T(8,128)(2,1)S(1)}, u32[]{:S(2)}, u32[]{:S(2)}) collective-permute-start(bf16[24,32,128]{2,1,0:T(8,128)(2,1)} %pack_amps.1), channel_id=1, source_target_pairs={{0,16},{1,17},{2,24},{3,25},{4,0},{5,1},{6,8},{7,9},{8,18},{9,19},... | collective-permute-start | bytes 589832 | tf_op jit(solution)/shard_map/ppermute | solution.py:402
  12.9 14.3 %collective-permute-start.3 = (bf16[24,32,128]{2,1,0:T(8,128)(2,1)}, bf16[24,32,128]{2,1,0:T(8,128)(2,1)S(1)}, u32[]{:S(2)}, u32[]{:S(2)}) collective-permute-start(bf16[24,32,128]{2,1,0:T(8,128)(2,1)} %pack_amps.1), channel_id=1, source_target_pairs={{0,24},{1,25},{2,16},{3,17},{4,8},{5,9},{6,0},{7,1},{8,26},{9,27},... | collective-permute-start | bytes 589832 | tf_op jit(solution)/shard_map/ppermute | solution.py:402
  18.8 0.8 %copy-start.3 = (s32[8,8,16]{2,1,0:T(8,128)S(1)}, s32[8,8,16]{2,1,0:T(8,128)}, u32[]{:S(2)}) copy-start(s32[8,8,16]{2,1,0:T(8,128)} %ti_ref.5) | copy-start | bytes 12292
  27.3 3.5 %collective-permute-start.4 = (bf16[96,64,128]{2,1,0:T(8,128)(2,1)S(1)}, bf16[96,64,128]{2,1,0:T(8,128)(2,1)S(1)}, u32[]{:S(2)}, u32[]{:S(2)}) collective-permute-start(bf16[96,64,128]{2,1,0:T(8,128)(2,1)S(1)} %get-tuple-element.30), channel_id=1, source_target_pairs={{0,1},{1,0},{2,3},{3,2},{4,5},{5,4},{6,7},{7,6},{8,9},{9,8},{10,11... | collective-permute-start | bytes 4718600 | tf_op jit(solution)/shard_map/ppermute | solution.py:382
  29.3 19.7 %copy-start = (f32[2,16,4096]{2,1,0:T(8,128)S(1)}, f32[2,16,4096]{2,1,0:T(8,128)}, u32[]{:S(2)}) copy-start(f32[2,16,4096]{2,1,0:T(8,128)} %denominators.1.inv_ref) | copy-start | bytes 1572868
  29.3 19.7 %copy-start.1 = (bf16[6,1,2,16,4096]{4,3,2,1,0:T(8,128)(2,1)S(1)}, bf16[6,1,2,16,4096]{4,3,2,1,0:T(8,128)(2,1)}, u32[]{:S(2)}) copy-start(bf16[6,1,2,16,4096]{4,3,2,1,0:T(8,128)(2,1)} %hist_ref.1) | copy-start | bytes 4718596
  29.3 19.7 %copy-start.2 = (bf16[1,2,16,4096]{3,2,1,0:T(8,128)(2,1)S(1)}, bf16[1,2,16,4096]{3,2,1,0:T(8,128)(2,1)}, u32[]{:S(2)}) copy-start(bf16[1,2,16,4096]{3,2,1,0:T(8,128)(2,1)} %amps_ref.3) | copy-start | bytes 786436
  29.3 19.7 %copy-start.4 = (bf16[1,2,16,4096]{3,2,1,0:T(8,128)(2,1)S(1)}, bf16[1,2,16,4096]{3,2,1,0:T(8,128)(2,1)}, u32[]{:S(2)}) copy-start(bf16[1,2,16,4096]{3,2,1,0:T(8,128)(2,1)} %ovov_ref.1) | copy-start | bytes 786436
  32.9 7.3 %collective-permute-start.5 = (bf16[24,32,128]{2,1,0:T(8,128)(2,1)S(1)}, bf16[24,32,128]{2,1,0:T(8,128)(2,1)S(1)}, u32[]{:S(2)}, u32[]{:S(2)}) collective-permute-start(bf16[24,32,128]{2,1,0:T(8,128)(2,1)S(1)} %get-tuple-element.37), channel_id=1, source_target_pairs={{0,2},{1,3},{2,0},{3,1},{4,6},{5,7},{6,4},{7,5},{8,10},{9,11},{10,... | collective-permute-start | bytes 589832 | tf_op jit(solution)/shard_map/ppermute | solution.py:382
  33.2 14.0 %collective-permute-start.6 = (bf16[24,32,128]{2,1,0:T(8,128)(2,1)S(1)}, bf16[24,32,128]{2,1,0:T(8,128)(2,1)S(1)}, u32[]{:S(2)}, u32[]{:S(2)}) collective-permute-start(bf16[24,32,128]{2,1,0:T(8,128)(2,1)S(1)} %get-tuple-element.38), channel_id=1, source_target_pairs={{0,4},{1,5},{2,6},{3,7},{4,0},{5,1},{6,2},{7,3},{8,12},{9,13},{10,... | collective-permute-start | bytes 589832 | tf_op jit(solution)/shard_map/ppermute | solution.py:382
  38.5 10.5 %collective-permute-start.7 = (bf16[24,32,128]{2,1,0:T(8,128)(2,1)S(1)}, bf16[24,32,128]{2,1,0:T(8,128)(2,1)S(1)}, u32[]{:S(2)}, u32[]{:S(2)}) collective-permute-start(bf16[24,32,128]{2,1,0:T(8,128)(2,1)S(1)} %get-tuple-element.39), channel_id=1, source_target_pairs={{0,6},{1,7},{2,4},{3,5},{4,2},{5,3},{6,0},{7,1},{8,14},{9,15},{10,... | collective-permute-start | bytes 589832 | tf_op jit(solution)/shard_map/ppermute | solution.py:382

commit v6 on v5

--- a/solution.py
+++ b/solution.py
@@ -364,15 +364,14 @@
         total = total + sums_ref[n]
     lane = lax.broadcasted_iota(jnp.int32, total.shape, 1)
     total = jnp.where(lane == nhist, jnp.sqrt(jnp.maximum(total, 0.0)), total) * scale
-    for m in range(nhist + 1):
-        out_ref[m] = total[0, m]
+    out_ref[...] = total[0, : nhist + 1]
 
 
 def finish(sums, nhist, scale):
     return pl.pallas_call(
         functools.partial(finish_kernel, nhist, scale),
         in_specs=[VMEM],
-        out_specs=SMEM,
+        out_specs=VMEM,
         out_shape=jax.ShapeDtypeStruct((nhist + 1,), F32),
         name="finish_gram",
     )(sums)
@@ -399,11 +398,13 @@
     assert ns == npair == 2 * nq
     packed = pack(amps, tile_index, capt, across)
     axes = ("reorder", "pair")
-    turned = [lax.ppermute(packed, axes, spread_perm(npair, nq, m)) for m in range(nq)]
+    order = [n // 2 if n % 2 == 0 else nq - 1 - n // 2 for n in range(nq)]
+    turned = [lax.ppermute(packed, axes, spread_perm(npair, nq, m)) for m in order]
     late = lax.optimization_barrier((packed, cycle_ints, tile_index, slab, eps_occ, eps_vir))
     meta, mine, send = prep(*late[1:3], capt, across, nq)
     inv = denominators(*late[2:], capt, across)
     turned, send, inv = lax.optimization_barrier((turned, send, inv))
+    turned = [turned[order.index(m)] for m in range(nq)]
     theirs = swap(send, "pair", npair, 1)
     sums = multiply(0, meta, mine, turned, [], nq)
     partial = multiply(1, meta, theirs, turned, [sums], nq)

time: 64.4 us -> 61.7 us (0.958)
  starting transfers between devices: 18.8 us -> 16.2 us
    ppermute x4, starting transfers between devices: 11.8 us -> 9.98 us  [local(): lax.ppermute(packed, axes, spread_perm(npair, nq, m))]
    ppermute x4, starting transfers between devices: 7 us -> 6.25 us  [swap(): return lax.ppermute(x, axis, [(n, n ^ step) for n in range(size)])]
  transfers between devices with their start and end apart: 8 -> 8, of which waited for: 4 -> 4; matrix products, arithmetic and copies ran while one was open for 2% -> 2% of each run, Pallas kernels for 19% -> 20%
where the time goes in v6:
time: 61.7 us; the launch traced here: 61.1 us
  Pallas kernels  20.5 us (33%)
  starting transfers between devices  16.2 us (26%)
  blocking collectives  10.9 us (18%)
  waiting for transfers between devices  10.6 us (17%)
  local copies, waits for them, and re-layouts  2.15 us (3%)
  between operations  0.75 us (1%)
    all_to_all x1, blocking collectives, local(): sums = lax.all_to_all(gram, axes, split_axis=0, concat_axis=0, tiled=True)  10.9 us
    ppermute x4, waiting for transfers between devices, swap(): return lax.ppermute(x, axis, [(n, n ^ step) for n in range(size)])  10.6 us
    ppermute x4, starting transfers between devices, local(): lax.ppermute(packed, axes, spread_perm(npair, nq, m))  9.98 us
    pallas_call x1, Pallas kernels, prep(): pl.pallas_call(functools.partial(prep_kernel, capt, across, nq, nmax), in...  7.67 us
    ppermute x4, starting transfers between devices, swap(): return lax.ppermute(x, axis, [(n, n ^ step) for n in range(size)])  6.25 us
    pallas_call x2, Pallas kernels, multiply(): pl.pallas_call(functools.partial(multiply_kernel, which, nq, nq * LIVE2 +...  3.77 us
    pallas_call x1, Pallas kernels, update(): pl.pallas_call(functools.partial(update_kernel, capt, across, nq), in_spe...  2.81 us
    pallas_call x1, Pallas kernels, denominators(): pl.pallas_call(functools.partial(denom_kernel, capt, across), in_specs=[S...  2.6 us
  transfers between devices with their start and end apart: 8, of which 4 were waited for; matrix products, arithmetic and copies ran while one was open for 2% of the time, Pallas kernels for 20%

profile of v6, /device:TPU:0, one launch (start us, length us, event | category | flops | bytes accessed | tf_op | source)
XLA Modules:
  0.0 61.1 jit_solution(10124004946345983243)
XLA Ops:
  0.6 2.4 %pack_amps.1 = bf16[24,32,128]{2,1,0:T(8,128)(2,1)} custom-call(s32[8,8,16]{2,1,0:T(8,128)} %ti_ref.5, bf16[1,2,16,4096]{3,2,1,0:T(8,128)(2,1)} %amps_ref.3), custom_call_target="tpu_custom_call" | custom-call | flops 100000000 | bytes 500000 | tf_op jit(solution)/shard_map/pack_amps/pallas_call | solution.py:62
  3.0 1.6 %collective-permute-start = (bf16[24,32,128]{2,1,0:T(8,128)(2,1)}, bf16[24,32,128]{2,1,0:T(8,128)(2,1)S(1)}, u32[]{:S(2)}, u32[]{:S(2)}) collective-permute-start(bf16[24,32,128]{2,1,0:T(8,128)(2,1)} %pack_amps.1), channel_id=1, source_target_pairs={{0,0},{1,1},{2,8},{3,9},{4,16},{5,17},{6,24},{7,25},{8,2},{9,3},{1... | collective-permute-start | bytes 589832 | tf_op jit(solution)/shard_map/ppermute | solution.py:402
  4.6 7.5 %collective-permute-start.1 = (bf16[24,32,128]{2,1,0:T(8,128)(2,1)}, bf16[24,32,128]{2,1,0:T(8,128)(2,1)S(1)}, u32[]{:S(2)}, u32[]{:S(2)}) collective-permute-start(bf16[24,32,128]{2,1,0:T(8,128)(2,1)} %pack_amps.1), channel_id=1, source_target_pairs={{0,24},{1,25},{2,16},{3,17},{4,8},{5,9},{6,0},{7,1},{8,26},{9,27},... | collective-permute-start | bytes 589832 | tf_op jit(solution)/shard_map/ppermute | solution.py:402
  12.1 0.7 %collective-permute-start.2 = (bf16[24,32,128]{2,1,0:T(8,128)(2,1)}, bf16[24,32,128]{2,1,0:T(8,128)(2,1)S(1)}, u32[]{:S(2)}, u32[]{:S(2)}) collective-permute-start(bf16[24,32,128]{2,1,0:T(8,128)(2,1)} %pack_amps.1), channel_id=1, source_target_pairs={{0,8},{1,9},{2,0},{3,1},{4,24},{5,25},{6,16},{7,17},{8,10},{9,11},... | collective-permute-start | bytes 589832 | tf_op jit(solution)/shard_map/ppermute | solution.py:402
  12.8 0.2 collective-permute-start.3
  13.0 1.4 %reshape.15.vir_ref = f32[25,64]{1,0:T(8,128)} reshape(f32[1600]{0:T(1024)} %param.15) | data formatting | bytes 12800 | tf_op jit(solution)/shard_map/reshape | solution.py:225
  14.4 2.6 %denominators.1.inv_ref = f32[2,16,4096]{2,1,0:T(8,128)} custom-call(s32[8,8,16]{2,1,0:T(8,128)} %ti_ref.5, s32[8]{0:T(128)} %slab_ref, f32[200]{0:T(256)} %occ_ref, f32[25,64]{1,0:T(8,128)} %reshape.15.vir_ref), custom_call_target="tpu_custom_call" | custom-call | flops 10000000 | bytes 1000000 | tf_op jit(solution)/shard_map/denominators/pallas_call | solution.py:217
  17.0 0.8 %copy-done.3 = s32[8,8,16]{2,1,0:T(8,128)S(1)} copy-done((s32[8,8,16]{2,1,0:T(8,128)S(1)}, s32[8,8,16]{2,1,0:T(8,128)}, u32[]{:S(2)}) %copy-start.3) | copy-done | bytes 4120
  17.7 7.7 %prep_integrals.1 = (s32[1568]{0:T(1024)S(1)}, bf16[96,64,128]{2,1,0:T(8,128)(2,1)S(1)}, bf16[96,64,128]{2,1,0:T(8,128)(2,1)S(1)}) custom-call(s32[8,8,16]{2,1,0:T(8,128)S(1)} %copy-done.3, bf16[625,64,128]{2,1,0:T(8,128)(2,1)} %bitcast.9), custom_call_target="tpu_custom_call" | custom-call | flops 1000000000 | bytes 40000000 | tf_op jit(solution)/shard_map/prep_integrals/pallas_call | solution.py:171
  25.4 0.1 collective-permute-start.4
  25.5 2.2 %multiply_own.1.refs_4_ = f32[97,32,128]{2,1,0:T(8,128)S(1)} custom-call(s32[1568]{0:T(1024)S(1)} %get-tuple-element.29.meta_ref, bf16[96,64,128]{2,1,0:T(8,128)(2,1)S(1)} %get-tuple-element.35.tiles_ref, bf16[24,32,128]{2,1,0:T(8,128)(2,1)S(1)} %collective-permute-done.refs_0_, bf16[24,32,128]{2,1,0:T(8,128)(2,1)S(1)} %collective-permute-done.2.refs_1_, ...), custom_call_target="tpu_custom_call" | custom-call | flops 1000000000 | bytes 6000000 | tf_op jit(solution)/shard_map/multiply_own/pallas_call | solution.py:283
  27.7 0.0 copy-start.1
  27.7 0.0 copy-start.4
  27.7 1.2 %collective-permute-done.4.tiles_ref = bf16[96,64,128]{2,1,0:T(8,128)(2,1)S(1)} collective-permute-done((bf16[96,64,128]{2,1,0:T(8,128)(2,1)S(1)}, bf16[96,64,128]{2,1,0:T(8,128)(2,1)S(1)}, u32[]{:S(2)}, u32[]{:S(2)}) %collective-permute-start.4) | collective-permute-done | bytes 1572896 | tf_op jit(solution)/shard_map/ppermute | solution.py:381
  28.9 1.6 %multiply_sibling.1 = (bf16[24,32,128]{2,1,0:T(8,128)(2,1)S(1)}, bf16[24,32,128]{2,1,0:T(8,128)(2,1)S(1)}, bf16[24,32,128]{2,1,0:T(8,128)(2,1)S(1)}, bf16[24,32,128]{2,1,0:T(8,128)(2,1)S(1)}) custom-call(s32[1568]{0:T(1024)S(1)} %get-tuple-element.29.meta_ref, bf16[96,64,128]{2,1,0:T(8,128)(2,1)S(1)} %collective-permute-done.4.tiles_ref, ...), custom_call_target="tpu_custom_call" | custom-call | flops 1000000000 | bytes 6000000 | tf_op jit(solution)/shard_map/multiply_sibling/pallas_call | solution.py:283
  30.5 2.6 %collective-permute-start.5 = (bf16[24,32,128]{2,1,0:T(8,128)(2,1)S(1)}, bf16[24,32,128]{2,1,0:T(8,128)(2,1)S(1)}, u32[]{:S(2)}, u32[]{:S(2)}) collective-permute-start(bf16[24,32,128]{2,1,0:T(8,128)(2,1)S(1)} %get-tuple-element.37), channel_id=1, source_target_pairs={{0,2},{1,3},{2,0},{3,1},{4,6},{5,7},{6,4},{7,5},{8,10},{9,11},{10,... | collective-permute-start | bytes 589832 | tf_op jit(solution)/shard_map/ppermute | solution.py:381
  33.2 2.2 %collective-permute-start.6 = (bf16[24,32,128]{2,1,0:T(8,128)(2,1)S(1)}, bf16[24,32,128]{2,1,0:T(8,128)(2,1)S(1)}, u32[]{:S(2)}, u32[]{:S(2)}) collective-permute-start(bf16[24,32,128]{2,1,0:T(8,128)(2,1)S(1)} %get-tuple-element.38), channel_id=1, source_target_pairs={{0,4},{1,5},{2,6},{3,7},{4,0},{5,1},{6,2},{7,3},{8,12},{9,13},{10,... | collective-permute-start | bytes 589832 | tf_op jit(solution)/shard_map/ppermute | solution.py:381
  35.3 1.4 %collective-permute-start.7 = (bf16[24,32,128]{2,1,0:T(8,128)(2,1)S(1)}, bf16[24,32,128]{2,1,0:T(8,128)(2,1)S(1)}, u32[]{:S(2)}, u32[]{:S(2)}) collective-permute-start(bf16[24,32,128]{2,1,0:T(8,128)(2,1)S(1)} %get-tuple-element.39), channel_id=1, source_target_pairs={{0,6},{1,7},{2,4},{3,5},{4,2},{5,3},{6,0},{7,1},{8,14},{9,15},{10,... | collective-permute-start | bytes 589832 | tf_op jit(solution)/shard_map/ppermute | solution.py:381
  36.7 2.2 %collective-permute-done.5.refs_1_ = bf16[24,32,128]{2,1,0:T(8,128)(2,1)S(1)} collective-permute-done((bf16[24,32,128]{2,1,0:T(8,128)(2,1)S(1)}, bf16[24,32,128]{2,1,0:T(8,128)(2,1)S(1)}, u32[]{:S(2)}, u32[]{:S(2)}) %collective-permute-start.5) | collective-permute-done | bytes 196640 | tf_op jit(solution)/shard_map/ppermute | solution.py:381
  38.9 5.4 %collective-permute-done.6.refs_2_ = bf16[24,32,128]{2,1,0:T(8,128)(2,1)S(1)} collective-permute-done((bf16[24,32,128]{2,1,0:T(8,128)(2,1)S(1)}, bf16[24,32,128]{2,1,0:T(8,128)(2,1)S(1)}, u32[]{:S(2)}, u32[]{:S(2)}) %collective-permute-start.6) | collective-permute-done | bytes 196640 | tf_op jit(solution)/shard_map/ppermute | solution.py:381
  44.3 1.8 %collective-permute-done.7.refs_3_ = bf16[24,32,128]{2,1,0:T(8,128)(2,1)S(1)} collective-permute-done((bf16[24,32,128]{2,1,0:T(8,128)(2,1)S(1)}, bf16[24,32,128]{2,1,0:T(8,128)(2,1)S(1)}, u32[]{:S(2)}, u32[]{:S(2)}) %collective-permute-start.7) | collective-permute-done | bytes 196640 | tf_op jit(solution)/shard_map/ppermute | solution.py:381
  46.1 2.8 %update_amps.1 = (bf16[1,2,16,4096]{3,2,1,0:T(8,128)(2,1)}, f32[32,1,128]{2,1,0:T(1,128)S(1)}) custom-call(s32[8,8,16]{2,1,0:T(8,128)S(1)} %copy-done.3, bf16[1,2,16,4096]{3,2,1,0:T(8,128)(2,1)S(1)} %copy-done.2, bf16[1,2,16,4096]{3,2,1,0:T(8,128)(2,1)S(1)} %copy-done.4, bf16[6,1,2,16,4096]{4,3,2,1,0:T(8,128)(2,1)S(1)} %copy-done.1, ...), custom_call_target="tpu_custom_call" | custom-call | flops 100000000 | bytes 6000000 | tf_op jit(solution)/shard_map/update_amps/pallas_call | solution.py:344
  49.0 10.9 %all_to_all.5.sums_ref = f32[32,1,128]{2,1,0:T(1,128)} all-to-all(f32[32,1,128]{2,1,0:T(1,128)S(1)} %get-tuple-element.41), channel_id=1, replica_groups=mesh['reorder'=4,'pair'=8] {'reorder','pair'}, dimensions={0} | all-to-all | bytes 32768 | tf_op jit(solution)/shard_map/all_to_all | solution.py:415
  59.9 1.3 %finish_gram.1 = f32[7]{0:T(128)} custom-call(f32[32,1,128]{2,1,0:T(1,128)} %all_to_all.5.sums_ref), custom_call_target="tpu_custom_call" | custom-call | tf_op jit(solution)/shard_map/finish_gram/pallas_call | solution.py:371
  (11 shorter events, 0.0 us)
Async XLA Ops:
  3.0 22.4 %collective-permute-start = (bf16[24,32,128]{2,1,0:T(8,128)(2,1)}, bf16[24,32,128]{2,1,0:T(8,128)(2,1)S(1)}, u32[]{:S(2)}, u32[]{:S(2)}) collective-permute-start(bf16[24,32,128]{2,1,0:T(8,128)(2,1)} %pack_amps.1), channel_id=1, source_target_pairs={{0,0},{1,1},{2,8},{3,9},{4,16},{5,17},{6,24},{7,25},{8,2},{9,3},{1... | collective-permute-start | bytes 589832 | tf_op jit(solution)/shard_map/ppermute | solution.py:402
  4.6 20.8 %collective-permute-start.1 = (bf16[24,32,128]{2,1,0:T(8,128)(2,1)}, bf16[24,32,128]{2,1,0:T(8,128)(2,1)S(1)}, u32[]{:S(2)}, u32[]{:S(2)}) collective-permute-start(bf16[24,32,128]{2,1,0:T(8,128)(2,1)} %pack_amps.1), channel_id=1, source_target_pairs={{0,24},{1,25},{2,16},{3,17},{4,8},{5,9},{6,0},{7,1},{8,26},{9,27},... | collective-permute-start | bytes 589832 | tf_op jit(solution)/shard_map/ppermute | solution.py:402
  12.1 13.3 %collective-permute-start.2 = (bf16[24,32,128]{2,1,0:T(8,128)(2,1)}, bf16[24,32,128]{2,1,0:T(8,128)(2,1)S(1)}, u32[]{:S(2)}, u32[]{:S(2)}) collective-permute-start(bf16[24,32,128]{2,1,0:T(8,128)(2,1)} %pack_amps.1), channel_id=1, source_target_pairs={{0,8},{1,9},{2,0},{3,1},{4,24},{5,25},{6,16},{7,17},{8,10},{9,11},... | collective-permute-start | bytes 589832 | tf_op jit(solution)/shard_map/ppermute | solution.py:402
  12.8 12.6 %collective-permute-start.3 = (bf16[24,32,128]{2,1,0:T(8,128)(2,1)}, bf16[24,32,128]{2,1,0:T(8,128)(2,1)S(1)}, u32[]{:S(2)}, u32[]{:S(2)}) collective-permute-start(bf16[24,32,128]{2,1,0:T(8,128)(2,1)} %pack_amps.1), channel_id=1, source_target_pairs={{0,16},{1,17},{2,24},{3,25},{4,0},{5,1},{6,8},{7,9},{8,18},{9,19},... | collective-permute-start | bytes 589832 | tf_op jit(solution)/shard_map/ppermute | solution.py:402
  17.0 0.8 %copy-start.3 = (s32[8,8,16]{2,1,0:T(8,128)S(1)}, s32[8,8,16]{2,1,0:T(8,128)}, u32[]{:S(2)}) copy-start(s32[8,8,16]{2,1,0:T(8,128)} %ti_ref.5) | copy-start | bytes 12292
  25.4 3.5 %collective-permute-start.4 = (bf16[96,64,128]{2,1,0:T(8,128)(2,1)S(1)}, bf16[96,64,128]{2,1,0:T(8,128)(2,1)S(1)}, u32[]{:S(2)}, u32[]{:S(2)}) collective-permute-start(bf16[96,64,128]{2,1,0:T(8,128)(2,1)S(1)} %get-tuple-element.30), channel_id=1, source_target_pairs={{0,1},{1,0},{2,3},{3,2},{4,5},{5,4},{6,7},{7,6},{8,9},{9,8},{10,11... | collective-permute-start | bytes 4718600 | tf_op jit(solution)/shard_map/ppermute | solution.py:381
  27.7 18.4 %copy-start = (f32[2,16,4096]{2,1,0:T(8,128)S(1)}, f32[2,16,4096]{2,1,0:T(8,128)}, u32[]{:S(2)}) copy-start(f32[2,16,4096]{2,1,0:T(8,128)} %denominators.1.inv_ref) | copy-start | bytes 1572868
  27.7 18.4 %copy-start.1 = (bf16[6,1,2,16,4096]{4,3,2,1,0:T(8,128)(2,1)S(1)}, bf16[6,1,2,16,4096]{4,3,2,1,0:T(8,128)(2,1)}, u32[]{:S(2)}) copy-start(bf16[6,1,2,16,4096]{4,3,2,1,0:T(8,128)(2,1)} %hist_ref.1) | copy-start | bytes 4718596
  27.7 18.4 %copy-start.2 = (bf16[1,2,16,4096]{3,2,1,0:T(8,128)(2,1)S(1)}, bf16[1,2,16,4096]{3,2,1,0:T(8,128)(2,1)}, u32[]{:S(2)}) copy-start(bf16[1,2,16,4096]{3,2,1,0:T(8,128)(2,1)} %amps_ref.3) | copy-start | bytes 786436
  27.7 18.4 %copy-start.4 = (bf16[1,2,16,4096]{3,2,1,0:T(8,128)(2,1)S(1)}, bf16[1,2,16,4096]{3,2,1,0:T(8,128)(2,1)}, u32[]{:S(2)}) copy-start(bf16[1,2,16,4096]{3,2,1,0:T(8,128)(2,1)} %ovov_ref.1) | copy-start | bytes 786436
  30.5 8.4 %collective-permute-start.5 = (bf16[24,32,128]{2,1,0:T(8,128)(2,1)S(1)}, bf16[24,32,128]{2,1,0:T(8,128)(2,1)S(1)}, u32[]{:S(2)}, u32[]{:S(2)}) collective-permute-start(bf16[24,32,128]{2,1,0:T(8,128)(2,1)S(1)} %get-tuple-element.37), channel_id=1, source_target_pairs={{0,2},{1,3},{2,0},{3,1},{4,6},{5,7},{6,4},{7,5},{8,10},{9,11},{10,... | collective-permute-start | bytes 589832 | tf_op jit(solution)/shard_map/ppermute | solution.py:381
  33.2 11.1 %collective-permute-start.6 = (bf16[24,32,128]{2,1,0:T(8,128)(2,1)S(1)}, bf16[24,32,128]{2,1,0:T(8,128)(2,1)S(1)}, u32[]{:S(2)}, u32[]{:S(2)}) collective-permute-start(bf16[24,32,128]{2,1,0:T(8,128)(2,1)S(1)} %get-tuple-element.38), channel_id=1, source_target_pairs={{0,4},{1,5},{2,6},{3,7},{4,0},{5,1},{6,2},{7,3},{8,12},{9,13},{10,... | collective-permute-start | bytes 589832 | tf_op jit(solution)/shard_map/ppermute | solution.py:381
  35.3 10.8 %collective-permute-start.7 = (bf16[24,32,128]{2,1,0:T(8,128)(2,1)S(1)}, bf16[24,32,128]{2,1,0:T(8,128)(2,1)S(1)}, u32[]{:S(2)}, u32[]{:S(2)}) collective-permute-start(bf16[24,32,128]{2,1,0:T(8,128)(2,1)S(1)} %get-tuple-element.39), channel_id=1, source_target_pairs={{0,6},{1,7},{2,4},{3,5},{4,2},{5,3},{6,0},{7,1},{8,14},{9,15},{10,... | collective-permute-start | bytes 589832 | tf_op jit(solution)/shard_map/ppermute | solution.py:381

commit v7 on v6

--- a/solution.py
+++ b/solution.py
@@ -75,8 +75,9 @@
 
 def prep_kernel(
     capt, across, nq, nmax, ti_ref, hbm_ref,
-    meta_ref, mine_ref, send_ref, ints_ref, wide_ref, tab_ref, sem,
+    meta_ref, mine_ref, send0_ref, send1_ref, ints_ref, wide_ref, tab_ref, sem,
 ):
+    stride = nmax + 8
     fetch_ints = pltpu.make_async_copy(hbm_ref, ints_ref, sem)
     fetch_ints.start()
     dead = across * across
@@ -87,13 +88,15 @@
 
     def build(which, who, k):
         def field(f):
-            return (which * 5 + f) * nmax
+            return (which * 5 + f) * stride
 
         parity = lax.rem(k, 2)
 
-        def one_first(q, cnt):
-            i = (plane ^ q) * 2 + (who & 1)
-            out = (lax.shift_right_logical(who, 1) ^ plane ^ q) * LIVE2
+        def one_first(n, cnt):
+            e = jnp.where(n < nq // 2, nq, 2 * nq - 1) - 1 - 2 * n
+            i = who ^ (2 * e)
+            q = lax.shift_right_logical(who, 1) ^ plane ^ e
+            out = n * LIVE2
             for a in range(across + 1):
                 tab_ref[a] = -1
             live_in = jnp.int32(0)
@@ -131,54 +134,64 @@
                     cnt = cnt + hit.astype(jnp.int32)
             return cnt
 
-        total = lax.fori_loop(0, nq, one_first, jnp.int32(0))
-        meta_ref[15 * nmax + which] = total
-        return total
-
-    def gather(which, total, tiles_ref):
+        for group in range(2):
+            end = lax.fori_loop(
+                group * nq // 2, (group + 1) * nq // 2, one_first, jnp.int32(group * nmax // 2)
+            )
+            meta_ref[15 * stride + 2 * which + group] = end
+
+    def gather(which, group, tiles_ref, offset):
+        first = group * nmax // 2
+        total = meta_ref[15 * stride + 2 * which + group]
+
         def fetch(step, carry):
             for u in range(4):
-                e = jnp.minimum(step * 4 + u, total - 1)
+                e = jnp.minimum(first + step * 4 + u, total - 1)
                 for m in range(2):
-                    at = jnp.maximum(meta_ref[(which * 5 + 3 + m) * nmax + e], 0)
+                    at = jnp.maximum(meta_ref[(which * 5 + 3 + m) * stride + e], 0)
                     wide_ref[2 * u + m] = ints_ref[lax.shift_right_logical(at, 1)].astype(F32)
             for u in range(4):
-                e = jnp.minimum(step * 4 + u, total - 1)
+                e = jnp.minimum(first + step * 4 + u, total - 1)
                 for m in range(2):
-                    at = meta_ref[(which * 5 + 3 + m) * nmax + e]
+                    at = meta_ref[(which * 5 + 3 + m) * stride + e]
                     jj = jnp.maximum(at, 0) & 1
                     tile = wide_ref[2 * u + m, pl.ds(jj, ROWS, stride=2), :]
                     if m == 1:
                         tile = jnp.where(at >= 0, tile, 0.0)
-                    tiles_ref[e, m * ROWS : (m + 1) * ROWS] = tile.astype(BF16)
+                    tiles_ref[e - offset, m * ROWS : (m + 1) * ROWS] = tile.astype(BF16)
             return carry
 
-        lax.fori_loop(0, (total + 3) // 4, fetch, 0)
-
-    total_send = build(2, sibling, me)
-    total_mine = build(0, me, me)
+        lax.fori_loop(0, (total - first + 3) // 4, fetch, 0)
+
+    build(2, sibling, me)
+    build(0, me, me)
     build(1, me, sibling)
     fetch_ints.wait()
-    gather(2, total_send, send_ref)
-    gather(0, total_mine, mine_ref)
+    for group, send_ref in enumerate((send0_ref, send1_ref)):
+        gather(2, group, send_ref, group * nmax // 2)
+    for group in range(2):
+        gather(0, group, mine_ref, 0)
 
 
 def prep(cycle_ints, ti, capt, across, nq):
-    nmax = nq * LIVE2 + 8
+    nmax = nq * LIVE2
     ints = cycle_ints[0].transpose(1, 2, 0, 3).reshape(across, across, 2, ROWS, LANES)
     ints = ints.transpose(0, 1, 3, 2, 4).reshape(across * across, 2 * ROWS, LANES)
-    tiles = jax.ShapeDtypeStruct((nq * LIVE2, 2 * ROWS, LANES), BF16)
+    tiles = jax.ShapeDtypeStruct((nmax, 2 * ROWS, LANES), BF16)
+    half = jax.ShapeDtypeStruct((nmax // 2, 2 * ROWS, LANES), BF16)
     return pl.pallas_call(
         functools.partial(prep_kernel, capt, across, nq, nmax),
         in_specs=[SMEM, pl.BlockSpec(memory_space=pltpu.HBM)],
-        out_specs=[SMEM, VMEM, VMEM],
+        out_specs=[SMEM, VMEM, VMEM, VMEM],
         scratch_shapes=[
             pltpu.VMEM(ints.shape, BF16),
             pltpu.VMEM((8, 2 * ROWS, LANES), F32),
             pltpu.SMEM((64,), jnp.int32),
             pltpu.SemaphoreType.DMA,
         ],
-        out_shape=[jax.ShapeDtypeStruct((15 * nmax + 8,), jnp.int32), tiles, tiles],
+        out_shape=[
+            jax.ShapeDtypeStruct((15 * (nmax + 8) + 8,), jnp.int32), tiles, half, half
+        ],
         compiler_params=pltpu.CompilerParams(vmem_limit_bytes=50 * 1024 * 1024),
         cost_estimate=pl.CostEstimate(flops=10**9, bytes_accessed=40 * 10**6, transcendentals=0),
         name="prep_integrals",
@@ -225,13 +238,20 @@
     )(ti, slab, eps_occ, eps_vir.reshape(across, 64))
 
 
-def multiply_kernel(which, nq, nmax, unroll, meta_ref, tiles_ref, *refs):
+def sum_order(nq):
+    return [e for e in range(nq - 1, -1, -2)] + [e for e in range(nq - 2, -1, -2)]
+
+
+def multiply_kernel(group, nq, nmax, unroll, meta_ref, tiles_ref, *refs):
     amps_refs, refs = refs[:nq], refs[nq:]
-    if which == 0:
+    half = nmax // 2
+    stride = nmax + 8
+    if group is None:
         sum_ref, amps_ref = refs
         sum_ref[...] = jnp.zeros(sum_ref.shape, F32)
     else:
-        sum_ref, out_refs, amps_ref = refs[0], refs[1:-1], refs[-1]
+        own_ref, out_refs, (amps_ref, sum_ref) = refs[0], refs[1:-2], refs[-2:]
+        sum_ref[0:half] = own_ref[group * half : (group + 1) * half]
     for q in range(nq):
         amps_ref[q * LIVE2 : (q + 1) * LIVE2] = amps_refs[q][...]
     low = lax.broadcasted_iota(jnp.int32, (ROWS, LANES), 1) < 64
@@ -248,47 +268,63 @@
         ]
         return jnp.concatenate(parts, axis=0).astype(BF16)
 
-    total = meta_ref[15 * nmax + which]
-
-    def several(step, carry):
-        results = []
-        for u in range(unroll):
-            e = jnp.minimum(step * unroll + u, total - 1)
-            at = which * 5 * nmax + e
-            left = jnp.concatenate(
-                [amps_ref[meta_ref[nmax + at]], amps_ref[meta_ref[2 * nmax + at]]], axis=1
-            )
-            right = jnp.concatenate(
-                [spread(tiles_ref[e, 0:ROWS]), spread(tiles_ref[e, ROWS : 2 * ROWS])], axis=0
-            )
-            place = jnp.where(step * unroll + u < total, meta_ref[at], nq * LIVE2)
-            results.append((place, jnp.dot(left, right, preferred_element_type=F32)))
-        for place, value in results:
-            if which == 0:
-                sum_ref[place] = value
-            else:
-                sum_ref[place] += value
-        return carry
-
-    lax.fori_loop(0, (total + unroll - 1) // unroll, several, 0)
-    if which == 1:
-        for q in range(nq):
-            out_refs[q][...] = sum_ref[q * LIVE2 : (q + 1) * LIVE2].astype(BF16)
-
-
-def multiply(which, meta, tiles, amps, sums, nq):
-    block = jax.ShapeDtypeStruct((LIVE2, ROWS, LANES), BF16)
-    total = jax.ShapeDtypeStruct((nq * LIVE2 + 1, ROWS, LANES), F32)
-    out = [block] * nq if which == 1 else total
-    return pl.pallas_call(
-        functools.partial(multiply_kernel, which, nq, nq * LIVE2 + 8, 8),
+    for g in range(2) if group is None else [group]:
+        which = 0 if group is None else 1
+        first = g * half
+        total = meta_ref[15 * stride + 2 * which + g]
+
+        def several(step, carry):
+            results = []
+            for u in range(unroll):
+                e = jnp.minimum(first + step * unroll + u, total - 1)
+                at = which * 5 * stride + e
+                left = jnp.concatenate(
+                    [amps_ref[meta_ref[stride + at]], amps_ref[meta_ref[2 * stride + at]]],
+                    axis=1,
+                )
+                tile = e if group is None else e - first
+                right = jnp.concatenate(
+                    [
+                        spread(tiles_ref[tile, 0:ROWS]),
+                        spread(tiles_ref[tile, ROWS : 2 * ROWS]),
+                    ],
+                    axis=0,
+                )
+                place = meta_ref[at]
+                if group is not None:
+                    inside = first + step * unroll + u < total
+                    place = jnp.where(inside, place - first, half)
+                results.append((place, jnp.dot(left, right, preferred_element_type=F32)))
+            for place, value in results:
+                if group is None:
+                    sum_ref[place] = value
+                else:
+                    sum_ref[place] += value
+            return carry
+
+        lax.fori_loop(0, (total - first + unroll - 1) // unroll, several, 0)
+    if group is not None:
+        for n in range(nq // 2):
+            out_refs[n][...] = sum_ref[n * LIVE2 : (n + 1) * LIVE2].astype(BF16)
+
+
+def multiply(group, meta, tiles, amps, sums, nq):
+    nmax = nq * LIVE2
+    scratch = [pltpu.VMEM((nmax, ROWS, LANES), BF16)]
+    if group is None:
+        out = jax.ShapeDtypeStruct((nmax, ROWS, LANES), F32)
+    else:
+        out = [jax.ShapeDtypeStruct((LIVE2, ROWS, LANES), BF16)] * (nq // 2)
+        scratch.append(pltpu.VMEM((nmax // 2 + 1, ROWS, LANES), F32))
+    return pl.pallas_call(
+        functools.partial(multiply_kernel, group, nq, nmax, 8),
         in_specs=[SMEM] + [VMEM] * (1 + len(amps) + len(sums)),
         out_specs=jax.tree.map(lambda _: VMEM, out),
         out_shape=out,
-        scratch_shapes=[pltpu.VMEM((nq * LIVE2, ROWS, LANES), BF16)],
+        scratch_shapes=scratch,
         compiler_params=pltpu.CompilerParams(vmem_limit_bytes=24 * 1024 * 1024),
         cost_estimate=pl.CostEstimate(flops=10**9, bytes_accessed=6 * 10**6, transcendentals=0),
-        name=("multiply_own", "multiply_sibling")[which],
+        name="multiply_own" if group is None else f"multiply_sibling_{group}",
     )(meta, tiles, *amps, *sums)
 
 
@@ -398,17 +434,22 @@
     assert ns == npair == 2 * nq
     packed = pack(amps, tile_index, capt, across)
     axes = ("reorder", "pair")
-    order = [n // 2 if n % 2 == 0 else nq - 1 - n // 2 for n in range(nq)]
+    order = [n // 2 if n % 2 == 0 else nq - 1 - n // 2 for n in range(nq)][::-1]
     turned = [lax.ppermute(packed, axes, spread_perm(npair, nq, m)) for m in order]
     late = lax.optimization_barrier((packed, cycle_ints, tile_index, slab, eps_occ, eps_vir))
-    meta, mine, send = prep(*late[1:3], capt, across, nq)
+    meta, mine, *send = prep(*late[1:3], capt, across, nq)
     inv = denominators(*late[2:], capt, across)
     turned, send, inv = lax.optimization_barrier((turned, send, inv))
     turned = [turned[order.index(m)] for m in range(nq)]
-    theirs = swap(send, "pair", npair, 1)
-    sums = multiply(0, meta, mine, turned, [], nq)
-    partial = multiply(1, meta, theirs, turned, [sums], nq)
-    parts = [partial[0]] + [swap(partial[e], "pair", npair, 2 * e) for e in range(1, nq)]
+    theirs = [swap(tiles, "pair", npair, 1) for tiles in send]
+    sums = multiply(None, meta, mine, turned, [], nq)
+    partial = []
+    for group in range(2):
+        partial += multiply(group, meta, theirs[group], turned, [sums], nq)
+    parts = [
+        swap(part, "pair", npair, 2 * e) if e else part
+        for e, part in zip(sum_order(nq), partial)
+    ]
     new_amps, gram = update(
         tile_index, amps, ovov, history, inv, parts, npair * nq, capt, across
     )

time: 61.7 us -> 60.3 us (0.977)
  waiting for transfers between devices: 10.6 us -> 7.97 us
  Pallas kernels: 20.5 us -> 22.4 us
    ppermute x4 -> x5, waiting for transfers between devices: 10.6 us -> 7.96 us  [swap(): return lax.ppermute(x, axis, [(n, n ^ step) for n in range(size)])]
    pallas_call x2 -> x3, Pallas kernels: 3.77 us -> 5.4 us  [multiply(): pl.pallas_call(functools.partial(multiply_kernel, group, nq, nmax, 8), in...]
    ppermute x4 -> x5, starting transfers between devices: 6.25 us -> 5.99 us  [swap(): return lax.ppermute(x, axis, [(n, n ^ step) for n in range(size)])]
  transfers between devices with their start and end apart: 8 -> 9, of which waited for: 4 -> 2; matrix products, arithmetic and copies ran while one was open for 2% -> 2% of each run, Pallas kernels for 20% -> 26%
where the time goes in v7:
time: 60.3 us; the launch traced here: 59.8 us
  Pallas kernels  22.4 us (37%)
  starting transfers between devices  15.9 us (26%)
  blocking collectives  10.7 us (18%)
  waiting for transfers between devices  7.97 us (13%)
  local copies, waits for them, and re-layouts  2.13 us (4%)
  between operations  0.75 us (1%)
    all_to_all x1, blocking collectives, local(): sums = lax.all_to_all(gram, axes, split_axis=0, concat_axis=0, tiled=True)  10.7 us
    ppermute x4, starting transfers between devices, local(): lax.ppermute(packed, axes, spread_perm(npair, nq, m))  9.92 us
    ppermute x5, waiting for transfers between devices, swap(): return lax.ppermute(x, axis, [(n, n ^ step) for n in range(size)])  7.96 us
    pallas_call x1, Pallas kernels, prep(): pl.pallas_call(functools.partial(prep_kernel, capt, across, nq, nmax), in...  7.84 us
    ppermute x5, starting transfers between devices, swap(): return lax.ppermute(x, axis, [(n, n ^ step) for n in range(size)])  5.99 us
    pallas_call x3, Pallas kernels, multiply(): pl.pallas_call(functools.partial(multiply_kernel, group, nq, nmax, 8), in...  5.4 us
    pallas_call x1, Pallas kernels, update(): pl.pallas_call(functools.partial(update_kernel, capt, across, nq), in_spe...  2.81 us
    pallas_call x1, Pallas kernels, denominators(): pl.pallas_call(functools.partial(denom_kernel, capt, across), in_specs=[S...  2.6 us
  transfers between devices with their start and end apart: 9, of which 2 were waited for; matrix products, arithmetic and copies ran while one was open for 2% of the time, Pallas kernels for 26%

profile of v7, /device:TPU:0, one launch (start us, length us, event | category | flops | bytes accessed | tf_op | source)
XLA Modules:
  0.0 59.8 jit_solution(1998165224963773989)
XLA Ops:
  0.6 2.4 %pack_amps.1 = bf16[24,32,128]{2,1,0:T(8,128)(2,1)} custom-call(s32[8,8,16]{2,1,0:T(8,128)} %ti_ref.5, bf16[1,2,16,4096]{3,2,1,0:T(8,128)(2,1)} %amps_ref.3), custom_call_target="tpu_custom_call" | custom-call | flops 100000000 | bytes 500000 | tf_op jit(solution)/shard_map/pack_amps/pallas_call | solution.py:62
  3.1 1.6 %collective-permute-start.3 = (bf16[24,32,128]{2,1,0:T(8,128)(2,1)}, bf16[24,32,128]{2,1,0:T(8,128)(2,1)S(1)}, u32[]{:S(2)}, u32[]{:S(2)}) collective-permute-start(bf16[24,32,128]{2,1,0:T(8,128)(2,1)} %pack_amps.1), channel_id=1, source_target_pairs={{0,0},{1,1},{2,8},{3,9},{4,16},{5,17},{6,24},{7,25},{8,2},{9,3},{1... | collective-permute-start | bytes 589832 | tf_op jit(solution)/shard_map/ppermute | solution.py:438
  4.6 7.6 %collective-permute-start.2 = (bf16[24,32,128]{2,1,0:T(8,128)(2,1)}, bf16[24,32,128]{2,1,0:T(8,128)(2,1)S(1)}, u32[]{:S(2)}, u32[]{:S(2)}) collective-permute-start(bf16[24,32,128]{2,1,0:T(8,128)(2,1)} %pack_amps.1), channel_id=1, source_target_pairs={{0,24},{1,25},{2,16},{3,17},{4,8},{5,9},{6,0},{7,1},{8,26},{9,27},... | collective-permute-start | bytes 589832 | tf_op jit(solution)/shard_map/ppermute | solution.py:438
  12.2 0.7 %collective-permute-start.1 = (bf16[24,32,128]{2,1,0:T(8,128)(2,1)}, bf16[24,32,128]{2,1,0:T(8,128)(2,1)S(1)}, u32[]{:S(2)}, u32[]{:S(2)}) collective-permute-start(bf16[24,32,128]{2,1,0:T(8,128)(2,1)} %pack_amps.1), channel_id=1, source_target_pairs={{0,8},{1,9},{2,0},{3,1},{4,24},{5,25},{6,16},{7,17},{8,10},{9,11},... | collective-permute-start | bytes 589832 | tf_op jit(solution)/shard_map/ppermute | solution.py:438
  12.9 0.1 collective-permute-start
  13.0 1.4 %reshape.15.vir_ref = f32[25,64]{1,0:T(8,128)} reshape(f32[1600]{0:T(1024)} %param.15) | data formatting | bytes 12800 | tf_op jit(solution)/shard_map/reshape | solution.py:238
  14.3 2.6 %denominators.1.inv_ref = f32[2,16,4096]{2,1,0:T(8,128)} custom-call(s32[8,8,16]{2,1,0:T(8,128)} %ti_ref.5, s32[8]{0:T(128)} %slab_ref, f32[200]{0:T(256)} %occ_ref, f32[25,64]{1,0:T(8,128)} %reshape.15.vir_ref), custom_call_target="tpu_custom_call" | custom-call | flops 10000000 | bytes 1000000 | tf_op jit(solution)/shard_map/denominators/pallas_call | solution.py:230
  16.9 0.8 %copy-done.3 = s32[8,8,16]{2,1,0:T(8,128)S(1)} copy-done((s32[8,8,16]{2,1,0:T(8,128)S(1)}, s32[8,8,16]{2,1,0:T(8,128)}, u32[]{:S(2)}) %copy-start.3) | copy-done | bytes 4120
  17.7 7.8 %prep_integrals.1 = (s32[1568]{0:T(1024)S(1)}, bf16[96,64,128]{2,1,0:T(8,128)(2,1)S(1)}, bf16[48,64,128]{2,1,0:T(8,128)(2,1)S(1)}, bf16[48,64,128]{2,1,0:T(8,128)(2,1)S(1)}) custom-call(s32[8,8,16]{2,1,0:T(8,128)S(1)} %copy-done.3, bf16[625,64,128]{2,1,0:T(8,128)(2,1)} %bitcast.9), custom_call_target="tpu_custom_call" | custom-call | flops 1000000000 | bytes 40000000 | tf_op jit(solution)/shard_map/prep_integrals/pallas_call | solution.py:182
  25.6 0.0 collective-permute-done.1.refs_1_
  25.6 0.1 collective-permute-start.4
  25.7 0.5 collective-permute-start.7
  26.2 2.4 %multiply_own.1.refs_4_ = f32[96,32,128]{2,1,0:T(8,128)S(1)} custom-call(s32[1568]{0:T(1024)S(1)} %get-tuple-element.32.meta_ref, bf16[96,64,128]{2,1,0:T(8,128)(2,1)S(1)} %get-tuple-element.38.tiles_ref, bf16[24,32,128]{2,1,0:T(8,128)(2,1)S(1)} %collective-permute-done.3.refs_0_, bf16[24,32,128]{2,1,0:T(8,128)(2,1)S(1)} %collective-permute-done.1.refs_1_, ...), custom_call_target="tpu_custom_call" | custom-call | flops 1000000000 | bytes 6000000 | tf_op jit(solution)/shard_map/multiply_own/pallas_call | solution.py:319
  28.6 0.0 collective-permute-done.4.tiles_ref
  28.6 1.6 %multiply_sibling_0.1 = (bf16[24,32,128]{2,1,0:T(8,128)(2,1)S(1)}, bf16[24,32,128]{2,1,0:T(8,128)(2,1)S(1)}) custom-call(s32[1568]{0:T(1024)S(1)} %get-tuple-element.32.meta_ref, bf16[48,64,128]{2,1,0:T(8,128)(2,1)S(1)} %collective-permute-done.4.tiles_ref, bf16[24,32,128]{2,1,0:T(8,128)(2,1)S(1)} %collective-permute-done.3.refs_0_, ...), custom_call_target="tpu_custom_call" | custom-call | flops 1000000000 | bytes 6000000 | tf_op jit(solution)/shard_map/multiply_sibling_0/pallas_call | solution.py:319
  30.3 0.5 collective-permute-start.5
  30.8 4.9 %collective-permute-start.6 = (bf16[24,32,128]{2,1,0:T(8,128)(2,1)S(1)}, bf16[24,32,128]{2,1,0:T(8,128)(2,1)S(1)}, u32[]{:S(2)}, u32[]{:S(2)}) collective-permute-start(bf16[24,32,128]{2,1,0:T(8,128)(2,1)S(1)} %get-tuple-element.40), channel_id=1, source_target_pairs={{0,2},{1,3},{2,0},{3,1},{4,6},{5,7},{6,4},{7,5},{8,10},{9,11},{10,... | collective-permute-start | bytes 589832 | tf_op jit(solution)/shard_map/ppermute | solution.py:417
  35.6 1.3 %multiply_sibling_1.1 = (bf16[24,32,128]{2,1,0:T(8,128)(2,1)S(1)}, bf16[24,32,128]{2,1,0:T(8,128)(2,1)S(1)}) custom-call(s32[1568]{0:T(1024)S(1)} %get-tuple-element.32.meta_ref, bf16[48,64,128]{2,1,0:T(8,128)(2,1)S(1)} %collective-permute-done.7.tiles_ref, bf16[24,32,128]{2,1,0:T(8,128)(2,1)S(1)} %collective-permute-done.3.refs_0_, ...), custom_call_target="tpu_custom_call" | custom-call | flops 1000000000 | bytes 6000000 | tf_op jit(solution)/shard_map/multiply_sibling_1/pallas_call | solution.py:319
  37.0 0.1 collective-permute-start.8
  37.1 1.9 %collective-permute-done.5.refs_0_ = bf16[24,32,128]{2,1,0:T(8,128)(2,1)S(1)} collective-permute-done((bf16[24,32,128]{2,1,0:T(8,128)(2,1)S(1)}, bf16[24,32,128]{2,1,0:T(8,128)(2,1)S(1)}, u32[]{:S(2)}, u32[]{:S(2)}) %collective-permute-start.5) | collective-permute-done | bytes 196640 | tf_op jit(solution)/shard_map/ppermute | solution.py:417
  39.0 6.0 %collective-permute-done.6.refs_1_ = bf16[24,32,128]{2,1,0:T(8,128)(2,1)S(1)} collective-permute-done((bf16[24,32,128]{2,1,0:T(8,128)(2,1)S(1)}, bf16[24,32,128]{2,1,0:T(8,128)(2,1)S(1)}, u32[]{:S(2)}, u32[]{:S(2)}) %collective-permute-start.6) | collective-permute-done | bytes 196640 | tf_op jit(solution)/shard_map/ppermute | solution.py:417
  45.0 2.8 %update_amps.1 = (bf16[1,2,16,4096]{3,2,1,0:T(8,128)(2,1)}, f32[32,1,128]{2,1,0:T(1,128)S(1)}) custom-call(s32[8,8,16]{2,1,0:T(8,128)S(1)} %copy-done.3, bf16[1,2,16,4096]{3,2,1,0:T(8,128)(2,1)S(1)} %copy-done.2, bf16[1,2,16,4096]{3,2,1,0:T(8,128)(2,1)S(1)} %copy-done.4, bf16[6,1,2,16,4096]{4,3,2,1,0:T(8,128)(2,1)S(1)} %copy-done.1, ...), custom_call_target="tpu_custom_call" | custom-call | flops 100000000 | bytes 6000000 | tf_op jit(solution)/shard_map/update_amps/pallas_call | solution.py:380
  47.8 10.7 %all_to_all.5.sums_ref = f32[32,1,128]{2,1,0:T(1,128)} all-to-all(f32[32,1,128]{2,1,0:T(1,128)S(1)} %get-tuple-element.45), channel_id=1, replica_groups=mesh['reorder'=4,'pair'=8] {'reorder','pair'}, dimensions={0} | all-to-all | bytes 32768 | tf_op jit(solution)/shard_map/all_to_all | solution.py:456
  58.5 1.3 %finish_gram.1 = f32[7]{0:T(128)} custom-call(f32[32,1,128]{2,1,0:T(1,128)} %all_to_all.5.sums_ref), custom_call_target="tpu_custom_call" | custom-call | tf_op jit(solution)/shard_map/finish_gram/pallas_call | solution.py:407
  (14 shorter events, 0.0 us)
Async XLA Ops:
  3.1 22.5 %collective-permute-start.3 = (bf16[24,32,128]{2,1,0:T(8,128)(2,1)}, bf16[24,32,128]{2,1,0:T(8,128)(2,1)S(1)}, u32[]{:S(2)}, u32[]{:S(2)}) collective-permute-start(bf16[24,32,128]{2,1,0:T(8,128)(2,1)} %pack_amps.1), channel_id=1, source_target_pairs={{0,0},{1,1},{2,8},{3,9},{4,16},{5,17},{6,24},{7,25},{8,2},{9,3},{1... | collective-permute-start | bytes 589832 | tf_op jit(solution)/shard_map/ppermute | solution.py:438
  4.6 20.9 %collective-permute-start.2 = (bf16[24,32,128]{2,1,0:T(8,128)(2,1)}, bf16[24,32,128]{2,1,0:T(8,128)(2,1)S(1)}, u32[]{:S(2)}, u32[]{:S(2)}) collective-permute-start(bf16[24,32,128]{2,1,0:T(8,128)(2,1)} %pack_amps.1), channel_id=1, source_target_pairs={{0,24},{1,25},{2,16},{3,17},{4,8},{5,9},{6,0},{7,1},{8,26},{9,27},... | collective-permute-start | bytes 589832 | tf_op jit(solution)/shard_map/ppermute | solution.py:438
  12.2 13.4 %collective-permute-start.1 = (bf16[24,32,128]{2,1,0:T(8,128)(2,1)}, bf16[24,32,128]{2,1,0:T(8,128)(2,1)S(1)}, u32[]{:S(2)}, u32[]{:S(2)}) collective-permute-start(bf16[24,32,128]{2,1,0:T(8,128)(2,1)} %pack_amps.1), channel_id=1, source_target_pairs={{0,8},{1,9},{2,0},{3,1},{4,24},{5,25},{6,16},{7,17},{8,10},{9,11},... | collective-permute-start | bytes 589832 | tf_op jit(solution)/shard_map/ppermute | solution.py:438
  12.9 12.7 %collective-permute-start = (bf16[24,32,128]{2,1,0:T(8,128)(2,1)}, bf16[24,32,128]{2,1,0:T(8,128)(2,1)S(1)}, u32[]{:S(2)}, u32[]{:S(2)}) collective-permute-start(bf16[24,32,128]{2,1,0:T(8,128)(2,1)} %pack_amps.1), channel_id=1, source_target_pairs={{0,16},{1,17},{2,24},{3,25},{4,0},{5,1},{6,8},{7,9},{8,18},{9,19},... | collective-permute-start | bytes 589832 | tf_op jit(solution)/shard_map/ppermute | solution.py:438
  16.9 0.8 %copy-start.3 = (s32[8,8,16]{2,1,0:T(8,128)S(1)}, s32[8,8,16]{2,1,0:T(8,128)}, u32[]{:S(2)}) copy-start(s32[8,8,16]{2,1,0:T(8,128)} %ti_ref.5) | copy-start | bytes 12292
  25.6 3.0 %collective-permute-start.4 = (bf16[48,64,128]{2,1,0:T(8,128)(2,1)S(1)}, bf16[48,64,128]{2,1,0:T(8,128)(2,1)S(1)}, u32[]{:S(2)}, u32[]{:S(2)}) collective-permute-start(bf16[48,64,128]{2,1,0:T(8,128)(2,1)S(1)} %get-tuple-element.33), channel_id=1, source_target_pairs={{0,1},{1,0},{2,3},{3,2},{4,5},{5,4},{6,7},{7,6},{8,9},{9,8},{10,11... | collective-permute-start | bytes 2359304 | tf_op jit(solution)/shard_map/ppermute | solution.py:417
  25.7 10.0 %collective-permute-start.7 = (bf16[48,64,128]{2,1,0:T(8,128)(2,1)S(1)}, bf16[48,64,128]{2,1,0:T(8,128)(2,1)S(1)}, u32[]{:S(2)}, u32[]{:S(2)}) collective-permute-start(bf16[48,64,128]{2,1,0:T(8,128)(2,1)S(1)} %get-tuple-element.41), channel_id=1, source_target_pairs={{0,1},{1,0},{2,3},{3,2},{4,5},{5,4},{6,7},{7,6},{8,9},{9,8},{10,11... | collective-permute-start | bytes 2359304 | tf_op jit(solution)/shard_map/ppermute | solution.py:417
  30.3 8.7 %collective-permute-start.5 = (bf16[24,32,128]{2,1,0:T(8,128)(2,1)S(1)}, bf16[24,32,128]{2,1,0:T(8,128)(2,1)S(1)}, u32[]{:S(2)}, u32[]{:S(2)}) collective-permute-start(bf16[24,32,128]{2,1,0:T(8,128)(2,1)S(1)} %get-tuple-element.39), channel_id=1, source_target_pairs={{0,6},{1,7},{2,4},{3,5},{4,2},{5,3},{6,0},{7,1},{8,14},{9,15},{10,... | collective-permute-start | bytes 589832 | tf_op jit(solution)/shard_map/ppermute | solution.py:417
  30.8 14.2 %copy-start = (f32[2,16,4096]{2,1,0:T(8,128)S(1)}, f32[2,16,4096]{2,1,0:T(8,128)}, u32[]{:S(2)}) copy-start(f32[2,16,4096]{2,1,0:T(8,128)} %denominators.1.inv_ref) | copy-start | bytes 1572868
  30.8 14.3 %copy-start.1 = (bf16[6,1,2,16,4096]{4,3,2,1,0:T(8,128)(2,1)S(1)}, bf16[6,1,2,16,4096]{4,3,2,1,0:T(8,128)(2,1)}, u32[]{:S(2)}) copy-start(bf16[6,1,2,16,4096]{4,3,2,1,0:T(8,128)(2,1)} %hist_ref.1) | copy-start | bytes 4718596
  30.8 14.3 %copy-start.2 = (bf16[1,2,16,4096]{3,2,1,0:T(8,128)(2,1)S(1)}, bf16[1,2,16,4096]{3,2,1,0:T(8,128)(2,1)}, u32[]{:S(2)}) copy-start(bf16[1,2,16,4096]{3,2,1,0:T(8,128)(2,1)} %amps_ref.3) | copy-start | bytes 786436
  30.8 14.3 %copy-start.4 = (bf16[1,2,16,4096]{3,2,1,0:T(8,128)(2,1)S(1)}, bf16[1,2,16,4096]{3,2,1,0:T(8,128)(2,1)}, u32[]{:S(2)}) copy-start(bf16[1,2,16,4096]{3,2,1,0:T(8,128)(2,1)} %ovov_ref.1) | copy-start | bytes 786436
  30.8 14.2 %collective-permute-start.6 = (bf16[24,32,128]{2,1,0:T(8,128)(2,1)S(1)}, bf16[24,32,128]{2,1,0:T(8,128)(2,1)S(1)}, u32[]{:S(2)}, u32[]{:S(2)}) collective-permute-start(bf16[24,32,128]{2,1,0:T(8,128)(2,1)S(1)} %get-tuple-element.40), channel_id=1, source_target_pairs={{0,2},{1,3},{2,0},{3,1},{4,6},{5,7},{6,4},{7,5},{8,10},{9,11},{10,... | collective-permute-start | bytes 589832 | tf_op jit(solution)/shard_map/ppermute | solution.py:417
  37.0 8.0 %collective-permute-start.8 = (bf16[24,32,128]{2,1,0:T(8,128)(2,1)S(1)}, bf16[24,32,128]{2,1,0:T(8,128)(2,1)S(1)}, u32[]{:S(2)}, u32[]{:S(2)}) collective-permute-start(bf16[24,32,128]{2,1,0:T(8,128)(2,1)S(1)} %get-tuple-element.42), channel_id=1, source_target_pairs={{0,4},{1,5},{2,6},{3,7},{4,0},{5,1},{6,2},{7,3},{8,12},{9,13},{10,... | collective-permute-start | bytes 589832 | tf_op jit(solution)/shard_map/ppermute | solution.py:417

commit v8 on v7

--- a/solution.py
+++ b/solution.py
@@ -242,16 +242,25 @@
     return [e for e in range(nq - 1, -1, -2)] + [e for e in range(nq - 2, -1, -2)]
 
 
-def multiply_kernel(group, nq, nmax, unroll, meta_ref, tiles_ref, *refs):
-    amps_refs, refs = refs[:nq], refs[nq:]
+def multiply_kernel(part, nq, nmax, unroll, meta_ref, *refs):
     half = nmax // 2
     stride = nmax + 8
-    if group is None:
+    group = 1 if part == "both" else 0
+    tiles = {"own": 1, "sibling": 1, "both": 2}[part]
+    tiles_refs, amps_refs, refs = refs[:tiles], refs[tiles : tiles + nq], refs[tiles + nq :]
+    if part == "own":
         sum_ref, amps_ref = refs
+        work = [(0, tiles_refs[0], 0)]
+    elif part == "sibling":
+        own_ref, out_refs, (amps_ref, sum_ref) = refs[0], refs[1:-2], refs[-2:]
+        work = [(1, tiles_refs[0], 0)]
+    else:
+        out_refs, (amps_ref, sum_ref) = refs[:-2], refs[-2:]
+        work = [(0, tiles_refs[0], 0), (1, tiles_refs[1], half)]
+    if part == "sibling":
+        sum_ref[0:half] = own_ref[0:half]
+    else:
         sum_ref[...] = jnp.zeros(sum_ref.shape, F32)
-    else:
-        own_ref, out_refs, (amps_ref, sum_ref) = refs[0], refs[1:-2], refs[-2:]
-        sum_ref[0:half] = own_ref[group * half : (group + 1) * half]
     for q in range(nq):
         amps_ref[q * LIVE2 : (q + 1) * LIVE2] = amps_refs[q][...]
     low = lax.broadcasted_iota(jnp.int32, (ROWS, LANES), 1) < 64
@@ -268,10 +277,9 @@
         ]
         return jnp.concatenate(parts, axis=0).astype(BF16)
 
-    for g in range(2) if group is None else [group]:
-        which = 0 if group is None else 1
-        first = g * half
-        total = meta_ref[15 * stride + 2 * which + g]
+    first = group * half
+    for which, tiles_ref, offset in work:
+        total = meta_ref[15 * stride + 2 * which + group]
 
         def several(step, carry):
             results = []
@@ -282,50 +290,48 @@
                     [amps_ref[meta_ref[stride + at]], amps_ref[meta_ref[2 * stride + at]]],
                     axis=1,
                 )
-                tile = e if group is None else e - first
                 right = jnp.concatenate(
                     [
-                        spread(tiles_ref[tile, 0:ROWS]),
-                        spread(tiles_ref[tile, ROWS : 2 * ROWS]),
+                        spread(tiles_ref[e - offset, 0:ROWS]),
+                        spread(tiles_ref[e - offset, ROWS : 2 * ROWS]),
                     ],
                     axis=0,
                 )
-                place = meta_ref[at]
-                if group is not None:
-                    inside = first + step * unroll + u < total
-                    place = jnp.where(inside, place - first, half)
+                inside = first + step * unroll + u < total
+                place = jnp.where(inside, meta_ref[at] - first, half)
                 results.append((place, jnp.dot(left, right, preferred_element_type=F32)))
             for place, value in results:
-                if group is None:
+                if which == 0:
                     sum_ref[place] = value
                 else:
                     sum_ref[place] += value
             return carry
 
         lax.fori_loop(0, (total - first + unroll - 1) // unroll, several, 0)
-    if group is not None:
+    if part != "own":
         for n in range(nq // 2):
             out_refs[n][...] = sum_ref[n * LIVE2 : (n + 1) * LIVE2].astype(BF16)
 
 
-def multiply(group, meta, tiles, amps, sums, nq):
+def multiply(part, meta, tiles, amps, sums, nq):
     nmax = nq * LIVE2
     scratch = [pltpu.VMEM((nmax, ROWS, LANES), BF16)]
-    if group is None:
-        out = jax.ShapeDtypeStruct((nmax, ROWS, LANES), F32)
+    sum_shape = (nmax // 2 + 1, ROWS, LANES)
+    if part == "own":
+        out = jax.ShapeDtypeStruct(sum_shape, F32)
     else:
         out = [jax.ShapeDtypeStruct((LIVE2, ROWS, LANES), BF16)] * (nq // 2)
-        scratch.append(pltpu.VMEM((nmax // 2 + 1, ROWS, LANES), F32))
-    return pl.pallas_call(
-        functools.partial(multiply_kernel, group, nq, nmax, 8),
-        in_specs=[SMEM] + [VMEM] * (1 + len(amps) + len(sums)),
+        scratch.append(pltpu.VMEM(sum_shape, F32))
+    return pl.pallas_call(
+        functools.partial(multiply_kernel, part, nq, nmax, 8),
+        in_specs=[SMEM] + [VMEM] * (len(tiles) + len(amps) + len(sums)),
         out_specs=jax.tree.map(lambda _: VMEM, out),
         out_shape=out,
         scratch_shapes=scratch,
         compiler_params=pltpu.CompilerParams(vmem_limit_bytes=24 * 1024 * 1024),
         cost_estimate=pl.CostEstimate(flops=10**9, bytes_accessed=6 * 10**6, transcendentals=0),
-        name="multiply_own" if group is None else f"multiply_sibling_{group}",
-    )(meta, tiles, *amps, *sums)
+        name="multiply_" + part,
+    )(meta, *tiles, *amps, *sums)
 
 
 def update_kernel(
@@ -442,10 +448,10 @@
     turned, send, inv = lax.optimization_barrier((turned, send, inv))
     turned = [turned[order.index(m)] for m in range(nq)]
     theirs = [swap(tiles, "pair", npair, 1) for tiles in send]
-    sums = multiply(None, meta, mine, turned, [], nq)
-    partial = []
-    for group in range(2):
-        partial += multiply(group, meta, theirs[group], turned, [sums], nq)
+    sums = multiply("own", meta, [mine], turned, [], nq)
+    partial = multiply("sibling", meta, theirs[:1], turned, [sums], nq)
+    partial, mine = lax.optimization_barrier((list(partial), mine))
+    partial += multiply("both", meta, [mine, theirs[1]], turned, [], nq)
     parts = [
         swap(part, "pair", npair, 2 * e) if e else part
         for e, part in zip(sum_order(nq), partial)

time: 60.3 us -> 60.6 us (level)
  waiting for transfers between devices: 7.97 us -> 6.85 us
  starting transfers between devices: 15.9 us -> 17 us
    ppermute x5, starting transfers between devices: 5.99 us -> 7.14 us  [swap(): return lax.ppermute(x, axis, [(n, n ^ step) for n in range(size)])]
    ppermute x5, waiting for transfers between devices: 7.96 us -> 6.84 us  [swap(): return lax.ppermute(x, axis, [(n, n ^ step) for n in range(size)])]
  transfers between devices with their start and end apart: 9 -> 9, of which waited for: 2 -> 3; matrix products, arithmetic and copies ran while one was open for 2% -> 2% of each run, Pallas kernels for 26% -> 27%
where the time goes in v8:
time: 60.6 us; the launch traced here: 59.9 us
  Pallas kernels  22.6 us (37%)
  starting transfers between devices  17 us (28%)
  blocking collectives  10.5 us (17%)
  waiting for transfers between devices  6.85 us (11%)
  local copies, waits for them, and re-layouts  2.14 us (4%)
  between operations  0.77 us (1%)
    all_to_all x1, blocking collectives, local(): sums = lax.all_to_all(gram, axes, split_axis=0, concat_axis=0, tiled=True)  10.5 us
    ppermute x4, starting transfers between devices, local(): lax.ppermute(packed, axes, spread_perm(npair, nq, m))  9.9 us
    pallas_call x1, Pallas kernels, prep(): pl.pallas_call(functools.partial(prep_kernel, capt, across, nq, nmax), in...  7.84 us
    ppermute x5, starting transfers between devices, swap(): return lax.ppermute(x, axis, [(n, n ^ step) for n in range(size)])  7.14 us
    ppermute x5, waiting for transfers between devices, swap(): return lax.ppermute(x, axis, [(n, n ^ step) for n in range(size)])  6.84 us
    pallas_call x3, Pallas kernels, multiply(): pl.pallas_call(functools.partial(multiply_kernel, part, nq, nmax, 8), in_...  5.63 us
    pallas_call x1, Pallas kernels, update(): pl.pallas_call(functools.partial(update_kernel, capt, across, nq), in_spe...  2.81 us
    pallas_call x1, Pallas kernels, denominators(): pl.pallas_call(functools.partial(denom_kernel, capt, across), in_specs=[S...  2.6 us
  transfers between devices with their start and end apart: 9, of which 3 were waited for; matrix products, arithmetic and copies ran while one was open for 2% of the time, Pallas kernels for 27%

profile of v8, /device:TPU:0, one launch (start us, length us, event | category | flops | bytes accessed | tf_op | source)
XLA Modules:
  0.0 59.9 jit_solution(15622804544078963159)
XLA Ops:
  0.6 2.5 %pack_amps.1 = bf16[24,32,128]{2,1,0:T(8,128)(2,1)} custom-call(s32[8,8,16]{2,1,0:T(8,128)} %ti_ref.5, bf16[1,2,16,4096]{3,2,1,0:T(8,128)(2,1)} %amps_ref.3), custom_call_target="tpu_custom_call" | custom-call | flops 100000000 | bytes 500000 | tf_op jit(solution)/shard_map/pack_amps/pallas_call | solution.py:62
  3.1 1.6 %collective-permute-start.3 = (bf16[24,32,128]{2,1,0:T(8,128)(2,1)}, bf16[24,32,128]{2,1,0:T(8,128)(2,1)S(1)}, u32[]{:S(2)}, u32[]{:S(2)}) collective-permute-start(bf16[24,32,128]{2,1,0:T(8,128)(2,1)} %pack_amps.1), channel_id=1, source_target_pairs={{0,0},{1,1},{2,8},{3,9},{4,16},{5,17},{6,24},{7,25},{8,2},{9,3},{1... | collective-permute-start | bytes 589832 | tf_op jit(solution)/shard_map/ppermute | solution.py:444
  4.7 7.5 %collective-permute-start.2 = (bf16[24,32,128]{2,1,0:T(8,128)(2,1)}, bf16[24,32,128]{2,1,0:T(8,128)(2,1)S(1)}, u32[]{:S(2)}, u32[]{:S(2)}) collective-permute-start(bf16[24,32,128]{2,1,0:T(8,128)(2,1)} %pack_amps.1), channel_id=1, source_target_pairs={{0,24},{1,25},{2,16},{3,17},{4,8},{5,9},{6,0},{7,1},{8,26},{9,27},... | collective-permute-start | bytes 589832 | tf_op jit(solution)/shard_map/ppermute | solution.py:444
  12.1 0.7 %collective-permute-start.1 = (bf16[24,32,128]{2,1,0:T(8,128)(2,1)}, bf16[24,32,128]{2,1,0:T(8,128)(2,1)S(1)}, u32[]{:S(2)}, u32[]{:S(2)}) collective-permute-start(bf16[24,32,128]{2,1,0:T(8,128)(2,1)} %pack_amps.1), channel_id=1, source_target_pairs={{0,8},{1,9},{2,0},{3,1},{4,24},{5,25},{6,16},{7,17},{8,10},{9,11},... | collective-permute-start | bytes 589832 | tf_op jit(solution)/shard_map/ppermute | solution.py:444
  12.8 0.2 collective-permute-start
  13.0 1.4 %reshape.15.vir_ref = f32[25,64]{1,0:T(8,128)} reshape(f32[1600]{0:T(1024)} %param.15) | data formatting | bytes 12800 | tf_op jit(solution)/shard_map/reshape | solution.py:238
  14.4 2.6 %denominators.1.inv_ref = f32[2,16,4096]{2,1,0:T(8,128)} custom-call(s32[8,8,16]{2,1,0:T(8,128)} %ti_ref.5, s32[8]{0:T(128)} %slab_ref, f32[200]{0:T(256)} %occ_ref, f32[25,64]{1,0:T(8,128)} %reshape.15.vir_ref), custom_call_target="tpu_custom_call" | custom-call | flops 10000000 | bytes 1000000 | tf_op jit(solution)/shard_map/denominators/pallas_call | solution.py:230
  17.0 0.8 %copy-done.3 = s32[8,8,16]{2,1,0:T(8,128)S(1)} copy-done((s32[8,8,16]{2,1,0:T(8,128)S(1)}, s32[8,8,16]{2,1,0:T(8,128)}, u32[]{:S(2)}) %copy-start.3) | copy-done | bytes 4120
  17.7 7.8 %prep_integrals.1 = (s32[1568]{0:T(1024)S(1)}, bf16[96,64,128]{2,1,0:T(8,128)(2,1)S(1)}, bf16[48,64,128]{2,1,0:T(8,128)(2,1)S(1)}, bf16[48,64,128]{2,1,0:T(8,128)(2,1)S(1)}) custom-call(s32[8,8,16]{2,1,0:T(8,128)S(1)} %copy-done.3, bf16[625,64,128]{2,1,0:T(8,128)(2,1)} %bitcast.9), custom_call_target="tpu_custom_call" | custom-call | flops 1000000000 | bytes 40000000 | tf_op jit(solution)/shard_map/prep_integrals/pallas_call | solution.py:182
  25.6 0.1 collective-permute-start.4
  25.7 0.5 collective-permute-start.7
  26.2 1.6 %multiply_own.1.refs_5_ = f32[49,32,128]{2,1,0:T(8,128)S(1)} custom-call(s32[1568]{0:T(1024)S(1)} %get-tuple-element.35.meta_ref, bf16[96,64,128]{2,1,0:T(8,128)(2,1)S(1)} %get-tuple-element.46.refs_0_, bf16[24,32,128]{2,1,0:T(8,128)(2,1)S(1)} %collective-permute-done.3.refs_1_.refs_2_, bf16[24,32,128]{2,1,0:T(8,128)(2,1)S(1)} %collective-permute-done.1.refs_2_.refs_3_, ...), custom_call_target="tpu_custom_call" | custom-call | flops 1000000000 | bytes 6000000 | tf_op jit(solution)/shard_map/multiply_own/pallas_call | solution.py:325
  27.8 0.2 collective-permute-done.4.refs_0_
  28.0 1.3 %multiply_sibling.1 = (bf16[24,32,128]{2,1,0:T(8,128)(2,1)S(1)}, bf16[24,32,128]{2,1,0:T(8,128)(2,1)S(1)}) custom-call(s32[1568]{0:T(1024)S(1)} %get-tuple-element.35.meta_ref, bf16[48,64,128]{2,1,0:T(8,128)(2,1)S(1)} %collective-permute-done.4.refs_0_, bf16[24,32,128]{2,1,0:T(8,128)(2,1)S(1)} %collective-permute-done.3.refs_1_.refs_2_, ...), custom_call_target="tpu_custom_call" | custom-call | flops 1000000000 | bytes 6000000 | tf_op jit(solution)/shard_map/multiply_sibling/pallas_call | solution.py:325
  29.3 0.0 copy-start.4
  29.3 1.9 %collective-permute-start.5 = (bf16[24,32,128]{2,1,0:T(8,128)(2,1)S(1)}, bf16[24,32,128]{2,1,0:T(8,128)(2,1)S(1)}, u32[]{:S(2)}, u32[]{:S(2)}) collective-permute-start(bf16[24,32,128]{2,1,0:T(8,128)(2,1)S(1)} %get-tuple-element.44), channel_id=1, source_target_pairs={{0,6},{1,7},{2,4},{3,5},{4,2},{5,3},{6,0},{7,1},{8,14},{9,15},{10,... | collective-permute-start | bytes 589832 | tf_op jit(solution)/shard_map/ppermute | solution.py:423
  31.2 4.6 %collective-permute-start.6 = (bf16[24,32,128]{2,1,0:T(8,128)(2,1)S(1)}, bf16[24,32,128]{2,1,0:T(8,128)(2,1)S(1)}, u32[]{:S(2)}, u32[]{:S(2)}) collective-permute-start(bf16[24,32,128]{2,1,0:T(8,128)(2,1)S(1)} %get-tuple-element.45), channel_id=1, source_target_pairs={{0,2},{1,3},{2,0},{3,1},{4,6},{5,7},{6,4},{7,5},{8,10},{9,11},{10,... | collective-permute-start | bytes 589832 | tf_op jit(solution)/shard_map/ppermute | solution.py:423
  35.9 2.7 %multiply_both.1 = (bf16[24,32,128]{2,1,0:T(8,128)(2,1)S(1)}, bf16[24,32,128]{2,1,0:T(8,128)(2,1)S(1)}) custom-call(s32[1568]{0:T(1024)S(1)} %get-tuple-element.35.meta_ref, bf16[96,64,128]{2,1,0:T(8,128)(2,1)S(1)} %get-tuple-element.46.refs_0_, bf16[48,64,128]{2,1,0:T(8,128)(2,1)S(1)} %collective-permute-done.7.refs_1_, ...), custom_call_target="tpu_custom_call" | custom-call | flops 1000000000 | bytes 6000000 | tf_op jit(solution)/shard_map/multiply_both/pallas_call | solution.py:325
  38.6 0.1 collective-permute-start.8
  38.7 6.3 %collective-permute-done.6.refs_1_ = bf16[24,32,128]{2,1,0:T(8,128)(2,1)S(1)} collective-permute-done((bf16[24,32,128]{2,1,0:T(8,128)(2,1)S(1)}, bf16[24,32,128]{2,1,0:T(8,128)(2,1)S(1)}, u32[]{:S(2)}, u32[]{:S(2)}) %collective-permute-start.6) | collective-permute-done | bytes 196640 | tf_op jit(solution)/shard_map/ppermute | solution.py:423
  45.0 0.3 collective-permute-done.8.refs_2_
  45.3 2.8 %update_amps.1 = (bf16[1,2,16,4096]{3,2,1,0:T(8,128)(2,1)}, f32[32,1,128]{2,1,0:T(1,128)S(1)}) custom-call(s32[8,8,16]{2,1,0:T(8,128)S(1)} %copy-done.3, bf16[1,2,16,4096]{3,2,1,0:T(8,128)(2,1)S(1)} %copy-done.2, bf16[1,2,16,4096]{3,2,1,0:T(8,128)(2,1)S(1)} %copy-done.4, bf16[6,1,2,16,4096]{4,3,2,1,0:T(8,128)(2,1)S(1)} %copy-done.1, ...), custom_call_target="tpu_custom_call" | custom-call | flops 100000000 | bytes 6000000 | tf_op jit(solution)/shard_map/update_amps/pallas_call | solution.py:386
  48.1 10.5 %all_to_all.5.sums_ref = f32[32,1,128]{2,1,0:T(1,128)} all-to-all(f32[32,1,128]{2,1,0:T(1,128)S(1)} %get-tuple-element.51), channel_id=1, replica_groups=mesh['reorder'=4,'pair'=8] {'reorder','pair'}, dimensions={0} | all-to-all | bytes 32768 | tf_op jit(solution)/shard_map/all_to_all | solution.py:462
  58.7 1.3 %finish_gram.1 = f32[7]{0:T(128)} custom-call(f32[32,1,128]{2,1,0:T(1,128)} %all_to_all.5.sums_ref), custom_call_target="tpu_custom_call" | custom-call | tf_op jit(solution)/shard_map/finish_gram/pallas_call | solution.py:413
  (14 shorter events, 0.0 us)
Async XLA Ops:
  3.1 22.5 %collective-permute-start.3 = (bf16[24,32,128]{2,1,0:T(8,128)(2,1)}, bf16[24,32,128]{2,1,0:T(8,128)(2,1)S(1)}, u32[]{:S(2)}, u32[]{:S(2)}) collective-permute-start(bf16[24,32,128]{2,1,0:T(8,128)(2,1)} %pack_amps.1), channel_id=1, source_target_pairs={{0,0},{1,1},{2,8},{3,9},{4,16},{5,17},{6,24},{7,25},{8,2},{9,3},{1... | collective-permute-start | bytes 589832 | tf_op jit(solution)/shard_map/ppermute | solution.py:444
  4.7 20.9 %collective-permute-start.2 = (bf16[24,32,128]{2,1,0:T(8,128)(2,1)}, bf16[24,32,128]{2,1,0:T(8,128)(2,1)S(1)}, u32[]{:S(2)}, u32[]{:S(2)}) collective-permute-start(bf16[24,32,128]{2,1,0:T(8,128)(2,1)} %pack_amps.1), channel_id=1, source_target_pairs={{0,24},{1,25},{2,16},{3,17},{4,8},{5,9},{6,0},{7,1},{8,26},{9,27},... | collective-permute-start | bytes 589832 | tf_op jit(solution)/shard_map/ppermute | solution.py:444
  12.1 13.5 %collective-permute-start.1 = (bf16[24,32,128]{2,1,0:T(8,128)(2,1)}, bf16[24,32,128]{2,1,0:T(8,128)(2,1)S(1)}, u32[]{:S(2)}, u32[]{:S(2)}) collective-permute-start(bf16[24,32,128]{2,1,0:T(8,128)(2,1)} %pack_amps.1), channel_id=1, source_target_pairs={{0,8},{1,9},{2,0},{3,1},{4,24},{5,25},{6,16},{7,17},{8,10},{9,11},... | collective-permute-start | bytes 589832 | tf_op jit(solution)/shard_map/ppermute | solution.py:444
  12.8 12.8 %collective-permute-start = (bf16[24,32,128]{2,1,0:T(8,128)(2,1)}, bf16[24,32,128]{2,1,0:T(8,128)(2,1)S(1)}, u32[]{:S(2)}, u32[]{:S(2)}) collective-permute-start(bf16[24,32,128]{2,1,0:T(8,128)(2,1)} %pack_amps.1), channel_id=1, source_target_pairs={{0,16},{1,17},{2,24},{3,25},{4,0},{5,1},{6,8},{7,9},{8,18},{9,19},... | collective-permute-start | bytes 589832 | tf_op jit(solution)/shard_map/ppermute | solution.py:444
  17.0 0.8 %copy-start.3 = (s32[8,8,16]{2,1,0:T(8,128)S(1)}, s32[8,8,16]{2,1,0:T(8,128)}, u32[]{:S(2)}) copy-start(s32[8,8,16]{2,1,0:T(8,128)} %ti_ref.5) | copy-start | bytes 12292
  25.6 2.4 %collective-permute-start.4 = (bf16[48,64,128]{2,1,0:T(8,128)(2,1)S(1)}, bf16[48,64,128]{2,1,0:T(8,128)(2,1)S(1)}, u32[]{:S(2)}, u32[]{:S(2)}) collective-permute-start(bf16[48,64,128]{2,1,0:T(8,128)(2,1)S(1)} %get-tuple-element.36), channel_id=1, source_target_pairs={{0,1},{1,0},{2,3},{3,2},{4,5},{5,4},{6,7},{7,6},{8,9},{9,8},{10,11... | collective-permute-start | bytes 2359304 | tf_op jit(solution)/shard_map/ppermute | solution.py:423
  25.7 10.2 %collective-permute-start.7 = (bf16[48,64,128]{2,1,0:T(8,128)(2,1)S(1)}, bf16[48,64,128]{2,1,0:T(8,128)(2,1)S(1)}, u32[]{:S(2)}, u32[]{:S(2)}) collective-permute-start(bf16[48,64,128]{2,1,0:T(8,128)(2,1)S(1)} %get-tuple-element.47), channel_id=1, source_target_pairs={{0,1},{1,0},{2,3},{3,2},{4,5},{5,4},{6,7},{7,6},{8,9},{9,8},{10,11... | collective-permute-start | bytes 2359304 | tf_op jit(solution)/shard_map/ppermute | solution.py:423
  29.3 16.0 %copy-start = (f32[2,16,4096]{2,1,0:T(8,128)S(1)}, f32[2,16,4096]{2,1,0:T(8,128)}, u32[]{:S(2)}) copy-start(f32[2,16,4096]{2,1,0:T(8,128)} %denominators.1.inv_ref) | copy-start | bytes 1572868
  29.3 16.0 %copy-start.1 = (bf16[6,1,2,16,4096]{4,3,2,1,0:T(8,128)(2,1)S(1)}, bf16[6,1,2,16,4096]{4,3,2,1,0:T(8,128)(2,1)}, u32[]{:S(2)}) copy-start(bf16[6,1,2,16,4096]{4,3,2,1,0:T(8,128)(2,1)} %hist_ref.1) | copy-start | bytes 4718596
  29.3 16.0 %copy-start.2 = (bf16[1,2,16,4096]{3,2,1,0:T(8,128)(2,1)S(1)}, bf16[1,2,16,4096]{3,2,1,0:T(8,128)(2,1)}, u32[]{:S(2)}) copy-start(bf16[1,2,16,4096]{3,2,1,0:T(8,128)(2,1)} %amps_ref.3) | copy-start | bytes 786436
  29.3 16.0 %copy-start.4 = (bf16[1,2,16,4096]{3,2,1,0:T(8,128)(2,1)S(1)}, bf16[1,2,16,4096]{3,2,1,0:T(8,128)(2,1)}, u32[]{:S(2)}) copy-start(bf16[1,2,16,4096]{3,2,1,0:T(8,128)(2,1)} %ovov_ref.1) | copy-start | bytes 786436
  29.3 9.3 %collective-permute-start.5 = (bf16[24,32,128]{2,1,0:T(8,128)(2,1)S(1)}, bf16[24,32,128]{2,1,0:T(8,128)(2,1)S(1)}, u32[]{:S(2)}, u32[]{:S(2)}) collective-permute-start(bf16[24,32,128]{2,1,0:T(8,128)(2,1)S(1)} %get-tuple-element.44), channel_id=1, source_target_pairs={{0,6},{1,7},{2,4},{3,5},{4,2},{5,3},{6,0},{7,1},{8,14},{9,15},{10,... | collective-permute-start | bytes 589832 | tf_op jit(solution)/shard_map/ppermute | solution.py:423
  31.2 13.7 %collective-permute-start.6 = (bf16[24,32,128]{2,1,0:T(8,128)(2,1)S(1)}, bf16[24,32,128]{2,1,0:T(8,128)(2,1)S(1)}, u32[]{:S(2)}, u32[]{:S(2)}) collective-permute-start(bf16[24,32,128]{2,1,0:T(8,128)(2,1)S(1)} %get-tuple-element.45), channel_id=1, source_target_pairs={{0,2},{1,3},{2,0},{3,1},{4,6},{5,7},{6,4},{7,5},{8,10},{9,11},{10,... | collective-permute-start | bytes 589832 | tf_op jit(solution)/shard_map/ppermute | solution.py:423
  38.6 6.7 %collective-permute-start.8 = (bf16[24,32,128]{2,1,0:T(8,128)(2,1)S(1)}, bf16[24,32,128]{2,1,0:T(8,128)(2,1)S(1)}, u32[]{:S(2)}, u32[]{:S(2)}) collective-permute-start(bf16[24,32,128]{2,1,0:T(8,128)(2,1)S(1)} %get-tuple-element.48), channel_id=1, source_target_pairs={{0,4},{1,5},{2,6},{3,7},{4,0},{5,1},{6,2},{7,3},{8,12},{9,13},{10,... | collective-permute-start | bytes 589832 | tf_op jit(solution)/shard_map/ppermute | solution.py:423

commit v9 on v8

--- a/solution.py
+++ b/solution.py
@@ -233,7 +233,7 @@
         out_specs=VMEM,
         scratch_shapes=[pltpu.VMEM((2 * capt, 64), F32)] * 2,
         out_shape=jax.ShapeDtypeStruct((2, capt, TILE * TILE), F32),
-        cost_estimate=pl.CostEstimate(flops=10**7, bytes_accessed=10**6, transcendentals=0),
+        cost_estimate=pl.CostEstimate(flops=1000, bytes_accessed=1000, transcendentals=0),
         name="denominators",
     )(ti, slab, eps_occ, eps_vir.reshape(across, 64))
 
@@ -442,16 +442,17 @@
     axes = ("reorder", "pair")
     order = [n // 2 if n % 2 == 0 else nq - 1 - n // 2 for n in range(nq)][::-1]
     turned = [lax.ppermute(packed, axes, spread_perm(npair, nq, m)) for m in order]
-    late = lax.optimization_barrier((packed, cycle_ints, tile_index, slab, eps_occ, eps_vir))
-    meta, mine, *send = prep(*late[1:3], capt, across, nq)
-    inv = denominators(*late[2:], capt, across)
-    turned, send, inv = lax.optimization_barrier((turned, send, inv))
+    late = lax.optimization_barrier((packed, cycle_ints, tile_index))
+    meta, mine, *send = prep(*late[1:], capt, across, nq)
+    turned, send = lax.optimization_barrier((turned, send))
     turned = [turned[order.index(m)] for m in range(nq)]
     theirs = [swap(tiles, "pair", npair, 1) for tiles in send]
     sums = multiply("own", meta, [mine], turned, [], nq)
     partial = multiply("sibling", meta, theirs[:1], turned, [sums], nq)
     partial, mine = lax.optimization_barrier((list(partial), mine))
     partial += multiply("both", meta, [mine, theirs[1]], turned, [], nq)
+    late = lax.optimization_barrier((partial[-1], tile_index, slab, eps_occ, eps_vir))
+    inv = denominators(*late[1:], capt, across)
     parts = [
         swap(part, "pair", npair, 2 * e) if e else part
         for e, part in zip(sum_order(nq), partial)

time: 60.6 us -> 63.3 us (1.045)
  waiting for transfers between devices: 6.85 us -> 9.13 us
    ppermute x4, waiting for transfers between devices: 0.01 us -> 3.24 us  [local(): lax.ppermute(packed, axes, spread_perm(npair, nq, m))]
    unnamed x10 -> x14, local copies, waits for them, and re-layouts: 0.78 us -> 1.82 us
    ppermute x5, waiting for transfers between devices: 6.84 us -> 5.88 us  [swap(): return lax.ppermute(x, axis, [(n, n ^ step) for n in range(size)])]
    reshape x1, local copies, waits for them, and re-layouts: 1.36 us -> 0.68 us  [denominators(): eps_vir.reshape(across, 64)]
  transfers between devices with their start and end apart: 9 -> 9, of which waited for: 3 -> 4; matrix products, arithmetic and copies ran while one was open for 2% -> 1% of each run, Pallas kernels for 27% -> 22%
where the time goes in v9:
time: 63.3 us; the launch traced here: 62.8 us
  Pallas kernels  22.4 us (35%)
  starting transfers between devices  17.1 us (27%)
  blocking collectives  11 us (17%)
  waiting for transfers between devices  9.13 us (14%)
  local copies, waits for them, and re-layouts  2.5 us (4%)
  between operations  0.76 us (1%)
    all_to_all x1, blocking collectives, local(): sums = lax.all_to_all(gram, axes, split_axis=0, concat_axis=0, tiled=True)  11 us
    ppermute x4, starting transfers between devices, local(): lax.ppermute(packed, axes, spread_perm(npair, nq, m))  9.96 us
    pallas_call x1, Pallas kernels, prep(): pl.pallas_call(functools.partial(prep_kernel, capt, across, nq, nmax), in...  7.93 us
    ppermute x5, starting transfers between devices, swap(): return lax.ppermute(x, axis, [(n, n ^ step) for n in range(size)])  7.15 us
    ppermute x5, waiting for transfers between devices, swap(): return lax.ppermute(x, axis, [(n, n ^ step) for n in range(size)])  5.88 us
    pallas_call x3, Pallas kernels, multiply(): pl.pallas_call(functools.partial(multiply_kernel, part, nq, nmax, 8), in_...  5.36 us
    ppermute x4, waiting for transfers between devices, local(): lax.ppermute(packed, axes, spread_perm(npair, nq, m))  3.24 us
    pallas_call x1, Pallas kernels, update(): pl.pallas_call(functools.partial(update_kernel, capt, across, nq), in_spe...  2.81 us
  transfers between devices with their start and end apart: 9, of which 4 were waited for; matrix products, arithmetic and copies ran while one was open for 1% of the time, Pallas kernels for 22%

profile of v9, /device:TPU:0, one launch (start us, length us, event | category | flops | bytes accessed | tf_op | source)
XLA Modules:
  0.0 62.8 jit_solution(12974800118212399867)
XLA Ops:
  0.6 2.4 %pack_amps.1 = bf16[24,32,128]{2,1,0:T(8,128)(2,1)} custom-call(s32[8,8,16]{2,1,0:T(8,128)} %ti_ref.5, bf16[1,2,16,4096]{3,2,1,0:T(8,128)(2,1)} %amps_ref.3), custom_call_target="tpu_custom_call" | custom-call | flops 100000000 | bytes 500000 | tf_op jit(solution)/shard_map/pack_amps/pallas_call | solution.py:62
  3.0 1.6 %collective-permute-start.3 = (bf16[24,32,128]{2,1,0:T(8,128)(2,1)}, bf16[24,32,128]{2,1,0:T(8,128)(2,1)S(1)}, u32[]{:S(2)}, u32[]{:S(2)}) collective-permute-start(bf16[24,32,128]{2,1,0:T(8,128)(2,1)} %pack_amps.1), channel_id=1, source_target_pairs={{0,0},{1,1},{2,8},{3,9},{4,16},{5,17},{6,24},{7,25},{8,2},{9,3},{1... | collective-permute-start | bytes 589832 | tf_op jit(solution)/shard_map/ppermute | solution.py:444
  4.6 7.6 %collective-permute-start.2 = (bf16[24,32,128]{2,1,0:T(8,128)(2,1)}, bf16[24,32,128]{2,1,0:T(8,128)(2,1)S(1)}, u32[]{:S(2)}, u32[]{:S(2)}) collective-permute-start(bf16[24,32,128]{2,1,0:T(8,128)(2,1)} %pack_amps.1), channel_id=1, source_target_pairs={{0,24},{1,25},{2,16},{3,17},{4,8},{5,9},{6,0},{7,1},{8,26},{9,27},... | collective-permute-start | bytes 589832 | tf_op jit(solution)/shard_map/ppermute | solution.py:444
  12.2 0.7 %collective-permute-start.1 = (bf16[24,32,128]{2,1,0:T(8,128)(2,1)}, bf16[24,32,128]{2,1,0:T(8,128)(2,1)S(1)}, u32[]{:S(2)}, u32[]{:S(2)}) collective-permute-start(bf16[24,32,128]{2,1,0:T(8,128)(2,1)} %pack_amps.1), channel_id=1, source_target_pairs={{0,8},{1,9},{2,0},{3,1},{4,24},{5,25},{6,16},{7,17},{8,10},{9,11},... | collective-permute-start | bytes 589832 | tf_op jit(solution)/shard_map/ppermute | solution.py:444
  12.9 0.1 collective-permute-start
  13.0 0.8 %copy-done.3 = s32[8,8,16]{2,1,0:T(8,128)S(1)} copy-done((s32[8,8,16]{2,1,0:T(8,128)S(1)}, s32[8,8,16]{2,1,0:T(8,128)}, u32[]{:S(2)}) %copy-start.3) | copy-done | bytes 4120
  13.7 7.9 %prep_integrals.1 = (s32[1568]{0:T(1024)S(1)}, bf16[96,64,128]{2,1,0:T(8,128)(2,1)S(1)}, bf16[48,64,128]{2,1,0:T(8,128)(2,1)S(1)}, bf16[48,64,128]{2,1,0:T(8,128)(2,1)S(1)}) custom-call(s32[8,8,16]{2,1,0:T(8,128)S(1)} %copy-done.3, bf16[625,64,128]{2,1,0:T(8,128)(2,1)} %bitcast.9), custom_call_target="tpu_custom_call" | custom-call | flops 1000000000 | bytes 40000000 | tf_op jit(solution)/shard_map/prep_integrals/pallas_call | solution.py:182
  21.7 0.3 collective-permute-done.1.refs_2_.refs_3_
  22.0 2.9 %collective-permute-done.refs_3_.refs_4_ = bf16[24,32,128]{2,1,0:T(8,128)(2,1)S(1)} collective-permute-done((bf16[24,32,128]{2,1,0:T(8,128)(2,1)}, bf16[24,32,128]{2,1,0:T(8,128)(2,1)S(1)}, u32[]{:S(2)}, u32[]{:S(2)}) %collective-permute-start) | collective-permute-done | bytes 196640 | tf_op jit(solution)/shard_map/ppermute | solution.py:444
  24.9 0.5 collective-permute-start.5
  25.4 1.8 %multiply_own.1.refs_5_ = f32[49,32,128]{2,1,0:T(8,128)S(1)} custom-call(s32[1568]{0:T(1024)S(1)} %get-tuple-element.29.meta_ref, bf16[96,64,128]{2,1,0:T(8,128)(2,1)S(1)} %get-tuple-element.40.refs_0_, bf16[24,32,128]{2,1,0:T(8,128)(2,1)S(1)} %collective-permute-done.3.refs_1_.refs_2_, bf16[24,32,128]{2,1,0:T(8,128)(2,1)S(1)} %collective-permute-done.1.refs_2_.refs_3_, ...), custom_call_target="tpu_custom_call" | custom-call | flops 1000000000 | bytes 6000000 | tf_op jit(solution)/shard_map/multiply_own/pallas_call | solution.py:325
  27.3 1.3 %multiply_sibling.1 = (bf16[24,32,128]{2,1,0:T(8,128)(2,1)S(1)}, bf16[24,32,128]{2,1,0:T(8,128)(2,1)S(1)}) custom-call(s32[1568]{0:T(1024)S(1)} %get-tuple-element.29.meta_ref, bf16[48,64,128]{2,1,0:T(8,128)(2,1)S(1)} %collective-permute-done.4.refs_0_, bf16[24,32,128]{2,1,0:T(8,128)(2,1)S(1)} %collective-permute-done.3.refs_1_.refs_2_, ...), custom_call_target="tpu_custom_call" | custom-call | flops 1000000000 | bytes 6000000 | tf_op jit(solution)/shard_map/multiply_sibling/pallas_call | solution.py:325
  28.7 0.0 copy-start.2
  28.7 2.2 %multiply_both.1 = (bf16[24,32,128]{2,1,0:T(8,128)(2,1)S(1)}, bf16[24,32,128]{2,1,0:T(8,128)(2,1)S(1)}) custom-call(s32[1568]{0:T(1024)S(1)} %get-tuple-element.29.meta_ref, bf16[96,64,128]{2,1,0:T(8,128)(2,1)S(1)} %get-tuple-element.40.refs_0_, bf16[48,64,128]{2,1,0:T(8,128)(2,1)S(1)} %collective-permute-done.5.refs_1_, ...), custom_call_target="tpu_custom_call" | custom-call | flops 1000000000 | bytes 6000000 | tf_op jit(solution)/shard_map/multiply_both/pallas_call | solution.py:325
  30.9 5.1 %collective-permute-start.8 = (bf16[24,32,128]{2,1,0:T(8,128)(2,1)S(1)}, bf16[24,32,128]{2,1,0:T(8,128)(2,1)S(1)}, u32[]{:S(2)}, u32[]{:S(2)}) collective-permute-start(bf16[24,32,128]{2,1,0:T(8,128)(2,1)S(1)} %get-tuple-element.49), channel_id=1, source_target_pairs={{0,4},{1,5},{2,6},{3,7},{4,0},{5,1},{6,2},{7,3},{8,12},{9,13},{10,... | collective-permute-start | bytes 589832 | tf_op jit(solution)/shard_map/ppermute | solution.py:423
  36.0 1.5 %collective-permute-start.7 = (bf16[24,32,128]{2,1,0:T(8,128)(2,1)S(1)}, bf16[24,32,128]{2,1,0:T(8,128)(2,1)S(1)}, u32[]{:S(2)}, u32[]{:S(2)}) collective-permute-start(bf16[24,32,128]{2,1,0:T(8,128)(2,1)S(1)} %get-tuple-element.48), channel_id=1, source_target_pairs={{0,2},{1,3},{2,0},{3,1},{4,6},{5,7},{6,4},{7,5},{8,10},{9,11},{10,... | collective-permute-start | bytes 589832 | tf_op jit(solution)/shard_map/ppermute | solution.py:423
  37.6 0.7 %reshape.15.vir_ref = f32[25,64]{1,0:T(8,128)} reshape(f32[1600]{0:T(1024)S(1)} %copy-done.6) | data formatting | bytes 12800 | tf_op jit(solution)/shard_map/reshape | solution.py:238
  38.2 2.6 %denominators.1.inv_ref = f32[2,16,4096]{2,1,0:T(8,128)} custom-call(s32[8,8,16]{2,1,0:T(8,128)} %ti_ref.5, s32[8]{0:T(128)} %slab_ref, f32[200]{0:T(256)} %occ_ref, f32[25,64]{1,0:T(8,128)} %reshape.15.vir_ref), custom_call_target="tpu_custom_call" | custom-call | flops 1000 | bytes 1000 | tf_op jit(solution)/shard_map/denominators/pallas_call | solution.py:230
  40.8 4.6 %collective-permute-done.8.refs_2_ = bf16[24,32,128]{2,1,0:T(8,128)(2,1)S(1)} collective-permute-done((bf16[24,32,128]{2,1,0:T(8,128)(2,1)S(1)}, bf16[24,32,128]{2,1,0:T(8,128)(2,1)S(1)}, u32[]{:S(2)}, u32[]{:S(2)}) %collective-permute-start.8) | collective-permute-done | bytes 196640 | tf_op jit(solution)/shard_map/ppermute | solution.py:423
  45.4 1.3 %collective-permute-done.7.refs_1_ = bf16[24,32,128]{2,1,0:T(8,128)(2,1)S(1)} collective-permute-done((bf16[24,32,128]{2,1,0:T(8,128)(2,1)S(1)}, bf16[24,32,128]{2,1,0:T(8,128)(2,1)S(1)}, u32[]{:S(2)}, u32[]{:S(2)}) %collective-permute-start.7) | collective-permute-done | bytes 196640 | tf_op jit(solution)/shard_map/ppermute | solution.py:423
  46.8 1.0 %copy-done = f32[2,16,4096]{2,1,0:T(8,128)S(1)} copy-done((f32[2,16,4096]{2,1,0:T(8,128)S(1)}, f32[2,16,4096]{2,1,0:T(8,128)}, u32[]{:S(2)}) %copy-start) | copy-done | bytes 524312
  47.8 2.8 %update_amps.1 = (bf16[1,2,16,4096]{3,2,1,0:T(8,128)(2,1)}, f32[32,1,128]{2,1,0:T(1,128)S(1)}) custom-call(s32[8,8,16]{2,1,0:T(8,128)S(1)} %copy-done.4, bf16[1,2,16,4096]{3,2,1,0:T(8,128)(2,1)S(1)} %copy-done.2, bf16[1,2,16,4096]{3,2,1,0:T(8,128)(2,1)S(1)} %copy-done.5, bf16[6,1,2,16,4096]{4,3,2,1,0:T(8,128)(2,1)S(1)} %copy-done.1, ...), custom_call_target="tpu_custom_call" | custom-call | flops 100000000 | bytes 6000000 | tf_op jit(solution)/shard_map/update_amps/pallas_call | solution.py:386
  50.6 11.0 %all_to_all.5.sums_ref = f32[32,1,128]{2,1,0:T(1,128)} all-to-all(f32[32,1,128]{2,1,0:T(1,128)S(1)} %get-tuple-element.51), channel_id=1, replica_groups=mesh['reorder'=4,'pair'=8] {'reorder','pair'}, dimensions={0} | all-to-all | bytes 32768 | tf_op jit(solution)/shard_map/all_to_all | solution.py:463
  61.6 1.3 %finish_gram.1 = f32[7]{0:T(128)} custom-call(f32[32,1,128]{2,1,0:T(1,128)} %all_to_all.5.sums_ref), custom_call_target="tpu_custom_call" | custom-call | tf_op jit(solution)/shard_map/finish_gram/pallas_call | solution.py:413
  (18 shorter events, 0.0 us)
Async XLA Ops:
  3.0 18.7 %collective-permute-start.3 = (bf16[24,32,128]{2,1,0:T(8,128)(2,1)}, bf16[24,32,128]{2,1,0:T(8,128)(2,1)S(1)}, u32[]{:S(2)}, u32[]{:S(2)}) collective-permute-start(bf16[24,32,128]{2,1,0:T(8,128)(2,1)} %pack_amps.1), channel_id=1, source_target_pairs={{0,0},{1,1},{2,8},{3,9},{4,16},{5,17},{6,24},{7,25},{8,2},{9,3},{1... | collective-permute-start | bytes 589832 | tf_op jit(solution)/shard_map/ppermute | solution.py:444
  4.6 17.1 %collective-permute-start.2 = (bf16[24,32,128]{2,1,0:T(8,128)(2,1)}, bf16[24,32,128]{2,1,0:T(8,128)(2,1)S(1)}, u32[]{:S(2)}, u32[]{:S(2)}) collective-permute-start(bf16[24,32,128]{2,1,0:T(8,128)(2,1)} %pack_amps.1), channel_id=1, source_target_pairs={{0,24},{1,25},{2,16},{3,17},{4,8},{5,9},{6,0},{7,1},{8,26},{9,27},... | collective-permute-start | bytes 589832 | tf_op jit(solution)/shard_map/ppermute | solution.py:444
  12.2 9.9 %collective-permute-start.1 = (bf16[24,32,128]{2,1,0:T(8,128)(2,1)}, bf16[24,32,128]{2,1,0:T(8,128)(2,1)S(1)}, u32[]{:S(2)}, u32[]{:S(2)}) collective-permute-start(bf16[24,32,128]{2,1,0:T(8,128)(2,1)} %pack_amps.1), channel_id=1, source_target_pairs={{0,8},{1,9},{2,0},{3,1},{4,24},{5,25},{6,16},{7,17},{8,10},{9,11},... | collective-permute-start | bytes 589832 | tf_op jit(solution)/shard_map/ppermute | solution.py:444
  12.9 12.1 %collective-permute-start = (bf16[24,32,128]{2,1,0:T(8,128)(2,1)}, bf16[24,32,128]{2,1,0:T(8,128)(2,1)S(1)}, u32[]{:S(2)}, u32[]{:S(2)}) collective-permute-start(bf16[24,32,128]{2,1,0:T(8,128)(2,1)} %pack_amps.1), channel_id=1, source_target_pairs={{0,16},{1,17},{2,24},{3,25},{4,0},{5,1},{6,8},{7,9},{8,18},{9,19},... | collective-permute-start | bytes 589832 | tf_op jit(solution)/shard_map/ppermute | solution.py:444
  13.0 0.8 %copy-start.3 = (s32[8,8,16]{2,1,0:T(8,128)S(1)}, s32[8,8,16]{2,1,0:T(8,128)}, u32[]{:S(2)}) copy-start(s32[8,8,16]{2,1,0:T(8,128)} %ti_ref.5) | copy-start | bytes 12292
  24.9 2.4 %collective-permute-start.4 = (bf16[48,64,128]{2,1,0:T(8,128)(2,1)S(1)}, bf16[48,64,128]{2,1,0:T(8,128)(2,1)S(1)}, u32[]{:S(2)}, u32[]{:S(2)}) collective-permute-start(bf16[48,64,128]{2,1,0:T(8,128)(2,1)S(1)} %get-tuple-element.32), channel_id=1, source_target_pairs={{0,1},{1,0},{2,3},{3,2},{4,5},{5,4},{6,7},{7,6},{8,9},{9,8},{10,11... | collective-permute-start | bytes 2359304 | tf_op jit(solution)/shard_map/ppermute | solution.py:423
  24.9 3.8 %collective-permute-start.5 = (bf16[48,64,128]{2,1,0:T(8,128)(2,1)S(1)}, bf16[48,64,128]{2,1,0:T(8,128)(2,1)S(1)}, u32[]{:S(2)}, u32[]{:S(2)}) collective-permute-start(bf16[48,64,128]{2,1,0:T(8,128)(2,1)S(1)} %get-tuple-element.41), channel_id=1, source_target_pairs={{0,1},{1,0},{2,3},{3,2},{4,5},{5,4},{6,7},{7,6},{8,9},{9,8},{10,11... | collective-permute-start | bytes 2359304 | tf_op jit(solution)/shard_map/ppermute | solution.py:423
  28.7 8.9 %copy-start.6 = (f32[1600]{0:T(1024)S(1)}, f32[1600]{0:T(1024)}, u32[]{:S(2)}) copy-start(f32[1600]{0:T(1024)} %param.15) | copy-start | bytes 19204
  28.7 18.1 %copy-start.1 = (bf16[6,1,2,16,4096]{4,3,2,1,0:T(8,128)(2,1)S(1)}, bf16[6,1,2,16,4096]{4,3,2,1,0:T(8,128)(2,1)}, u32[]{:S(2)}) copy-start(bf16[6,1,2,16,4096]{4,3,2,1,0:T(8,128)(2,1)} %hist_ref.1) | copy-start | bytes 4718596
  28.7 18.0 %copy-start.2 = (bf16[1,2,16,4096]{3,2,1,0:T(8,128)(2,1)S(1)}, bf16[1,2,16,4096]{3,2,1,0:T(8,128)(2,1)}, u32[]{:S(2)}) copy-start(bf16[1,2,16,4096]{3,2,1,0:T(8,128)(2,1)} %amps_ref.3) | copy-start | bytes 786436
  28.7 18.0 %copy-start.4 = (s32[8,8,16]{2,1,0:T(8,128)S(1)}, s32[8,8,16]{2,1,0:T(8,128)}, u32[]{:S(2)}) copy-start(s32[8,8,16]{2,1,0:T(8,128)} %ti_ref.5) | copy-start | bytes 12292
  28.7 18.0 %copy-start.5 = (bf16[1,2,16,4096]{3,2,1,0:T(8,128)(2,1)S(1)}, bf16[1,2,16,4096]{3,2,1,0:T(8,128)(2,1)}, u32[]{:S(2)}) copy-start(bf16[1,2,16,4096]{3,2,1,0:T(8,128)(2,1)} %ovov_ref.1) | copy-start | bytes 786436
  30.9 14.5 %collective-permute-start.8 = (bf16[24,32,128]{2,1,0:T(8,128)(2,1)S(1)}, bf16[24,32,128]{2,1,0:T(8,128)(2,1)S(1)}, u32[]{:S(2)}, u32[]{:S(2)}) collective-permute-start(bf16[24,32,128]{2,1,0:T(8,128)(2,1)S(1)} %get-tuple-element.49), channel_id=1, source_target_pairs={{0,4},{1,5},{2,6},{3,7},{4,0},{5,1},{6,2},{7,3},{8,12},{9,13},{10,... | collective-permute-start | bytes 589832 | tf_op jit(solution)/shard_map/ppermute | solution.py:423
  36.0 9.4 %collective-permute-start.6 = (bf16[24,32,128]{2,1,0:T(8,128)(2,1)S(1)}, bf16[24,32,128]{2,1,0:T(8,128)(2,1)S(1)}, u32[]{:S(2)}, u32[]{:S(2)}) collective-permute-start(bf16[24,32,128]{2,1,0:T(8,128)(2,1)S(1)} %get-tuple-element.47), channel_id=1, source_target_pairs={{0,6},{1,7},{2,4},{3,5},{4,2},{5,3},{6,0},{7,1},{8,14},{9,15},{10,... | collective-permute-start | bytes 589832 | tf_op jit(solution)/shard_map/ppermute | solution.py:423
  36.0 10.7 %collective-permute-start.7 = (bf16[24,32,128]{2,1,0:T(8,128)(2,1)S(1)}, bf16[24,32,128]{2,1,0:T(8,128)(2,1)S(1)}, u32[]{:S(2)}, u32[]{:S(2)}) collective-permute-start(bf16[24,32,128]{2,1,0:T(8,128)(2,1)S(1)} %get-tuple-element.48), channel_id=1, source_target_pairs={{0,2},{1,3},{2,0},{3,1},{4,6},{5,7},{6,4},{7,5},{8,10},{9,11},{10,... | collective-permute-start | bytes 589832 | tf_op jit(solution)/shard_map/ppermute | solution.py:423
  46.7 1.0 %copy-start = (f32[2,16,4096]{2,1,0:T(8,128)S(1)}, f32[2,16,4096]{2,1,0:T(8,128)}, u32[]{:S(2)}) copy-start(f32[2,16,4096]{2,1,0:T(8,128)} %denominators.1.inv_ref) | copy-start | bytes 1572868
